TPU v7x, 32 devices: a whole 2x2x4 slice. The times are simulated.
32 devices in a mesh: dp: 8 (over y, x, core), tensor: 4 (over z).
Axes of the slice: x: 2, y: 2, z: 4, core: 2. Of those that a mesh axis runs over, the one named last changes fastest.
Arguments:
- tokens: bfloat16 [20480, 1024], P(('dp', 'tensor')), may hold values from -6 to 6
- lengths: int32 [8, 2], P('dp'), may hold values from 1024 to 1536, as said below
- row_order: int32 [8, 2560], P('dp'), may hold values from 0 to 2559, each once within a row
- attention_gain: bfloat16 [1024], P('dp'), may hold values from 0.099609375 to 1.8984375
- query_gain: bfloat16 [128], P('dp'), may hold values from 0.796875 to 1.796875
- key_gain: bfloat16 [128], P('dp'), may hold values from 0.796875 to 1.796875
- query_weight: bfloat16 [1024, 2048], P('dp', 'tensor'), may hold values from -0.1875 to 0.1875
- key_matrix: bfloat16 [1024, 1024], P('dp', 'tensor'), may hold values from -0.1875 to 0.1875
- value_matrix: bfloat16 [1024, 1024], P('dp', 'tensor'), may hold values from -0.1875 to 0.1875
- output_weight: bfloat16 [2048, 1024], P('tensor', 'dp'), may hold values from -1 to 1
- feedforward_gain: bfloat16 [1024], P('dp'), may hold values from 0.099609375 to 1.8984375
- gate_weight: bfloat16 [1024, 3072], P('dp', 'tensor'), may hold values from -0.1875 to 0.1875
- up_weight: bfloat16 [1024, 3072], P('dp', 'tensor'), may hold values from -0.1875 to 0.1875
- down_weight: bfloat16 [3072, 1024], P('tensor', 'dp'), may hold values from -0.109375 to 0.109375
- cotangent: bfloat16 [20480, 1024], P(('dp', 'tensor')), may hold values from -6 to 6
Outputs:
- layer_output: bfloat16 [20480, 1024], P(('dp', 'tensor'))
- input_grad: bfloat16 [20480, 1024], P(('dp', 'tensor'))
- attention_gain_grad: float32 [1024], P('dp')
- query_gain_grad: float32 [128], P('dp')
- key_gain_grad: float32 [128], P('dp')
- query_weight_grad: float32 [1024, 2048], P('dp', 'tensor')
- key_weight_grad: float32 [1024, 1024], P('dp', 'tensor')
- value_weight_grad: float32 [1024, 1024], P('dp', 'tensor')
- output_weight_grad: float32 [2048, 1024], P('tensor', 'dp')
- feedforward_gain_grad: float32 [1024], P('dp')
- gate_weight_grad: float32 [1024, 3072], P('dp', 'tensor')
- up_weight_grad: float32 [1024, 3072], P('dp', 'tensor')
- down_weight_grad: float32 [3072, 1024], P('tensor', 'dp')
Inputs may be any that keep to these rules, and one draw needn't show every extreme that they name: Each row of lengths holds the lengths of the 2 sequences that fill one group's 2560 tokens. Each row of row_order holds every place of 0 to 2559 once.
All inputs are finite; a program needn't handle non-finite values.
Results may differ from a plain program's by a relative error of at most 0.025.
Values may be sent and summed in bfloat16 or wider, within the bound.
A program may use at most 256 MiB of HBM per device.

v0:
```python
import jax
import jax.numpy as jnp
from jax import lax
from jax.sharding import PartitionSpec as P

HEAD_SIZE = 128


EPSILON = 1e-06
THETA = 1000000.0


def rms_norm(value_rows, gain):
    scale = lax.rsqrt(jnp.mean(value_rows * value_rows, axis=-1, keepdims=True) + EPSILON)
    return value_rows * scale * gain


def rotate(value_rows, cosine, sine):
    half = value_rows.shape[-1] // 2
    first = value_rows[..., :half]
    second = value_rows[..., half:]
    return jnp.concatenate(
        [first * cosine - second * sine, second * cosine + first * sine], axis=-1
    )


def layout(lengths_row, permuted_order_row):
    ends = jnp.cumsum(lengths_row)
    starts = ends - lengths_row
    document_ids = jnp.sum((permuted_order_row[:, None] >= ends[None, :]).astype(jnp.int32), axis=1)
    chosen = document_ids[:, None] == jnp.arange(lengths_row.shape[0], dtype=jnp.int32)[None, :]
    begin = jnp.sum(jnp.where(chosen, starts[None, :], 0), axis=1)
    return (document_ids, permuted_order_row - begin)


def rotary_tables(position, width):
    half = width // 2
    inverse = THETA ** (-(jnp.arange(half, dtype=jnp.float32) * 2.0 / width))
    angle = position.astype(jnp.float32)[:, None] * inverse[None, :]
    return (jnp.cos(angle)[:, None, :], jnp.sin(angle)[:, None, :])


def contract_rows(left, right):
    return lax.dot_general(
        left, right, (((0,), (0,)), ((), ())), preferred_element_type=jnp.float32
    )


def contract_columns(left, right):
    return lax.dot_general(
        left, right, (((1,), (1,)), ((), ())), preferred_element_type=jnp.float32
    )


def local(
    tokens,
    lengths,
    row_order,
    attention_gain,
    query_gain,
    key_gain,
    query_weight,
    key_matrix,
    value_matrix,
    output_weight,
    feedforward_gain,
    gate_weight,
    up_weight,
    down_weight,
    cotangent,
):
    own_rows = tokens.shape[0]
    query_width = query_weight.shape[1]
    key_width = key_matrix.shape[1]
    query_heads = query_width // HEAD_SIZE
    kv_heads = key_width // HEAD_SIZE
    group_size = query_heads // kv_heads
    hidden_width = gate_weight.shape[1]
    group_rows = own_rows * lax.axis_size("tensor")
    rows_per_block = min(512, group_rows)
    block_list = group_rows // rows_per_block
    scale = HEAD_SIZE ** (-0.5)
    order_all = row_order[0]
    document_ids, position = layout(lengths[0], order_all)
    cosine, sine = rotary_tables(position, HEAD_SIZE)
    document_blocks = document_ids.reshape(block_list, rows_per_block)
    order_blocks = order_all.reshape(block_list, rows_per_block)
    local_weights = (
        attention_gain,
        query_gain,
        key_gain,
        jnp.concatenate([query_weight, key_matrix, value_matrix], axis=1),
        output_weight.T,
        feedforward_gain,
        jnp.concatenate([gate_weight, up_weight], axis=1),
        down_weight.T,
    )

    def project(normed_rows, joined_qkv, gain_query, gain_key):
        projected = jnp.dot(normed_rows, joined_qkv, preferred_element_type=jnp.float32)
        query_raw = projected[:, :query_width].reshape(group_rows, query_heads, HEAD_SIZE)
        key_unnormed = projected[:, query_width : query_width + key_width].reshape(
            group_rows, kv_heads, HEAD_SIZE
        )
        value_rows = (
            projected[:, query_width + key_width :]
            .reshape(group_rows, kv_heads, HEAD_SIZE)
            .astype(jnp.bfloat16)
        )
        query_rows = rotate(rms_norm(query_raw, gain_query), cosine, sine).astype(jnp.bfloat16)
        keys = rotate(rms_norm(key_unnormed, gain_key), cosine, sine).astype(jnp.bfloat16)
        return (query_raw, key_unnormed, query_rows, keys, value_rows)

    def masked_scores(query_block, keys, document_block, order_block):
        scores = (
            jnp.einsum("qkgd,skd->kgqs", query_block, keys, preferred_element_type=jnp.float32)
            * scale
        )
        allowed = (document_block[:, None] == document_ids[None, :]) & (
            order_block[:, None] >= order_all[None, :]
        )
        return jnp.where(allowed, scores, -jnp.inf)

    gathered = (
        lax.all_gather(local_weights[0], "dp", axis=0, tiled=True),
        lax.all_gather(local_weights[1], "dp", axis=0, tiled=True),
        lax.all_gather(local_weights[2], "dp", axis=0, tiled=True),
        lax.all_gather(local_weights[3], "dp", axis=0, tiled=True),
        lax.all_gather(local_weights[4], "dp", axis=0, tiled=True),
        lax.all_gather(local_weights[5], "dp", axis=0, tiled=True),
        lax.all_gather(local_weights[6], "dp", axis=0, tiled=True),
        lax.all_gather(local_weights[7], "dp", axis=0, tiled=True),
    )
    gain_one = gathered[0].astype(jnp.float32)
    inputs = tokens.astype(jnp.float32)
    normed_all = lax.all_gather(
        rms_norm(inputs, gain_one).astype(jnp.bfloat16), "tensor", axis=0, tiled=True
    )
    query_raw, key_unnormed, query_rows, keys, value_rows = project(
        normed_all, gathered[3], gathered[1].astype(jnp.float32), gathered[2].astype(jnp.float32)
    )
    query_blocks = query_rows.reshape(block_list, rows_per_block, kv_heads, group_size, HEAD_SIZE)

    def forward_block(carry, items):
        query_block, document_block, order_block = items
        scores = masked_scores(query_block, keys, document_block, order_block)
        top = jnp.max(scores, axis=-1, keepdims=True)
        expo = jnp.exp(scores - top)
        total = jnp.sum(expo, axis=-1, keepdims=True)
        weights = (expo / total).astype(jnp.bfloat16)
        mixed_heads = jnp.einsum(
            "kgqs,skd->qkgd", weights, value_rows, preferred_element_type=jnp.float32
        )
        return (carry, (mixed_heads, top + jnp.log(total)))

    _, (mixed_heads, log_totals) = lax.scan(
        forward_block, 0, (query_blocks, document_blocks, order_blocks)
    )
    attended = mixed_heads.reshape(group_rows, query_width).astype(jnp.bfloat16)
    output_fwd = gathered[4]
    middle = inputs + lax.psum_scatter(
        contract_columns(attended, output_fwd).astype(jnp.bfloat16),
        "tensor",
        scatter_dimension=0,
        tiled=True,
    ).astype(jnp.float32)
    normed_two_all = lax.all_gather(
        rms_norm(middle, gathered[5].astype(jnp.float32)).astype(jnp.bfloat16),
        "tensor",
        axis=0,
        tiled=True,
    )
    gate_up = jnp.dot(normed_two_all, gathered[6], preferred_element_type=jnp.float32)
    activated = (jax.nn.silu(gate_up[:, :hidden_width]) * gate_up[:, hidden_width:]).astype(
        jnp.bfloat16
    )
    down_fwd = gathered[7]
    result = middle + lax.psum_scatter(
        contract_columns(activated, down_fwd).astype(jnp.bfloat16),
        "tensor",
        scatter_dimension=0,
        tiled=True,
    ).astype(jnp.float32)
    layer_output = result.astype(jnp.bfloat16)
    weights_back = (
        lax.all_gather(local_weights[0], "dp", axis=0, tiled=True),
        lax.all_gather(local_weights[1], "dp", axis=0, tiled=True),
        lax.all_gather(local_weights[2], "dp", axis=0, tiled=True),
        lax.all_gather(local_weights[3], "dp", axis=0, tiled=True),
        lax.all_gather(local_weights[4], "dp", axis=0, tiled=True),
        lax.all_gather(local_weights[5], "dp", axis=0, tiled=True),
        lax.all_gather(local_weights[6], "dp", axis=0, tiled=True),
        lax.all_gather(local_weights[7], "dp", axis=0, tiled=True),
    )
    normed_back = lax.all_gather(
        rms_norm(inputs, weights_back[0].astype(jnp.float32)).astype(jnp.bfloat16),
        "tensor",
        axis=0,
        tiled=True,
    )
    normed_two_back = lax.all_gather(
        rms_norm(middle, weights_back[5].astype(jnp.float32)).astype(jnp.bfloat16),
        "tensor",
        axis=0,
        tiled=True,
    )
    gain_one_back = weights_back[0].astype(jnp.float32)
    gain_query_back = weights_back[1].astype(jnp.float32)
    gain_key_back = weights_back[2].astype(jnp.float32)
    joined_qkv = weights_back[3]
    output_back = weights_back[4]
    gain_two_back = weights_back[5].astype(jnp.float32)
    joined_gate_up = weights_back[6]
    down_back = weights_back[7]
    cotangent_all = lax.all_gather(cotangent, "tensor", axis=0, tiled=True)
    gate_up = jnp.dot(normed_two_back, joined_gate_up, preferred_element_type=jnp.float32)

    def swish_product(gate_in, up_in):
        return jax.nn.silu(gate_in) * up_in

    product, pull_swish = jax.vjp(
        swish_product, gate_up[:, :hidden_width], gate_up[:, hidden_width:]
    )
    activated_back = product.astype(jnp.bfloat16)
    down_grad_rows = contract_rows(cotangent_all, activated_back)
    activated_grad = jnp.dot(cotangent_all, down_back, preferred_element_type=jnp.float32)
    gate_grad, upward_grad = pull_swish(activated_grad)
    gate_up_grad = jnp.concatenate([gate_grad, upward_grad], axis=1).astype(jnp.bfloat16)
    gate_up_weight_grad = contract_rows(normed_two_back, gate_up_grad)
    normed_two_grad = lax.psum_scatter(
        contract_columns(gate_up_grad, joined_gate_up).astype(jnp.bfloat16),
        "tensor",
        scatter_dimension=0,
        tiled=True,
    ).astype(jnp.float32)
    _, pull_norm_two = jax.vjp(rms_norm, middle, gain_two_back)
    middle_norm_grad, gain_two_grad = pull_norm_two(normed_two_grad)
    middle_grad = cotangent.astype(jnp.float32) + middle_norm_grad
    branch_all = lax.all_gather(middle_grad.astype(jnp.bfloat16), "tensor", axis=0, tiled=True)
    query_raw, key_unnormed, query_rows, keys, value_rows = project(
        normed_back, joined_qkv, gain_query_back, gain_key_back
    )
    query_blocks = query_rows.reshape(block_list, rows_per_block, kv_heads, group_size, HEAD_SIZE)
    output_grad_rows = contract_rows(branch_all, attended)
    attended_grad = jnp.dot(branch_all, output_back, preferred_element_type=jnp.float32).astype(
        jnp.bfloat16
    )
    grad_blocks = attended_grad.reshape(block_list, rows_per_block, kv_heads, group_size, HEAD_SIZE)

    def backward_block(carry, items):
        key_sum, value_sum = carry
        query_block, document_block, order_block, total_block, grad_block = items
        scores = masked_scores(query_block, keys, document_block, order_block)
        probs = jnp.exp(scores - total_block)
        probs_grad = jnp.einsum(
            "qkgd,skd->kgqs", grad_block, value_rows, preferred_element_type=jnp.float32
        )
        inner = jnp.sum(probs * probs_grad, axis=-1, keepdims=True)
        score_grad = (probs * (probs_grad - inner)).astype(jnp.bfloat16)
        query_grad = (
            jnp.einsum("kgqs,skd->qkgd", score_grad, keys, preferred_element_type=jnp.float32)
            * scale
        )
        key_sum = (
            key_sum
            + jnp.einsum(
                "kgqs,qkgd->skd", score_grad, query_block, preferred_element_type=jnp.float32
            )
            * scale
        )
        value_sum = value_sum + jnp.einsum(
            "kgqs,qkgd->skd",
            probs.astype(jnp.bfloat16),
            grad_block,
            preferred_element_type=jnp.float32,
        )
        return ((key_sum, value_sum), query_grad)

    empty = jnp.zeros((group_rows, kv_heads, HEAD_SIZE), jnp.float32)
    (keys_grad, values_grad), query_grads = lax.scan(
        backward_block,
        (empty, empty),
        (query_blocks, document_blocks, order_blocks, log_totals, grad_blocks),
    )

    def head_map(raw, gain):
        return rotate(rms_norm(raw, gain), cosine, sine)

    _, pull_query = jax.vjp(head_map, query_raw, gain_query_back)
    query_raw_grad, gain_query_grad = pull_query(
        query_grads.reshape(group_rows, query_heads, HEAD_SIZE)
    )
    _, pull_key = jax.vjp(head_map, key_unnormed, gain_key_back)
    key_raw_grad, gain_key_grad = pull_key(keys_grad)
    qkv_grad = jnp.concatenate(
        [
            query_raw_grad.reshape(group_rows, query_width),
            key_raw_grad.reshape(group_rows, key_width),
            values_grad.reshape(group_rows, key_width),
        ],
        axis=1,
    ).astype(jnp.bfloat16)
    qkv_weight_grad = contract_rows(normed_back, qkv_grad)
    normed_grad = lax.psum_scatter(
        contract_columns(qkv_grad, joined_qkv).astype(jnp.bfloat16),
        "tensor",
        scatter_dimension=0,
        tiled=True,
    ).astype(jnp.float32)
    _, pull_norm_one = jax.vjp(rms_norm, inputs, gain_one_back)
    input_norm_grad, gain_one_grad = pull_norm_one(normed_grad)
    input_grad = (middle_grad + input_norm_grad).astype(jnp.bfloat16)
    summed = (
        lax.psum_scatter(
            gain_one_grad.astype(jnp.bfloat16), "dp", scatter_dimension=0, tiled=True
        ).astype(jnp.float32),
        lax.psum_scatter(
            gain_query_grad.astype(jnp.bfloat16), "dp", scatter_dimension=0, tiled=True
        ).astype(jnp.float32),
        lax.psum_scatter(
            gain_key_grad.astype(jnp.bfloat16), "dp", scatter_dimension=0, tiled=True
        ).astype(jnp.float32),
        lax.psum_scatter(
            qkv_weight_grad.astype(jnp.bfloat16), "dp", scatter_dimension=0, tiled=True
        ).astype(jnp.float32),
        lax.psum_scatter(
            output_grad_rows.astype(jnp.bfloat16), "dp", scatter_dimension=0, tiled=True
        ).astype(jnp.float32),
        lax.psum_scatter(
            gain_two_grad.astype(jnp.bfloat16), "dp", scatter_dimension=0, tiled=True
        ).astype(jnp.float32),
        lax.psum_scatter(
            gate_up_weight_grad.astype(jnp.bfloat16), "dp", scatter_dimension=0, tiled=True
        ).astype(jnp.float32),
        lax.psum_scatter(
            down_grad_rows.astype(jnp.bfloat16), "dp", scatter_dimension=0, tiled=True
        ).astype(jnp.float32),
    )
    gain_totals = lax.psum((summed[0], summed[1], summed[2], summed[5]), "tensor")
    qkv_total = summed[3]
    gate_up_total = summed[6]
    return (
        layer_output,
        input_grad,
        gain_totals[0],
        gain_totals[1],
        gain_totals[2],
        qkv_total[:, :query_width],
        qkv_total[:, query_width : query_width + key_width],
        qkv_total[:, query_width + key_width :],
        summed[4].T,
        gain_totals[3],
        gate_up_total[:, :hidden_width],
        gate_up_total[:, hidden_width:],
        summed[7].T,
    )


def solution(mesh):
    placed = (
        P(("dp", "tensor"), None),
        P("dp", None),
        P("dp", None),
        P("dp"),
        P("dp"),
        P("dp"),
        P("dp", "tensor"),
        P("dp", "tensor"),
        P("dp", "tensor"),
        P("tensor", "dp"),
        P("dp"),
        P("dp", "tensor"),
        P("dp", "tensor"),
        P("tensor", "dp"),
        P(("dp", "tensor"), None),
    )
    return jax.shard_map(
        local,
        mesh=mesh,
        in_specs=placed,
        out_specs=(
            P(("dp", "tensor"), None),
            P(("dp", "tensor"), None),
            P("dp"),
            P("dp"),
            P("dp"),
            P("dp", "tensor"),
            P("dp", "tensor"),
            P("dp", "tensor"),
            P("tensor", "dp"),
            P("dp"),
            P("dp", "tensor"),
            P("dp", "tensor"),
            P("tensor", "dp"),
        ),
        check_vma=False,
    )
```

profile of v0, /device:TPU:0, one launch (start us, length us, event | category | flops | bytes accessed | tf_op | source)
XLA Modules:
  0.0 1541.1 jit_solution(2622991587594587342)
XLA Ops:
  44.7 96.7 %all-gather.11.cloned.1.call-done = bf16[2560,1024]{1,0:T(8,128)(2,1)} async-done(((bf16[640,1024]{1,0:T(8,128)(2,1)}), bf16[2560,1024]{1,0:T(8,128)(2,1)}) %all-gather.11.cloned.1.call-update) | async-done | bytes 5242896 | tf_op jit(solution)/shard_map/all_gather | solution.py:136
  200.9 104.4 %while.27 = (s32[]{:T(128)}, bf16[5,512,2,2,128]{4,1,3,2,0:T(8,128)(2,1)}, f32[5,2,2,512,1]{3,2,1,4,0:T(2,128)S(1)}, s32[5,512]{1,0:T(8,128)S(1)}, s32[2560]{0:T...) while((s32[]{:T(128)}, ...), condition=%wide.region_9.10_spmd, body=%wide.region_6.9_spmd.sunk | while | flops 2751199232 | bytes 72470664 | solution.py:156
  330.6 81.9 %reduce-scatter.11.cloned.1.call-done = bf16[640,1024]{1,0:T(8,128)(2,1)} async-done(((bf16[2560,1024]{1,0:T(8,128)(2,1)}), bf16[640,1024]{1,0:T(8,128)(2,1)}) %reduce-scatter.11.cloned.1.call-update) | async-done | bytes 1310736 | tf_op jit(solution)/shard_map/reduce_scatter | solution.py:161
  417.5 30.1 %all-gather.19.cloned.1.call-done = bf16[1024,1536]{1,0:T(8,128)(2,1)} async-done(((bf16[128,1536]{1,0:T(8,128)(2,1)}), bf16[1024,1536]{1,0:T(8,128)(2,1)}) %all-gather.19.cloned.1.call-update) | async-done | bytes 3145744 | tf_op jit(solution)/shard_map/all_gather | solution.py:131
  447.7 100.1 %all-gather.17.cloned.1.call-done = bf16[2560,1024]{1,0:T(8,128)(2,1)} async-done(((bf16[640,1024]{1,0:T(8,128)(2,1)}), bf16[2560,1024]{1,0:T(8,128)(2,1)}) %all-gather.17.cloned.1.call-update) | async-done | bytes 5242896 | tf_op jit(solution)/shard_map/all_gather | solution.py:167
  547.7 14.8 fusion.85
  573.9 99.7 %all-gather.23.cloned.1.call-done = bf16[2560,1024]{1,0:T(8,128)(2,1)} async-done(((bf16[640,1024]{1,0:T(8,128)(2,1)}), bf16[2560,1024]{1,0:T(8,128)(2,1)}) %all-gather.23.cloned.1.call-update) | async-done | bytes 5242896 | tf_op jit(solution)/shard_map/all_gather | solution.py:215
  701.5 91.8 %reduce-scatter.15.cloned.1.call-done = bf16[640,1024]{1,0:T(8,128)(2,1)} async-done(((bf16[2560,1024]{1,0:T(8,128)(2,1)}), bf16[640,1024]{1,0:T(8,128)(2,1)}) %reduce-scatter.15.cloned.1.call-update) | async-done | bytes 1310736 | tf_op jit(solution)/shard_map/reduce_scatter | solution.py:230
  823.6 73.8 %all-gather.25.cloned.1.call-done = bf16[2560,1024]{1,0:T(8,128)(2,1)} async-done(((bf16[640,1024]{1,0:T(8,128)(2,1)}), bf16[2560,1024]{1,0:T(8,128)(2,1)}) %all-gather.25.cloned.1.call-update) | async-done | bytes 5242896 | tf_op jit(solution)/shard_map/all_gather | solution.py:239
  909.5 318.3 %while.28 = (s32[]{:T(128)}, f32[2560,2,128]{0,2,1:T(8,128)S(1)}, f32[2560,2,128]{0,2,1:T(8,128)}, f32[5,512,2,2,128]{4,1,0,3,2:T(8,128)}, bf16[5,512,2,2,128]{4...) while((s32[]{:T(128)}, f32[2560,2,128]{0,2,1:T(8,128)S(1)}, ...), condition=%wide.region_17.18_spmd.clone, body=%wide.region_15.17_spmd.clone.sunk | while | flops 6796998656 | bytes 191738096 | solution.py:280
  934.3 15.4 %fusion.135 = (f32[2,2,512]{2,1,0:T(2,128)S(1)}, f32[2,512,2,2560]{3,1,2,0:T(8,128)}) fusion(f32[2,512,2,2560]{3,1,2,0:T(8,128)} %fusion.134, f32[2,2,512]{2,1,0:T(2,128)S(1)} %dynamic-slice_bitcast_fusion.2, pred[512,2560]{1,0:T(8,128)(4,1)S(1)} %compare_and_fusion.5, bf16[2560,2,128]{2,0,1:T(8,128)(2,1)} %get-tuple-element.729, ...), kind=kOutput, calls=%fused_computation.23.clone.1 | convolution fusion | flops 1368389632 | bytes 45105152 | tf_op jit(solution)/shard_map/while/body/eval_jaxpr/qkgd,skd->kgqs/dot_general | solution.py:255
  949.7 16.9 %fusion.136 = bf16[2,2,512,2560]{3,2,1,0:T(8,128)(2,1)S(1)} fusion(f32[2,512,2,2560]{3,1,2,0:T(8,128)} %get-tuple-element.649, f32[2,512,2,2560]{3,1,2,0:T(8,128)} %fusion.134, f32[2,2,512]{2,1,0:T(2,128)S(1)} %get-tuple-element.650, f32[2,2,512]{2,1,0:T(2,128)S(1)} %dynamic-slice_bitcast_fusion.2, pred[512,2560]{1,0:T(8,128)(4,1)S(1)} %compare_and_fusion.5), kind=kLoop, calls=%fused_computation.25.clone.1 | loop fusion | flops 31457280 | bytes 53755904 | tf_op jit(solution)/shard_map/while/body/eval_jaxpr/convert_element_type | solution.py:259
  999.1 15.2 fusion.135
  1014.3 15.7 %fusion.136 = bf16[2,2,512,2560]{3,2,1,0:T(8,128)(2,1)S(1)} fusion(f32[2,512,2,2560]{3,1,2,0:T(8,128)} %get-tuple-element.649, f32[2,512,2,2560]{3,1,2,0:T(8,128)} %fusion.134, f32[2,2,512]{2,1,0:T(2,128)S(1)} %get-tuple-element.650, f32[2,2,512]{2,1,0:T(2,128)S(1)} %dynamic-slice_bitcast_fusion.2, pred[512,2560]{1,0:T(8,128)(4,1)S(1)} %compare_and_fusion.5), kind=kLoop, calls=%fused_computation.25.clone.1 | loop fusion | flops 31457280 | bytes 53755904 | tf_op jit(solution)/shard_map/while/body/eval_jaxpr/convert_element_type | solution.py:259
  1062.5 15.2 fusion.135
  1077.7 15.7 %fusion.136 = bf16[2,2,512,2560]{3,2,1,0:T(8,128)(2,1)S(1)} fusion(f32[2,512,2,2560]{3,1,2,0:T(8,128)} %get-tuple-element.649, f32[2,512,2,2560]{3,1,2,0:T(8,128)} %fusion.134, f32[2,2,512]{2,1,0:T(2,128)S(1)} %get-tuple-element.650, f32[2,2,512]{2,1,0:T(2,128)S(1)} %dynamic-slice_bitcast_fusion.2, pred[512,2560]{1,0:T(8,128)(4,1)S(1)} %compare_and_fusion.5), kind=kLoop, calls=%fused_computation.25.clone.1 | loop fusion | flops 31457280 | bytes 53755904 | tf_op jit(solution)/shard_map/while/body/eval_jaxpr/convert_element_type | solution.py:259
  1125.9 15.2 fusion.135
  1141.1 15.7 %fusion.136 = bf16[2,2,512,2560]{3,2,1,0:T(8,128)(2,1)S(1)} fusion(f32[2,512,2,2560]{3,1,2,0:T(8,128)} %get-tuple-element.649, f32[2,512,2,2560]{3,1,2,0:T(8,128)} %fusion.134, f32[2,2,512]{2,1,0:T(2,128)S(1)} %get-tuple-element.650, f32[2,2,512]{2,1,0:T(2,128)S(1)} %dynamic-slice_bitcast_fusion.2, pred[512,2560]{1,0:T(8,128)(4,1)S(1)} %compare_and_fusion.5), kind=kLoop, calls=%fused_computation.25.clone.1 | loop fusion | flops 31457280 | bytes 53755904 | tf_op jit(solution)/shard_map/while/body/eval_jaxpr/convert_element_type | solution.py:259
  1189.3 15.2 fusion.135
  1204.5 15.7 %fusion.136 = bf16[2,2,512,2560]{3,2,1,0:T(8,128)(2,1)S(1)} fusion(f32[2,512,2,2560]{3,1,2,0:T(8,128)} %get-tuple-element.649, f32[2,512,2,2560]{3,1,2,0:T(8,128)} %fusion.134, f32[2,2,512]{2,1,0:T(2,128)S(1)} %get-tuple-element.650, f32[2,2,512]{2,1,0:T(2,128)S(1)} %dynamic-slice_bitcast_fusion.2, pred[512,2560]{1,0:T(8,128)(4,1)S(1)} %compare_and_fusion.5), kind=kLoop, calls=%fused_computation.25.clone.1 | loop fusion | flops 31457280 | bytes 53755904 | tf_op jit(solution)/shard_map/while/body/eval_jaxpr/convert_element_type | solution.py:259
  1304.9 31.9 %reduce-scatter.19.cloned.1.call-done = bf16[128,1024]{1,0:T(8,128)(2,1)} async-done(((bf16[1024,1024]{1,0:T(8,128)(2,1)}), bf16[128,1024]{1,0:T(8,128)(2,1)}) %reduce-scatter.19.cloned.1.call-update) | async-done | bytes 262160 | tf_op jit(solution)/shard_map/reduce_scatter | solution.py:323
  1340.0 92.7 %reduce-scatter.17.cloned.1.call-done = bf16[640,1024]{1,0:T(8,128)(2,1)} async-done(((bf16[2560,1024]{1,0:T(8,128)(2,1)}), bf16[640,1024]{1,0:T(8,128)(2,1)}) %reduce-scatter.17.cloned.1.call-update) | async-done | bytes 1310736 | tf_op jit(solution)/shard_map/reduce_scatter | solution.py:304
  1435.1 14.3 all-reduce.11
  1462.3 67.2 %reduce-scatter.13.cloned.1.call-done = bf16[640,1024]{1,0:T(8,128)(2,1)} async-done(((bf16[2560,1024]{1,0:T(8,128)(2,1)}), bf16[640,1024]{1,0:T(8,128)(2,1)}) %reduce-scatter.13.cloned.1.call-update) | async-done | bytes 1310736 | tf_op jit(solution)/shard_map/reduce_scatter | solution.py:178
  (370 shorter events, 571.7 us)
Async XLA Ops:
  7.2 37.5 %all-gather.13.cloned.1.call-start = ((), (), s32[]{:S(2)}) async-start(), calls=%async_computation.9 | async-start | bytes 2359296 | tf_op jit(solution)/shard_map/all_gather | solution.py:128
  9.1 132.4 %all-gather.11.cloned.1.call-start = ((), (), s32[]{:S(2)}) async-start(), calls=%async_computation.8 | async-start | bytes 6553600 | tf_op jit(solution)/shard_map/all_gather | solution.py:136
  22.7 290.0 %all-gather.15.cloned.1.call-start = ((), (), s32[]{:S(2)}) async-start(), calls=%async_computation.10 | async-start | bytes 1179648 | tf_op jit(solution)/shard_map/all_gather | solution.py:129
  23.4 389.0 %reduce-scatter.11.cloned.1.call-start = ((), (), s32[]{:S(2)}) async-start(), calls=%async_computation.11 | async-start | bytes 6553600 | tf_op jit(solution)/shard_map/reduce_scatter | solution.py:161
  320.0 127.6 %all-gather.19.cloned.1.call-start = ((), (), s32[]{:S(2)}) async-start(), calls=%async_computation.13 | async-start | bytes 3538944 | tf_op jit(solution)/shard_map/all_gather | solution.py:131
  321.8 225.9 %all-gather.17.cloned.1.call-start = ((), (), s32[]{:S(2)}) async-start(), calls=%async_computation.12 | async-start | bytes 6553600 | tf_op jit(solution)/shard_map/all_gather | solution.py:167
  330.6 465.9 %copy-start.37 = (f32[8,1,128]{2,1,0:T(1,128)}, f32[8,1,128]{2,1,0:T(1,128)S(1)}, u32[]{:S(2)}) copy-start(f32[8,1,128]{2,1,0:T(1,128)S(1)} %convert_element_type.198) | copy-start | bytes 12292
  414.4 382.1 %copy-start.39 = (f32[640]{0:T(1024)}, f32[640]{0:T(1024)S(1)}, u32[]{:S(2)}) copy-start(f32[640]{0:T(1024)S(1)} %fusion.74) | copy-start | bytes 7684
  416.0 157.9 %all-gather.21.cloned.1.call-start = ((), (), s32[]{:S(2)}) async-start(), calls=%async_computation.14 | async-start | bytes 1769472 | tf_op jit(solution)/shard_map/all_gather | solution.py:132
  416.8 256.8 %all-gather.23.cloned.1.call-start = ((), (), s32[]{:S(2)}) async-start(), calls=%async_computation.16 | async-start | bytes 6553600 | tf_op jit(solution)/shard_map/all_gather | solution.py:215
  417.5 375.9 %reduce-scatter.15.cloned.1.call-start = ((), (), s32[]{:S(2)}) async-start(), calls=%async_computation.17 | async-start | bytes 6553600 | tf_op jit(solution)/shard_map/reduce_scatter | solution.py:230
  701.1 196.3 %all-gather.25.cloned.1.call-start = ((), (), s32[]{:S(2)}) async-start(), calls=%async_computation.18 | async-start | bytes 6553600 | tf_op jit(solution)/shard_map/all_gather | solution.py:239
  798.6 500.5 %reduce-scatter.25.cloned.1.call-start = ((), (), s32[]{:S(2)}) async-start(), calls=%async_computation.23 | async-start | bytes 1769472
  808.2 492.8 %reduce-scatter.23.cloned.1.call-start = ((), (), s32[]{:S(2)}) async-start(), calls=%async_computation.22 | async-start | bytes 3538944 | tf_op jit(solution)/shard_map/reduce_scatter | solution.py:332
  823.5 479.5 %reduce-scatter.21.cloned.1.call-start = ((), (), s32[]{:S(2)}) async-start(), calls=%async_computation.21 | async-start | bytes 1179648 | tf_op jit(solution)/shard_map/reduce_scatter | solution.py:326
  1257.6 79.2 %reduce-scatter.19.cloned.1.call-start = ((), (), s32[]{:S(2)}) async-start(), calls=%async_computation.20 | async-start | bytes 2359296 | tf_op jit(solution)/shard_map/reduce_scatter | solution.py:323
  1278.1 154.6 %reduce-scatter.17.cloned.1.call-start = ((), (), s32[]{:S(2)}) async-start(), calls=%async_computation.19 | async-start | bytes 6553600 | tf_op jit(solution)/shard_map/reduce_scatter | solution.py:304
  1287.7 241.7 %reduce-scatter.13.cloned.1.call-start = ((), (), s32[]{:S(2)}) async-start(), calls=%async_computation.15 | async-start | bytes 6553600 | tf_op jit(solution)/shard_map/reduce_scatter | solution.py:178
  1297.7 135.0 %copy-start.2 = (bf16[640,1024]{1,0:T(8,128)(2,1)S(1)}, bf16[640,1024]{1,0:T(8,128)(2,1)}, u32[]{:S(2)}) copy-start(bf16[640,1024]{1,0:T(8,128)(2,1)} %param.19) | copy-start | bytes 3932164
  1303.0 159.3 %copy-start.46 = (f32[640]{0:T(1024)S(1)}, f32[640]{0:T(1024)}, u32[]{:S(2)}) copy-start(f32[640]{0:T(1024)} %copy-done.45) | copy-start | bytes 7684
  1303.0 226.4 %copy-start.9 = (bf16[640,1024]{1,0:T(8,128)(2,1)S(1)}, bf16[640,1024]{1,0:T(8,128)(2,1)}, u32[]{:S(2)}) copy-start(bf16[640,1024]{1,0:T(8,128)(2,1)} %reduce-scatter.11.cloned.1.call-done) | copy-start | bytes 3932164
  1303.0 226.5 %copy-start.38 = (f32[8,1,128]{2,1,0:T(1,128)S(1)}, f32[8,1,128]{2,1,0:T(1,128)}, u32[]{:S(2)}) copy-start(f32[8,1,128]{2,1,0:T(1,128)} %copy-done.37) | copy-start | bytes 12292
  1303.0 226.4 %copy-start.40 = (f32[640]{0:T(1024)S(1)}, f32[640]{0:T(1024)}, u32[]{:S(2)}) copy-start(f32[640]{0:T(1024)} %copy-done.39) | copy-start | bytes 7684
  1303.0 226.4 %copy-start.48 = (f32[640]{0:T(1024)S(1)}, f32[640]{0:T(1024)}, u32[]{:S(2)}) copy-start(f32[640]{0:T(1024)} %copy-done.47) | copy-start | bytes 7684
  (69 other events, 1465.2 us)
Sparse Core Ops, SparseCore 0:
  10.5 30.7 all-gather.12
  43.4 98.0 all-gather.10
  143.3 21.9 all-gather.14
  320.2 92.2 reduce-scatter.10
  414.8 32.8 all-gather.18
  449.7 98.0 all-gather.16
  549.6 24.2 all-gather.20
  575.5 98.0 all-gather.22
  701.2 92.1 reduce-scatter.14
  798.7 98.5 all-gather.24
  900.6 36.8 reduce-scatter.24
  940.8 46.1 reduce-scatter.22
  1257.7 34.2 reduce-scatter.20
  1295.5 41.2 reduce-scatter.18
  1338.9 93.7 reduce-scatter.16
  1434.8 94.5 reduce-scatter.12
where the time goes:
time: 1550 us; the launch traced here: 1540 us
  waiting for transfers between devices  779 us (50%)
  matrix products  411 us (27%)
  other arithmetic  194 us (13%)
  local copies, waits for them, and re-layouts  77.8 us (5%)
  blocking collectives  59.2 us (4%)
  between operations  17 us (1%)
    all_gather x1, waiting for transfers between devices, local(): lax.all_gather(rms_norm(middle, gathered[5].astype(jnp.float32)).astype(j...  100 us
    all_gather x1, waiting for transfers between devices, local(): cotangent_all = lax.all_gather(cotangent, 'tensor', axis=0, tiled=True)  99.7 us
    all_gather x1, waiting for transfers between devices, local(): lax.all_gather(rms_norm(inputs, gain_one).astype(jnp.bfloat16), 'tensor',...  96.7 us
    reduce_scatter x1, waiting for transfers between devices, local(): lax.psum_scatter(contract_columns(qkv_grad, joined_qkv).astype(jnp.bfloat...  92.7 us
    reduce_scatter x1, waiting for transfers between devices, local(): lax.psum_scatter(contract_columns(gate_up_grad, joined_gate_up).astype(jn...  91.8 us
    reduce_scatter x1, waiting for transfers between devices, local(): lax.psum_scatter(contract_columns(attended, output_fwd).astype(jnp.bfloat...  81.9 us
    convert_element_type x5, other arithmetic, backward_block(): score_grad = (probs * (probs_grad - inner)).astype(jnp.bfloat16)  79.8 us
    dot_general x10, matrix products, masked_scores(): jnp.einsum('qkgd,skd->kgqs', query_block, keys, preferred_element_type=jn...  76.6 us
  transfers between devices with their start and end apart: 16, of which 11 were waited for; matrix products, arithmetic and copies ran while one was open for 41% of the time, Pallas kernels for 0%

commit v1 on v0

v1 whole, which is shorter than its diff:
```python
import functools

import jax
import jax.numpy as jnp
from jax import lax
from jax.experimental import pallas as pl
from jax.experimental.pallas import tpu as pltpu
from jax.sharding import PartitionSpec as P

HEAD_SIZE = 128
EPSILON = 1e-06
THETA = 1000000.0
AXES = ("dp", "tensor")
BLOCK = 256
HIDDEN_BLOCK = 512
SCALE = HEAD_SIZE ** (-0.5)
LOG2E = 1.4426950408889634
VMEM_LIMIT = 56 * 1024 * 1024
F32 = jnp.float32
BF16 = jnp.bfloat16


def dot_nn(left, right):
    return lax.dot_general(left, right, (((1,), (0,)), ((), ())), preferred_element_type=F32)


def dot_nt(left, right):
    return lax.dot_general(left, right, (((1,), (1,)), ((), ())), preferred_element_type=F32)


def dot_tn(left, right):
    return lax.dot_general(left, right, (((0,), (0,)), ((), ())), preferred_element_type=F32)


def row_scale(rows):
    return lax.rsqrt(jnp.mean(rows * rows, axis=-1, keepdims=True) + EPSILON)


def rotate(rows, cosine, sine):
    return rows * cosine + pltpu.roll(rows, HEAD_SIZE // 2, 1) * sine


def unrotate(rows, cosine, sine):
    return rows * cosine - pltpu.roll(rows, HEAD_SIZE // 2, 1) * sine


def project_kernel(
    query_heads, key_heads, x_ref, gain_ref, w_ref, gq_ref, gk_ref, cos_ref, sin_ref, normed_ref, qkv_ref, scale_ref
):
    x = x_ref[...].astype(F32)
    normed = (x * row_scale(x) * gain_ref[...]).astype(BF16)
    normed_ref[...] = normed
    raw = dot_nn(normed, w_ref[...])
    cosine, sine = cos_ref[...], sin_ref[...]
    lane = lax.broadcasted_iota(jnp.int32, (x.shape[0], HEAD_SIZE), 1)
    scales = jnp.zeros((x.shape[0], HEAD_SIZE), F32)
    for head in range(query_heads + key_heads):
        span = slice(head * HEAD_SIZE, (head + 1) * HEAD_SIZE)
        u = raw[:, span]
        r = row_scale(u)
        gain = gq_ref[...] if head < query_heads else gk_ref[...]
        qkv_ref[:, span] = rotate(u * r * gain, cosine, sine).astype(BF16)
        scales = jnp.where(lane == head, r, scales)
    span = slice((query_heads + key_heads) * HEAD_SIZE, None)
    qkv_ref[:, span] = raw[:, span].astype(BF16)
    scale_ref[...] = scales


def project(x, gain, weights, gain_query, gain_key, cosine, sine, query_heads, key_heads):
    rows, width = x.shape
    wide = weights.shape[1]
    whole = lambda shape: pl.BlockSpec(shape, lambda i: (0, 0))
    block = lambda cols: pl.BlockSpec((BLOCK, cols), lambda i: (i, 0))
    return pl.pallas_call(
        functools.partial(project_kernel, query_heads, key_heads),
        grid=(rows // BLOCK,),
        in_specs=[
            block(width),
            whole((1, width)),
            whole((width, wide)),
            whole((1, HEAD_SIZE)),
            whole((1, HEAD_SIZE)),
            block(HEAD_SIZE),
            block(HEAD_SIZE),
        ],
        out_specs=[block(width), block(wide), block(HEAD_SIZE)],
        out_shape=[
            jax.ShapeDtypeStruct((rows, width), BF16),
            jax.ShapeDtypeStruct((rows, wide), BF16),
            jax.ShapeDtypeStruct((rows, HEAD_SIZE), F32),
        ],
        compiler_params=pltpu.CompilerParams(vmem_limit_bytes=VMEM_LIMIT),
        cost_estimate=pl.CostEstimate(
            flops=2 * rows * width * wide, bytes_accessed=2 * rows * (2 * width + wide), transcendentals=0
        ),
        name="project",
    )(x, gain, weights, gain_query, gain_key, cosine, sine)


def first_place(info_ref, blocks, docs, places):
    start = jnp.zeros_like(places)
    for doc in range(docs):
        begin = info_ref[2 * blocks + doc]
        start = jnp.maximum(start, jnp.where(places >= begin, begin, 0))
    return start


def forward_kernel(group, blocks, docs, info_ref, q_ref, k_ref, v_ref, o_ref, lse_ref, wide_ref, acc_ref):
    i = pl.program_id(1)

    @pl.when(i == 0)
    def _():
        wide_ref[:, :HEAD_SIZE] = v_ref[...]
        wide_ref[:, HEAD_SIZE:] = jnp.ones_like(v_ref)

    queries = jnp.concatenate([q_ref[:, h * HEAD_SIZE : (h + 1) * HEAD_SIZE] for h in range(group)], axis=0)
    acc_ref[...] = jnp.zeros_like(acc_ref)
    shape = (group * BLOCK, BLOCK)

    def step(j, masked):
        rows = pl.ds(pl.multiple_of(j * BLOCK, BLOCK), BLOCK)
        weights = jnp.exp2(dot_nt(queries, k_ref[rows, :]) * (SCALE * LOG2E))
        if masked:
            places = i * BLOCK + lax.rem(lax.broadcasted_iota(jnp.int32, (group * BLOCK, 1), 0), BLOCK)
            start = first_place(info_ref, blocks, docs, places)
            other = j * BLOCK + lax.broadcasted_iota(jnp.int32, shape, 1)
            weights = jnp.where((other <= places) & (other >= start), weights, 0.0)
        acc_ref[...] += dot_nn(weights.astype(BF16), wide_ref[rows, :])

    low, clear = info_ref[i], info_ref[blocks + i]

    def masked_step(j, carry):
        step(j, True)
        return carry

    def clear_step(j, carry):
        step(j, False)
        return carry

    lax.fori_loop(low, jnp.minimum(clear, i), masked_step, 0)
    lax.fori_loop(jnp.minimum(clear, i), i, clear_step, 0)
    step(i, True)
    total = acc_ref[:, HEAD_SIZE:]
    out = (acc_ref[:, :HEAD_SIZE] / total).astype(BF16)
    for h in range(group):
        o_ref[:, h * HEAD_SIZE : (h + 1) * HEAD_SIZE] = out[h * BLOCK : (h + 1) * BLOCK]
    lse_ref[0, 0] = lax.dot_general(
        jnp.full((8, HEAD_SIZE), 1.0 / HEAD_SIZE, F32),
        jnp.log2(total),
        (((1,), (1,)), ((), ())),
        precision=lax.Precision.HIGHEST,
        preferred_element_type=F32,
    )


def attention_forward(info, qkv, query_heads, key_heads, docs):
    rows = qkv.shape[0]
    blocks = rows // BLOCK
    group = query_heads // key_heads
    wide = group * HEAD_SIZE
    return pl.pallas_call(
        functools.partial(forward_kernel, group, blocks, docs),
        grid_spec=pltpu.PrefetchScalarGridSpec(
            num_scalar_prefetch=1,
            grid=(key_heads, blocks),
            in_specs=[
                pl.BlockSpec((BLOCK, wide), lambda h, i, s: (i, h)),
                pl.BlockSpec((rows, HEAD_SIZE), lambda h, i, s: (0, query_heads + h)),
                pl.BlockSpec((rows, HEAD_SIZE), lambda h, i, s: (0, query_heads + key_heads + h)),
            ],
            out_specs=[
                pl.BlockSpec((BLOCK, wide), lambda h, i, s: (i, h)),
                pl.BlockSpec((1, 1, 8, group * BLOCK), lambda h, i, s: (h, i, 0, 0)),
            ],
            scratch_shapes=[
                pltpu.VMEM((rows, 2 * HEAD_SIZE), BF16),
                pltpu.VMEM((group * BLOCK, 2 * HEAD_SIZE), F32),
            ],
        ),
        out_shape=[
            jax.ShapeDtypeStruct((rows, query_heads * HEAD_SIZE), BF16),
            jax.ShapeDtypeStruct((key_heads, blocks, 8, group * BLOCK), F32),
        ],
        compiler_params=pltpu.CompilerParams(vmem_limit_bytes=VMEM_LIMIT),
        cost_estimate=pl.CostEstimate(
            flops=3 * rows * rows * HEAD_SIZE * query_heads // 2,
            bytes_accessed=4 * rows * query_heads * HEAD_SIZE,
            transcendentals=rows * rows * query_heads // 3,
        ),
        name="attention_forward",
    )(info, qkv, qkv, qkv)


def backward_kernel(
    group,
    query_heads,
    blocks,
    docs,
    info_ref,
    q_ref,
    k_ref,
    v_ref,
    o_ref,
    do_ref,
    lse_ref,
    cos_ref,
    sin_ref,
    scale_ref,
    gq_ref,
    gk_ref,
    dq_ref,
    dk_ref,
    dv_ref,
    dgain_ref,
    dk_acc,
    dv_acc,
    dq_acc,
):
    kv, i = pl.program_id(0), pl.program_id(1)

    @pl.when(i == 0)
    def _():
        dk_acc[...] = jnp.zeros_like(dk_acc)
        dv_acc[...] = jnp.zeros_like(dv_acc)

    @pl.when((i == 0) & (kv == 0))
    def _():
        dgain_ref[...] = jnp.zeros_like(dgain_ref)

    def stacked(ref):
        return jnp.concatenate([ref[:, h * HEAD_SIZE : (h + 1) * HEAD_SIZE] for h in range(group)], axis=0)

    queries, grads = stacked(q_ref), stacked(do_ref)
    product = stacked(o_ref).astype(F32) * grads.astype(F32)
    delta = lax.dot_general(
        jnp.ones((8, HEAD_SIZE), F32),
        product,
        (((1,), (1,)), ((), ())),
        precision=lax.Precision.HIGHEST,
        preferred_element_type=F32,
    )[:1]
    lse = lse_ref[0, 0, :1]
    dq_acc[...] = jnp.zeros_like(dq_acc)
    shape = (BLOCK, group * BLOCK)

    def step(j, masked):
        rows = pl.ds(pl.multiple_of(j * BLOCK, BLOCK), BLOCK)
        keys, values = k_ref[rows, :], v_ref[rows, :]
        probs = jnp.exp2(dot_nt(keys, queries) * (SCALE * LOG2E) - lse)
        if masked:
            places = i * BLOCK + lax.rem(lax.broadcasted_iota(jnp.int32, (1, group * BLOCK), 1), BLOCK)
            start = first_place(info_ref, blocks, docs, places)
            other = j * BLOCK + lax.broadcasted_iota(jnp.int32, shape, 0)
            probs = jnp.where((other <= places) & (other >= start), probs, 0.0)
        score_grad = (probs * (dot_nt(values, grads) - delta)).astype(BF16)
        dv_acc[rows, :] += dot_nn(probs.astype(BF16), grads)
        dk_acc[rows, :] += dot_nn(score_grad, queries)
        dq_acc[...] += dot_tn(score_grad, keys)

    low, clear = info_ref[i], info_ref[blocks + i]

    def masked_step(j, carry):
        step(j, True)
        return carry

    def clear_step(j, carry):
        step(j, False)
        return carry

    lax.fori_loop(low, jnp.minimum(clear, i), masked_step, 0)
    lax.fori_loop(jnp.minimum(clear, i), i, clear_step, 0)
    step(i, True)

    lane = lax.broadcasted_iota(jnp.int32, (BLOCK, HEAD_SIZE), 1)

    def raw_grad(grad, rotated, rows, head, gain):
        cosine, sine = cos_ref[rows, :], sin_ref[rows, :]
        r = jnp.sum(jnp.where(lane == head, scale_ref[rows, :], 0.0), axis=1, keepdims=True)
        unit = unrotate(rotated.astype(F32), cosine, sine) / gain
        back = unrotate(grad * SCALE, cosine, sine)
        scaled = back * gain
        raw = r * (scaled - unit * jnp.mean(scaled * unit, axis=1, keepdims=True))
        return raw.astype(BF16), jnp.sum(back * unit, axis=0, keepdims=True)

    here = pl.ds(pl.multiple_of(i * BLOCK, BLOCK), BLOCK)
    for h in range(group):
        span = slice(h * HEAD_SIZE, (h + 1) * HEAD_SIZE)
        raw, gain_grad = raw_grad(
            dq_acc[h * BLOCK : (h + 1) * BLOCK, :], q_ref[:, span], here, kv * group + h, gq_ref[...]
        )
        dq_ref[:, span] = raw
        dgain_ref[0:1, :] += gain_grad

    @pl.when(i == blocks - 1)
    def _():
        dv_ref[...] = dv_acc[...].astype(BF16)

        def finish(b, carry):
            rows = pl.ds(pl.multiple_of(b * BLOCK, BLOCK), BLOCK)
            raw, gain_grad = raw_grad(dk_acc[rows, :], k_ref[rows, :], rows, query_heads + kv, gk_ref[...])
            dk_ref[rows, :] = raw
            dgain_ref[1:2, :] += gain_grad
            return carry

        lax.fori_loop(0, blocks, finish, 0)


def attention_backward(
    info, qkv, attended, grads, lse, cosine, sine, scales, gain_query, gain_key, query_heads, key_heads, docs
):
    rows = qkv.shape[0]
    blocks = rows // BLOCK
    group = query_heads // key_heads
    wide = group * HEAD_SIZE
    per_block = pl.BlockSpec((BLOCK, wide), lambda h, i, s: (i, h))
    whole = lambda shape: pl.BlockSpec(shape, lambda h, i, s: (0, 0))
    return pl.pallas_call(
        functools.partial(backward_kernel, group, query_heads, blocks, docs),
        grid_spec=pltpu.PrefetchScalarGridSpec(
            num_scalar_prefetch=1,
            grid=(key_heads, blocks),
            in_specs=[
                per_block,
                pl.BlockSpec((rows, HEAD_SIZE), lambda h, i, s: (0, query_heads + h)),
                pl.BlockSpec((rows, HEAD_SIZE), lambda h, i, s: (0, query_heads + key_heads + h)),
                per_block,
                per_block,
                pl.BlockSpec((1, 1, 8, group * BLOCK), lambda h, i, s: (h, i, 0, 0)),
                whole((rows, HEAD_SIZE)),
                whole((rows, HEAD_SIZE)),
                whole((rows, HEAD_SIZE)),
                whole((1, HEAD_SIZE)),
                whole((1, HEAD_SIZE)),
            ],
            out_specs=[
                per_block,
                pl.BlockSpec((rows, HEAD_SIZE), lambda h, i, s: (0, h)),
                pl.BlockSpec((rows, HEAD_SIZE), lambda h, i, s: (0, h)),
                whole((8, HEAD_SIZE)),
            ],
            scratch_shapes=[
                pltpu.VMEM((rows, HEAD_SIZE), F32),
                pltpu.VMEM((rows, HEAD_SIZE), F32),
                pltpu.VMEM((group * BLOCK, HEAD_SIZE), F32),
            ],
        ),
        out_shape=[
            jax.ShapeDtypeStruct((rows, query_heads * HEAD_SIZE), BF16),
            jax.ShapeDtypeStruct((rows, key_heads * HEAD_SIZE), BF16),
            jax.ShapeDtypeStruct((rows, key_heads * HEAD_SIZE), BF16),
            jax.ShapeDtypeStruct((8, HEAD_SIZE), F32),
        ],
        compiler_params=pltpu.CompilerParams(vmem_limit_bytes=VMEM_LIMIT),
        cost_estimate=pl.CostEstimate(
            flops=10 * rows * rows * HEAD_SIZE * query_heads // 2,
            bytes_accessed=10 * rows * query_heads * HEAD_SIZE,
            transcendentals=rows * rows * query_heads // 3,
        ),
        name="attention_backward",
    )(info, qkv, qkv, qkv, attended, grads, lse, cosine, sine, scales, gain_query, gain_key)


def feed_kernel(
    x_ref, xt_ref, c_ref, ct_ref, g_ref, u_ref, d_ref, out_ref, ng_ref, dg_ref, du_ref, dd_ref, act_s, gg_s, ug_s
):
    j = pl.program_id(0)
    rows_all, width = x_ref.shape
    chunk = rows_all // 2

    @pl.when(j == 0)
    def _():
        out_ref[...] = jnp.zeros_like(out_ref)
        ng_ref[...] = jnp.zeros_like(ng_ref)

    def rows_step(m, carry):
        rows = pl.ds(pl.multiple_of(m * chunk, chunk), chunk)
        gate = dot_nn(x_ref[rows, :], g_ref[...])
        upward = dot_nn(x_ref[rows, :], u_ref[...])
        act_grad = dot_nn(c_ref[rows, :], d_ref[...])
        sig = 1.0 / (1.0 + jnp.exp(-gate))
        silu = gate * sig
        act = (silu * upward).astype(BF16)
        up_grad = (act_grad * silu).astype(BF16)
        gate_grad = (act_grad * upward * sig * (1.0 + gate * (1.0 - sig))).astype(BF16)
        act_s[rows, :] = act
        ug_s[rows, :] = up_grad
        gg_s[rows, :] = gate_grad
        out_ref[rows, :] += dot_nt(act, d_ref[...])
        ng_ref[rows, :] += dot_nt(gate_grad, g_ref[...]) + dot_nt(up_grad, u_ref[...])
        return carry

    lax.fori_loop(0, rows_all // chunk, rows_step, 0)

    def grad_step(m, carry):
        rows = pl.ds(pl.multiple_of(m * BLOCK, BLOCK), BLOCK)
        dg_ref[rows, :] = dot_nn(xt_ref[rows, :], gg_s[...]).astype(BF16)
        du_ref[rows, :] = dot_nn(xt_ref[rows, :], ug_s[...]).astype(BF16)
        dd_ref[rows, :] = dot_nn(ct_ref[rows, :], act_s[...]).astype(BF16)
        return carry

    lax.fori_loop(0, width // BLOCK, grad_step, 0)


def feed(x, xt, cot, cot_t, first, second, head_columns, hidden):
    rows, width = x.shape
    hb = HIDDEN_BLOCK
    whole = lambda shape: pl.BlockSpec(shape, lambda j: (0, 0))
    at = lambda base: pl.BlockSpec((width, hb), lambda j: (0, base + j))
    shift = head_columns // hb
    steps = hidden // hb
    return pl.pallas_call(
        feed_kernel,
        grid=(steps,),
        in_specs=[
            whole((rows, width)),
            whole((width, rows)),
            whole((rows, width)),
            whole((width, rows)),
            at(shift),
            at(0),
            at(steps),
        ],
        out_specs=[whole((rows, width)), whole((rows, width)), at(0), at(0), at(0)],
        out_shape=[
            jax.ShapeDtypeStruct((rows, width), F32),
            jax.ShapeDtypeStruct((rows, width), F32),
            jax.ShapeDtypeStruct((width, hidden), BF16),
            jax.ShapeDtypeStruct((width, hidden), BF16),
            jax.ShapeDtypeStruct((width, hidden), BF16),
        ],
        scratch_shapes=[pltpu.VMEM((rows, hb), BF16)] * 3,
        compiler_params=pltpu.CompilerParams(vmem_limit_bytes=VMEM_LIMIT),
        cost_estimate=pl.CostEstimate(
            flops=18 * rows * width * hidden,
            bytes_accessed=12 * width * hidden + 16 * rows * width,
            transcendentals=rows * hidden,
        ),
        name="feed_forward",
    )(x, xt, cot, cot_t, first, second, second)


def local(
    tokens,
    lengths,
    row_order,
    attention_gain,
    query_gain,
    key_gain,
    query_weight,
    key_matrix,
    value_matrix,
    output_weight,
    feedforward_gain,
    gate_weight,
    up_weight,
    down_weight,
    cotangent,
):
    span = lax.axis_size("tensor")
    pairs = lax.axis_size("dp") // 2
    half = span // 2
    rows, width = tokens.shape
    group_rows = rows * span
    blocks = group_rows // BLOCK
    docs = lengths.shape[1]
    query_heads = query_weight.shape[1] // HEAD_SIZE
    key_heads = key_matrix.shape[1] // HEAD_SIZE
    head_columns = query_weight.shape[1]
    hidden_columns = gate_weight.shape[1]
    shard = query_weight.shape[0]

    dp, t = lax.axis_index("dp"), lax.axis_index("tensor")
    p, c = dp // 2, lax.rem(dp, 2)
    q = t // half
    settled = c == q

    def send(x, route):
        moves = []
        for pp in range(pairs):
            for cc in range(2):
                for tt in range(span):
                    to = route(pp, cc, tt)
                    if to is not None:
                        moves.append(((pp * 2 + cc) * span + tt, (to[0] * 2 + to[1]) * span + to[2]))
        return lax.ppermute(x, AXES, moves)

    def sibling(x):
        return send(x, lambda pp, cc, tt: (pp, 1 - cc, tt))

    def swap(x):
        moved = send(x, lambda pp, cc, tt: (pp, 1 - cc, span - 1 - tt) if cc != tt // half else None)
        return jnp.where(settled, x, moved)

    def ordered(mine, other, first):
        return jnp.where(first, mine, other), jnp.where(first, other, mine)

    swapped = swap(tokens)
    stack = [swapped]
    bit = 1
    while bit < half:
        moved = send(jnp.concatenate(stack, axis=0), lambda pp, cc, tt: (pp, cc, tt ^ bit))
        stack += [moved[k * rows : (k + 1) * rows] for k in range(len(stack))]
        bit *= 2
    moved = sibling(jnp.concatenate(stack, axis=0))
    tokens_all = jnp.concatenate(stack + [moved], axis=0)
    cot_own = swap(cotangent)

    heads_local = jnp.concatenate([query_weight, key_matrix, value_matrix], axis=1)
    moved = send(heads_local, lambda pp, cc, tt: (pp, 1 - cc, tt) if cc != tt // half else None)
    pair = jnp.concatenate(ordered(heads_local, moved, c == 0), axis=0)
    moved = send(pair, lambda pp, cc, tt: (pp, cc, (tt + half) % span) if cc == tt // half else None)
    pair = jnp.where(settled, pair, moved)

    def gather_pairs(x):
        size = x.shape[0]
        out = jnp.zeros((pairs * size, x.shape[1]), x.dtype)
        put = lambda out, piece, at, shift: lax.dynamic_update_slice(out, piece, (at * size + shift, 0))
        if pairs == 4:
            cut = size // 2
            one = send(x, lambda pp, cc, tt: (pp ^ 1, cc, tt))
            two = send(x, lambda pp, cc, tt: (pp ^ 2, cc, tt))
            upper = send(two[:cut], lambda pp, cc, tt: (pp ^ 1, cc, tt))
            lower = send(one[cut:], lambda pp, cc, tt: (pp ^ 2, cc, tt))
            out = put(out, x, p, 0)
            out = put(out, one, p ^ 1, 0)
            out = put(out, two, p ^ 2, 0)
            out = put(out, upper, p ^ 3, 0)
            return put(out, lower, p ^ 3, cut)
        pieces, bit = [x], 1
        while bit < pairs:
            moved = send(jnp.concatenate(pieces, axis=0), lambda pp, cc, tt: (pp ^ bit, cc, tt))
            pieces += [moved[k * size : (k + 1) * size] for k in range(len(pieces))]
            bit *= 2
        for k, piece in enumerate(pieces):
            out = put(out, piece, p ^ k, 0)
        return out

    def scatter_pairs(x):
        size = x.shape[0] // pairs
        take = lambda at, shift, count: lax.dynamic_slice(x, (at * size + shift, 0), (count, x.shape[1]))
        if pairs == 4:
            cut = size // 2
            upper = send(take(p ^ 3, 0, cut), lambda pp, cc, tt: (pp ^ 1, cc, tt))
            lower = send(take(p ^ 3, cut, cut), lambda pp, cc, tt: (pp ^ 2, cc, tt))
            one = jnp.concatenate(
                [take(p ^ 1, 0, cut), (take(p ^ 1, cut, cut).astype(F32) + lower.astype(F32)).astype(BF16)], axis=0
            )
            two = jnp.concatenate(
                [(take(p ^ 2, 0, cut).astype(F32) + upper.astype(F32)).astype(BF16), take(p ^ 2, cut, cut)], axis=0
            )
            one = send(one, lambda pp, cc, tt: (pp ^ 1, cc, tt))
            two = send(two, lambda pp, cc, tt: (pp ^ 2, cc, tt))
            return (take(p, 0, size).astype(F32) + one.astype(F32) + two.astype(F32)).astype(BF16)
        pieces = [take(p ^ k, 0, size) for k in range(pairs)]
        while len(pieces) > 1:
            keep = len(pieces) // 2
            moved = send(jnp.concatenate(pieces[keep:], axis=0), lambda pp, cc, tt: (pp ^ keep, cc, tt))
            pieces = [
                (pieces[k].astype(F32) + moved[k * size : (k + 1) * size].astype(F32)).astype(BF16)
                for k in range(keep)
            ]
        return pieces[0]

    heads_weights = gather_pairs(pair)

    def halves(x):
        middle = x.shape[1] // 2
        return x[:, :middle], x[:, middle:]

    def wide_gather(parts):
        split = [halves(part) for part in parts]
        mine = jnp.concatenate([jnp.where(c == 0, a, b) for a, b in split], axis=1)
        theirs = jnp.concatenate([jnp.where(c == 0, b, a) for a, b in split], axis=1)
        moved = sibling(theirs)
        joined = jnp.concatenate(ordered(mine, moved, c == 0), axis=0)
        pieces = [joined] + [send(joined, lambda pp, cc, tt: (pp, cc, tt ^ r)) for r in range(1, span)]
        spread, at = [], 0
        for part in parts:
            wide = part.shape[1] // 2
            spread += [piece[:, at : at + wide] for piece in pieces]
            at += wide
        return gather_pairs(jnp.concatenate(spread, axis=1))

    first_own = wide_gather([output_weight.T, gate_weight])
    second_own = wide_gather([up_weight, down_weight.T])
    first_sib = sibling(first_own)
    second_sib = sibling(second_own)

    gains = jnp.concatenate([attention_gain, query_gain, key_gain, feedforward_gain])
    gains = lax.all_gather(gains, "dp", axis=0).astype(F32)
    small, tiny = attention_gain.shape[0], query_gain.shape[0]
    gain_one = gains[:, :small].reshape(1, width)
    gain_query = gains[:, small : small + tiny].reshape(1, HEAD_SIZE)
    gain_key = gains[:, small + tiny : small + 2 * tiny].reshape(1, HEAD_SIZE)
    gain_two = gains[:, small + 2 * tiny :].reshape(1, width)

    facts = jnp.concatenate([row_order[0], lengths[0]])
    facts = jnp.where(settled, facts, sibling(facts))
    order, length = facts[:group_rows].reshape(span, rows), facts[group_rows:]
    places = []
    for k in range(span):
        tt, cc = t ^ (k % half), c ^ (k // half)
        places.append(lax.dynamic_index_in_dim(order, jnp.where(cc == tt // half, tt, span - 1 - tt), 0, False))
    places = jnp.concatenate(places)
    inverse = jnp.argsort(places)
    before = jnp.arange(docs)[None, :] < jnp.arange(docs)[:, None]
    starts = jnp.sum(jnp.where(before, length[None, :], 0), axis=1).astype(jnp.int32)

    def start_of(place):
        return jnp.max(jnp.where(place[:, None] >= starts[None, :], starts[None, :], 0), axis=1)

    index = jnp.arange(blocks, dtype=jnp.int32) * BLOCK
    low = start_of(index) // BLOCK
    clear = (start_of(index + BLOCK - 1) + BLOCK - 1) // BLOCK
    info = jnp.concatenate([low, clear, starts]).astype(jnp.int32)
    index = jnp.arange(group_rows, dtype=jnp.int32)
    position = (index - start_of(index)).astype(F32)
    inverse_rate = THETA ** (-(jnp.arange(HEAD_SIZE // 2, dtype=F32) * 2.0 / HEAD_SIZE))
    angle = position[:, None] * inverse_rate[None, :]
    cosine, sine = jnp.cos(angle), jnp.sin(angle)
    cosine = jnp.concatenate([cosine, cosine], axis=1)
    sine = jnp.concatenate([-sine, sine], axis=1)

    tokens_sorted = jnp.take(tokens_all, inverse, axis=0, mode="clip")
    normed, qkv, scales = project(
        tokens_sorted, gain_one, heads_weights, gain_query, gain_key, cosine, sine, query_heads, key_heads
    )
    attended, lse = attention_forward(info, qkv, query_heads, key_heads, docs)
    attended_rows = jnp.take(attended, places, axis=0, mode="clip")

    def exchange(parts):
        out = [parts[0]]
        for k in range(1, span):
            out.append(send(parts[k], lambda pp, cc, tt: (pp, cc ^ (k // half), tt ^ (k % half))))
        return out

    arrived = exchange([attended_rows[k * rows : (k + 1) * rows] for k in range(span)])
    by_chunk = [
        jnp.where(settled, arrived[r], arrived[(1 - r // half) * half + r % half]) for r in range(span)
    ]
    split = [halves(piece) for piece in by_chunk]
    mixed_own = jnp.concatenate([jnp.where(c == 0, a, b) for a, b in split], axis=1)
    mixed_sib = jnp.concatenate([jnp.where(c == 0, b, a) for a, b in split], axis=1)
    columns = mixed_own.shape[1]
    inputs = swapped.astype(F32)
    middle = inputs + (dot_nt(mixed_own, first_own[:, :columns]) + dot_nt(mixed_sib, first_sib[:, :columns]))

    r_two = row_scale(middle)
    unit_two = middle * r_two
    normed_two = (unit_two * gain_two).astype(BF16)
    normed_two_t, cot_t = normed_two.T, cot_own.T
    hidden = span * (hidden_columns // 2)
    sib = feed(normed_two, normed_two_t, cot_own, cot_t, first_sib, second_sib, columns, hidden)
    own = feed(normed_two, normed_two_t, cot_own, cot_t, first_own, second_own, columns, hidden)
    layer_output = swap((middle + (own[0] + sib[0])).astype(BF16))
    normed_two_grad = own[1] + sib[1]
    gain_two_grad = jnp.sum(normed_two_grad * unit_two, axis=0)
    scaled = normed_two_grad * gain_two
    middle_grad = cot_own.astype(F32) + r_two * (
        scaled - unit_two * jnp.mean(scaled * unit_two, axis=-1, keepdims=True)
    )
    branch = middle_grad.astype(BF16)

    grad_own = dot_nn(branch, first_own[:, :columns]).astype(BF16)
    grad_sib = dot_nn(branch, first_sib[:, :columns]).astype(BF16)
    wide = columns // span
    by_chunk = []
    for r in range(span):
        a, b = ordered(grad_own[:, r * wide : (r + 1) * wide], grad_sib[:, r * wide : (r + 1) * wide], c == 0)
        by_chunk.append(jnp.concatenate([a, b], axis=1))
    arrived = exchange(
        [jnp.where(settled, by_chunk[k], by_chunk[(1 - k // half) * half + k % half]) for k in range(span)]
    )
    attended_grad = jnp.take(jnp.concatenate(arrived, axis=0), inverse, axis=0, mode="clip")
    query_grad, key_grad, value_grad, head_gains = attention_backward(
        info,
        qkv,
        attended,
        attended_grad,
        lse,
        cosine,
        sine,
        scales,
        gain_query,
        gain_key,
        query_heads,
        key_heads,
        docs,
    )
    qkv_grad = jnp.concatenate([query_grad, key_grad, value_grad], axis=1)
    partial = dot_nt(jnp.take(qkv_grad, places, axis=0, mode="clip"), heads_weights).astype(BF16)
    parts = [partial[k * rows : (k + 1) * rows] for k in range(span)]
    moved = sibling(jnp.concatenate(parts[half:], axis=0))
    parts = [
        (parts[k].astype(F32) + moved[k * rows : (k + 1) * rows].astype(F32)).astype(BF16) for k in range(half)
    ]
    while len(parts) > 1:
        keep = len(parts) // 2
        moved = send(jnp.concatenate(parts[keep:], axis=0), lambda pp, cc, tt: (pp, cc, tt ^ keep))
        parts = [
            (parts[k].astype(F32) + moved[k * rows : (k + 1) * rows].astype(F32)).astype(BF16) for k in range(keep)
        ]
    normed_grad = parts[0].astype(F32)
    r_one = row_scale(inputs)
    unit_one = inputs * r_one
    gain_one_grad = jnp.sum(normed_grad * unit_one, axis=0)
    scaled = normed_grad * gain_one
    input_grad = swap(
        (middle_grad + r_one * (scaled - unit_one * jnp.mean(scaled * unit_one, axis=-1, keepdims=True))).astype(BF16)
    )

    def wide_scatter(own_parts, sib_parts):
        moved = sibling(jnp.concatenate(sib_parts, axis=1))
        total = (jnp.concatenate(own_parts, axis=1).astype(F32) + moved.astype(F32)).astype(BF16)
        total = scatter_pairs(total)
        widths = [part.shape[1] // span for part in own_parts]
        pieces = []
        for r in range(span):
            at, cols = 0, []
            for w in widths:
                cols.append(total[:, at + r * w : at + (r + 1) * w])
                at += span * w
            pieces.append(jnp.concatenate(cols, axis=1))
        summed = pieces[0].astype(F32)
        for r in range(1, span):
            summed = summed + send(pieces[r], lambda pp, cc, tt: (pp, cc, tt ^ r)).astype(F32)
        top, bottom = summed[:shard], summed[shard:]
        mine, theirs = jnp.where(c == 0, top, bottom), jnp.where(c == 0, bottom, top)
        moved = sibling(theirs.astype(BF16)).astype(F32)
        low_half, high_half = ordered(mine, moved, c == 0)
        out, at = [], 0
        for w in widths:
            out.append(jnp.concatenate([low_half[:, at : at + w], high_half[:, at : at + w]], axis=1))
            at += w
        return out

    up_grad, down_grad = wide_scatter(own[3:5], sib[3:5])
    output_grads = [dot_tn(branch, mixed).astype(BF16) for mixed in (mixed_own, mixed_sib)]
    output_grad, gate_grad = wide_scatter([output_grads[0], own[2]], [output_grads[1], sib[2]])

    heads_grad = dot_tn(normed, qkv_grad).astype(BF16)
    mine = scatter_pairs(heads_grad)
    moved = send(mine, lambda pp, cc, tt: (pp, cc, (tt + half) % span) if cc != tt // half else None)
    summed = mine.astype(F32) + moved.astype(F32)
    top, bottom = summed[:shard], summed[shard:]
    theirs = jnp.where(c == 0, bottom, top).astype(BF16)
    moved = send(theirs, lambda pp, cc, tt: (pp, 1 - cc, tt) if cc == tt // half else None).astype(F32)
    summed = jnp.where(settled, jnp.where(c == 0, top, bottom), moved)
    key_columns = key_heads * HEAD_SIZE

    gain_sums = lax.psum(
        jnp.concatenate([gain_one_grad, head_gains[0], head_gains[1], gain_two_grad]), AXES
    )
    cut = lambda at, size: lax.dynamic_slice(gain_sums, (at + dp * size,), (size,))
    return (
        layer_output,
        input_grad,
        cut(0, small),
        cut(width, tiny),
        cut(width + HEAD_SIZE, tiny),
        summed[:, :head_columns],
        summed[:, head_columns : head_columns + key_columns],
        summed[:, head_columns + key_columns :],
        output_grad.T,
        cut(width + 2 * HEAD_SIZE, small),
        gate_grad,
        up_grad,
        down_grad.T,
    )


def solution(mesh):
    placed = (
        P(AXES, None),
        P("dp", None),
        P("dp", None),
        P("dp"),
        P("dp"),
        P("dp"),
        P("dp", "tensor"),
        P("dp", "tensor"),
        P("dp", "tensor"),
        P("tensor", "dp"),
        P("dp"),
        P("dp", "tensor"),
        P("dp", "tensor"),
        P("tensor", "dp"),
        P(AXES, None),
    )
    return jax.shard_map(
        local,
        mesh=mesh,
        in_specs=placed,
        out_specs=(
            P(AXES, None),
            P(AXES, None),
            P("dp"),
            P("dp"),
            P("dp"),
            P("dp", "tensor"),
            P("dp", "tensor"),
            P("dp", "tensor"),
            P("tensor", "dp"),
            P("dp"),
            P("dp", "tensor"),
            P("dp", "tensor"),
            P("tensor", "dp"),
        ),
        check_vma=False,
    )
```

time: 1550 us -> 914 us (0.59)
  waiting for transfers between devices: 779 us -> 313 us
  matrix products: 411 us -> 37.7 us
  Pallas kernels: 0 us -> 179 us
  other arithmetic: 194 us -> 79.7 us
  starting transfers between devices: 1.06 us -> 110 us
  local copies, waits for them, and re-layouts: 77.8 us -> 126 us
    all_gather x8 -> x0, waiting for transfers between devices: 412 us -> none  [the longest x1 100 us: local(): lax.all_gather(rms_norm(middle, gathered[5].astype(jnp.float32)).astype(j...]
    dot_general x47 -> x8, matrix products: 411 us -> 37.7 us  [the longest x3 15.6 us: dot_nt(): lax.dot_general(left, right, (((1,), (1,)), ((), ())), preferred_element_...]
    reduce_scatter x7 -> x0, waiting for transfers between devices: 365 us -> none  [the longest x1 92.7 us: local(): lax.psum_scatter(contract_columns(qkv_grad, joined_qkv).astype(jnp.bfloat...]
    ppermute x0 -> x63, waiting for transfers between devices: none -> 313 us  [send(): return lax.ppermute(x, AXES, moves)]
    pallas_call x0 -> x5, Pallas kernels: none -> 179 us  [the longest x1 64.5 us: attention_backward(): pl.pallas_call(functools.partial(backward_kernel, group, query_heads, blo...]
    ppermute x0 -> x63, starting transfers between devices: none -> 110 us  [send(): return lax.ppermute(x, AXES, moves)]
    convert_element_type x16, other arithmetic: 89.9 us -> 29.1 us  [the longest x2 10.9 us: wide_scatter(): (jnp.concatenate(own_parts, axis=1).astype(F32) + moved.astype(F32)).asty...]
    gather x0 -> x4, local copies, waits for them, and re-layouts: none -> 48.9 us  [the longest x1 15.6 us: local(): jnp.take(qkv_grad, places, axis=0, mode='clip')]
  transfers between devices with their start and end apart: 16 -> 63, of which waited for: 11 -> 30; matrix products, arithmetic and copies ran while one was open for 41% -> 23% of each run, Pallas kernels for 0% -> 16%
where the time goes in v1:
time: 914 us; the launch traced here: 902 us
  waiting for transfers between devices  313 us (34%)
  Pallas kernels  179 us (20%)
  local copies, waits for them, and re-layouts  126 us (14%)
  starting transfers between devices  110 us (12%)
  other arithmetic  79.7 us (9%)
  blocking collectives  54 us (6%)
  matrix products  37.7 us (4%)
    ppermute x63, waiting for transfers between devices, send(): return lax.ppermute(x, AXES, moves)  313 us
    ppermute x63, starting transfers between devices, send(): return lax.ppermute(x, AXES, moves)  110 us
    pallas_call x1, Pallas kernels, attention_backward(): pl.pallas_call(functools.partial(backward_kernel, group, query_heads, blo...  64.5 us
    pallas_call x2, Pallas kernels, feed(): pl.pallas_call(feed_kernel, grid=(steps,), in_specs=[whole((rows, width))...  63.1 us
    psum x1, blocking collectives, local(): lax.psum(jnp.concatenate([gain_one_grad, head_gains[0], head_gains[1], ga...  39.5 us
    pallas_call x1, Pallas kernels, attention_forward(): pl.pallas_call(functools.partial(forward_kernel, group, blocks, docs), gr...  36.2 us
    unnamed x103, local copies, waits for them, and re-layouts  24.5 us
  transfers between devices with their start and end apart: 63, of which 30 were waited for; matrix products, arithmetic and copies ran while one was open for 23% of the time, Pallas kernels for 16%

profile of v1, /device:TPU:0, one launch (start us, length us, event | category | flops | bytes accessed | tf_op | source)
XLA Modules:
  0.0 901.9 jit_solution(6280668976777112951)
XLA Ops:
  20.7 14.6 %all-reduce = bf16[2304]{0:T(1024)(128)(2,1)S(1)} all-reduce(bf16[2304]{0:T(1024)(128)(2,1)S(1)} %dynamic-update-slice), channel_id=2, replica_groups=mesh['dp'=8,'tensor'=4] {'dp'}, use_global_device_ids=true, to_apply=%add | all-reduce | flops 2304 | bytes 9216
  59.2 11.6 %collective-permute-done.14 = bf16[256,640]{1,0:T(8,128)(2,1)S(1)} collective-permute-done((bf16[256,640]{1,0:T(8,128)(2,1)S(1)}, bf16[256,640]{1,0:T(8,128)(2,1)S(1)}, u32[]{:S(2)}, u32[]{:S(2)}) %collective-permute-start.14) | collective-permute-done | bytes 327712 | tf_op jit(solution)/shard_map/ppermute | solution.py:485
  80.4 29.0 %collective-permute-start.5 = (bf16[256,1024]{1,0:T(8,128)(2,1)S(1)}, bf16[256,1024]{1,0:T(8,128)(2,1)S(1)}, u32[]{:S(2)}, u32[]{:S(2)}) collective-permute-start(bf16[256,1024]{1,0:T(8,128)(2,1)S(1)} %pad_maximum_fusion.17), channel_id=1, source_target_pairs={{0,2},{1,3},{6,4},{7,5},{8,10},{9,11},{14,12},{15,13},{16,18},{17,... | collective-permute-start | bytes 1572872 | tf_op jit(solution)/shard_map/ppermute | solution.py:485
  119.0 33.8 %collective-permute-done.7 = bf16[256,1024]{1,0:T(8,128)(2,1)S(1)} collective-permute-done((bf16[256,1024]{1,0:T(8,128)(2,1)S(1)}, bf16[256,1024]{1,0:T(8,128)(2,1)S(1)}, u32[]{:S(2)}, u32[]{:S(2)}) %collective-permute-start.7) | collective-permute-done | bytes 524320 | tf_op jit(solution)/shard_map/ppermute | solution.py:485
  170.9 18.8 %collective-permute-done.2 = bf16[640,1024]{0,1:T(8,128)(2,1)S(1)} collective-permute-done((bf16[640,1024]{0,1:T(8,128)(2,1)S(1)}, bf16[640,1024]{0,1:T(8,128)(2,1)S(1)}, u32[]{:S(2)}, u32[]{:S(2)}) %collective-permute-start.2) | collective-permute-done | bytes 1310752 | tf_op jit(solution)/shard_map/ppermute | solution.py:485
  239.6 15.2 %gather_fusion = bf16[2560,1024]{1,0:T(8,128)(2,1)} fusion(bf16[2560,1024]{1,0:T(8,128)(2,1)} %copy.54, s32[3072]{0:T(1024)S(1)} %pad_clamp_fusion.1), kind=kCustom, calls=%fused_computation | custom fusion | bytes 10496000 | tf_op jit(solution)/shard_map/jit(_take)/gather | solution.py:624
  254.8 15.1 %project.1 = (bf16[2560,1024]{1,0:T(8,128)(2,1)}, bf16[2560,1024]{1,0:T(8,128)(2,1)}, f32[2560,128]{1,0:T(8,128)}) custom-call(bf16[2560,1024]{1,0:T(8,128)(2,1)} %gather_fusion, f32[1,1024]{1,0:T(1,128)} %bitcast.34, bf16[1024,1024]{1,0:T(8,128)(2,1)} %copy-done.13, f32[1,128]{1,0:T(1,128)} %reshape.89.gq_ref, f32[1,128]{1,0:T(1,128)} %reshape.90.gk_ref, ...), custom_call_target="tpu_custom_call" | custom-call | flops 5368709120 | bytes 15728640 | tf_op jit(solution)/shard_map/project/pallas_call | solution.py:74
  269.9 36.2 %attention_forward.1 = (bf16[2560,512]{1,0:T(8,128)(2,1)}, f32[2,10,8,512]{3,2,1,0:T(8,128)}) custom-call(s32[22]{0:T(128)} %pad_add_fusion.2.info_ref, bf16[2560,1024]{1,0:T(8,128)(2,1)} %get-tuple-element.34.q_ref.k_ref.v_ref, bf16[2560,1024]{1,0:T(8,128)(2,1)} %get-tuple-element.34.q_ref.k_ref.v_ref, bf16[2560,1024]{1,0:T(8,128)(2,1)} %get-tuple-element.34.q_ref.k_ref.v_ref), custom_call_target="tpu_custom_call" | custom-call | flops 5033164800 | bytes 5242880 | tf_op jit(solution)/shard_map/attention_forward/pallas_call | solution.py:161
  306.1 9.8 %gather_fusion.1 = bf16[2560,512]{1,0:T(8,128)(2,1)S(1)} fusion(bf16[2560,512]{1,0:T(8,128)(2,1)} %get-tuple-element.35.o_ref, s32[3072]{0:T(1024)S(1)} %pad_clamp_fusion), kind=kCustom, calls=%fused_computation.1 | custom fusion | bytes 5253120 | tf_op jit(solution)/shard_map/jit(_take)/gather | solution.py:629
  325.8 12.9 %collective-permute-done.11 = bf16[640,512]{1,0:T(8,128)(2,1)S(1)} collective-permute-done((bf16[640,512]{1,0:T(8,128)(2,1)}, bf16[640,512]{1,0:T(8,128)(2,1)S(1)}, u32[]{:S(2)}, u32[]{:S(2)}) %collective-permute-start.11) | collective-permute-done | bytes 655392 | tf_op jit(solution)/shard_map/ppermute | solution.py:485
  338.6 13.0 %collective-permute-done.12 = bf16[640,512]{1,0:T(8,128)(2,1)} collective-permute-done((bf16[640,512]{1,0:T(8,128)(2,1)}, bf16[640,512]{1,0:T(8,128)(2,1)}, u32[]{:S(2)}, u32[]{:S(2)}) %collective-permute-start.12) | collective-permute-done | bytes 655392 | tf_op jit(solution)/shard_map/ppermute | solution.py:485
  365.7 31.8 %feed_forward.2 = (f32[640,1024]{1,0:T(8,128)}, f32[640,1024]{1,0:T(8,128)}, bf16[1024,1536]{1,0:T(8,128)(2,1)}, bf16[1024,1536]{1,0:T(8,128)(2,1)}, bf16[1024,1536]{1,0:T(8,128)(2,1)}) custom-call(bf16[640,1024]{1,0:T(8,128)(2,1)} %copy.61.x_ref, bf16[1024,640]{1,0:T(8,128)(2,1)} %fusion.65.xt_ref, bf16[640,1024]{1,0:T(8,128)(2,1)} %copy.62.c_ref, ...), custom_call_target="tpu_custom_call" | custom-call | flops 18119393280 | bytes 29360128 | tf_op jit(solution)/shard_map/feed_forward/pallas_call | solution.py:411
  404.0 31.3 %feed_forward.3 = (f32[640,1024]{1,0:T(8,128)}, f32[640,1024]{1,0:T(8,128)}, bf16[1024,1536]{1,0:T(8,128)(2,1)}, bf16[1024,1536]{1,0:T(8,128)(2,1)}, bf16[1024,1536]{1,0:T(8,128)(2,1)}) custom-call(bf16[640,1024]{1,0:T(8,128)(2,1)} %copy.61.x_ref, bf16[1024,640]{1,0:T(8,128)(2,1)} %fusion.65.xt_ref, bf16[640,1024]{1,0:T(8,128)(2,1)} %copy.62.c_ref, ...), custom_call_target="tpu_custom_call" | custom-call | flops 18119393280 | bytes 29360128 | tf_op jit(solution)/shard_map/feed_forward/pallas_call | solution.py:411
  478.2 12.4 %collective-permute-done.35 = bf16[640,512]{1,0:T(8,128)(2,1)S(1)} collective-permute-done((bf16[640,512]{1,0:T(8,128)(2,1)S(1)}, bf16[640,512]{1,0:T(8,128)(2,1)S(1)}, u32[]{:S(2)}, u32[]{:S(2)}) %collective-permute-start.35) | collective-permute-done | bytes 655392 | tf_op jit(solution)/shard_map/ppermute | solution.py:485
  500.9 64.5 %attention_backward.1 = (bf16[2560,512]{1,0:T(8,128)(2,1)}, bf16[2560,256]{1,0:T(8,128)(2,1)}, bf16[2560,256]{1,0:T(8,128)(2,1)}, f32[8,128]{1,0:T(8,128)}) custom-call(s32[22]{0:T(128)} %pad_add_fusion.2.info_ref, bf16[2560,1024]{1,0:T(8,128)(2,1)} %get-tuple-element.34.q_ref.k_ref.v_ref, bf16[2560,1024]{1,0:T(8,128)(2,1)} %get-tuple-element.34.q_ref.k_ref.v_ref, ...), custom_call_target="tpu_custom_call" | custom-call | flops 16777216000 | bytes 13107200 | tf_op jit(solution)/shard_map/attention_backward/pallas_call | solution.py:317
  571.9 15.6 %gather_fusion.3 = bf16[2560,1024]{1,0:T(8,128)(2,1)} fusion(bf16[2560,1024]{1,0:T(8,128)(2,1)} %constant_dynamic-update-slice_fusion.3, s32[3072]{0:T(1024)S(1)} %pad_clamp_fusion), kind=kCustom, calls=%fused_computation.3 | custom fusion | bytes 10496000 | tf_op jit(solution)/shard_map/jit(_take)/gather | solution.py:691
  598.7 9.1 %convolution_convert_fusion.1 = bf16[1024,1024]{1,0:T(8,128)(2,1)S(1)} fusion(bf16[2560,1024]{1,0:T(8,128)(2,1)} %get-tuple-element.46, bf16[2560,1024]{1,0:T(8,128)(2,1)} %constant_dynamic-update-slice_fusion.3), kind=kOutput, calls=%fused_computation.37 | convolution fusion | flops 5369757696 | bytes 12582912 | tf_op jit(solution)/shard_map/dot_general | solution.py:32
  610.1 10.3 %collective-permute-start.39 = (bf16[128,1024]{1,0:T(8,128)(2,1)}, bf16[128,1024]{1,0:T(8,128)(2,1)}, u32[]{:S(2)}, u32[]{:S(2)}) collective-permute-start(bf16[128,1024]{1,0:T(8,128)(2,1)} %get-tuple-element.124), channel_id=1, source_target_pairs={{0,16},{1,17},{2,18},{3,19},{4,20},{5,21},{6,22},{7,23},{8,24},{9,... | collective-permute-start | bytes 786440 | tf_op jit(solution)/shard_map/ppermute | solution.py:485
  651.1 36.2 %collective-permute-done.43 = bf16[256,1024]{1,0:T(8,128)(2,1)S(1)} collective-permute-done((bf16[256,1024]{1,0:T(8,128)(2,1)S(1)}, bf16[256,1024]{1,0:T(8,128)(2,1)S(1)}, u32[]{:S(2)}, u32[]{:S(2)}) %collective-permute-start.43) | collective-permute-done | bytes 524320 | tf_op jit(solution)/shard_map/ppermute | solution.py:485
  699.5 39.5 %psum.7 = f32[2304]{0:T(1024)S(1)} all-reduce(f32[2304]{0:T(1024)S(1)} %pad_maximum_fusion.38), channel_id=1, replica_groups=mesh['dp'=8,'tensor'=4] {'dp','tensor'}, use_global_device_ids=true, to_apply=%region_11.12 | all-reduce | flops 2304 | bytes 18432 | tf_op jit(solution)/shard_map/psum | solution.py:751
  768.7 12.2 %collective-permute-done.55 = bf16[128,3072]{1,0:T(8,128)(2,1)S(1)} collective-permute-done((bf16[128,3072]{1,0:T(8,128)(2,1)S(1)}, bf16[128,3072]{1,0:T(8,128)(2,1)S(1)}, u32[]{:S(2)}, u32[]{:S(2)}) %collective-permute-start.55) | collective-permute-done | bytes 786464 | tf_op jit(solution)/shard_map/ppermute | solution.py:485
  785.8 25.2 %collective-permute-done.47 = bf16[256,2560]{1,0:T(8,128)(2,1)S(1)} collective-permute-done((bf16[256,2560]{1,0:T(8,128)(2,1)S(1)}, bf16[256,2560]{1,0:T(8,128)(2,1)S(1)}, u32[]{:S(2)}, u32[]{:S(2)}) %collective-permute-start.47) | collective-permute-done | bytes 1310752 | tf_op jit(solution)/shard_map/ppermute | solution.py:485
  823.6 27.1 %collective-permute-done.51 = bf16[256,640]{1,0:T(8,128)(2,1)S(1)} collective-permute-done((bf16[256,640]{1,0:T(8,128)(2,1)S(1)}, bf16[256,640]{1,0:T(8,128)(2,1)S(1)}, u32[]{:S(2)}, u32[]{:S(2)}) %collective-permute-start.51) | collective-permute-done | bytes 327712 | tf_op jit(solution)/shard_map/ppermute | solution.py:485
  873.8 23.8 %collective-permute-done.60 = bf16[256,768]{1,0:T(8,128)(2,1)S(1)} collective-permute-done((bf16[256,768]{1,0:T(8,128)(2,1)}, bf16[256,768]{1,0:T(8,128)(2,1)S(1)}, u32[]{:S(2)}, u32[]{:S(2)}) %collective-permute-start.60) | collective-permute-done | bytes 393248 | tf_op jit(solution)/shard_map/ppermute | solution.py:485
  (384 shorter events, 349.8 us)
Async XLA Ops:
  3.6 51.3 %collective-permute-start.23 = (bf16[128,768]{1,0:T(8,128)(2,1)}, bf16[128,768]{1,0:T(8,128)(2,1)}, u32[]{:S(2)}, u32[]{:S(2)}) collective-permute-start(bf16[128,768]{1,0:T(8,128)(2,1)} %pad_maximum_fusion.35), channel_id=1, source_target_pairs={{0,4},{1,5},{2,6},{3,7},{4,0},{5,1},{6,2},{7,3},{8,12},{9,13},{10,... | collective-permute-start | bytes 589832 | tf_op jit(solution)/shard_map/ppermute | solution.py:485
  6.6 52.4 %collective-permute-start.4 = (bf16[128,1024]{1,0:T(8,128)(2,1)S(1)}, bf16[128,1024]{1,0:T(8,128)(2,1)S(1)}, u32[]{:S(2)}, u32[]{:S(2)}) collective-permute-start(bf16[128,1024]{1,0:T(8,128)(2,1)S(1)} %constant_dynamic-update-slice_fusion), channel_id=1, source_target_pairs={{2,6},{3,7},{4,0},{5,1},{10,14},{11,15},{12,8},{13,9},{18,22},{19,... | collective-permute-start | bytes 786440 | tf_op jit(solution)/shard_map/ppermute | solution.py:485
  8.6 150.0 %collective-permute-start = (bf16[640,1024]{0,1:T(8,128)(2,1)S(1)}, bf16[640,1024]{0,1:T(8,128)(2,1)}, u32[]{:S(2)}, u32[]{:S(2)}) collective-permute-start(bf16[640,1024]{0,1:T(8,128)(2,1)S(1)} %copy.53), channel_id=1, source_target_pairs={{2,5},{3,4},{4,3},{5,2},{10,13},{11,12},{12,11},{13,10},{18,21},{1... | collective-permute-start | bytes 3932168 | tf_op jit(solution)/shard_map/ppermute | solution.py:485
  59.1 54.3 %collective-permute-start.24 = (bf16[256,768]{1,0:T(8,128)(2,1)S(1)}, bf16[256,768]{1,0:T(8,128)(2,1)S(1)}, u32[]{:S(2)}, u32[]{:S(2)}) collective-permute-start(bf16[256,768]{1,0:T(8,128)(2,1)S(1)} %pad_maximum_fusion.20), channel_id=1, source_target_pairs={{0,1},{1,0},{2,3},{3,2},{4,5},{5,4},{6,7},{7,6},{8,9},{9,8},{10,11... | collective-permute-start | bytes 1179656 | tf_op jit(solution)/shard_map/ppermute | solution.py:485
  70.9 45.2 %collective-permute-start.25 = (bf16[256,768]{1,0:T(8,128)(2,1)S(1)}, bf16[256,768]{1,0:T(8,128)(2,1)S(1)}, u32[]{:S(2)}, u32[]{:S(2)}) collective-permute-start(bf16[256,768]{1,0:T(8,128)(2,1)S(1)} %pad_maximum_fusion.20), channel_id=1, source_target_pairs={{0,2},{1,3},{2,0},{3,1},{4,6},{5,7},{6,4},{7,5},{8,10},{9,11},{10,... | collective-permute-start | bytes 1179656 | tf_op jit(solution)/shard_map/ppermute | solution.py:485
  113.4 57.1 %collective-permute-start.17 = (bf16[256,2560]{1,0:T(8,128)(2,1)S(1)}, bf16[256,2560]{1,0:T(8,128)(2,1)S(1)}, u32[]{:S(2)}, u32[]{:S(2)}) collective-permute-start(bf16[256,2560]{1,0:T(8,128)(2,1)S(1)} %slice_dynamic-update-slice_fusion.6), channel_id=1, source_target_pairs={{0,8},{1,9},{2,10},{3,11},{4,12},{5,13},{6,14},{7,15},{8,0},{9,1},... | collective-permute-start | bytes 3932168 | tf_op jit(solution)/shard_map/ppermute | solution.py:485
  116.1 54.0 %collective-permute-start.18 = (bf16[256,2560]{1,0:T(8,128)(2,1)S(1)}, bf16[256,2560]{1,0:T(8,128)(2,1)S(1)}, u32[]{:S(2)}, u32[]{:S(2)}) collective-permute-start(bf16[256,2560]{1,0:T(8,128)(2,1)S(1)} %slice_dynamic-update-slice_fusion.6), channel_id=1, source_target_pairs={{0,16},{1,17},{2,18},{3,19},{4,20},{5,21},{6,22},{7,23},{8,24},{9,... | collective-permute-start | bytes 3932168 | tf_op jit(solution)/shard_map/ppermute | solution.py:485
  161.2 41.6 %collective-permute-start.27 = (bf16[256,3072]{1,0:T(8,128)(2,1)S(1)}, bf16[256,3072]{1,0:T(8,128)(2,1)S(1)}, u32[]{:S(2)}, u32[]{:S(2)}) collective-permute-start(bf16[256,3072]{1,0:T(8,128)(2,1)S(1)} %slice_dynamic-update-slice_fusion), channel_id=1, source_target_pairs={{0,8},{1,9},{2,10},{3,11},{4,12},{5,13},{6,14},{7,15},{8,0},{9,1},... | collective-permute-start | bytes 4718600 | tf_op jit(solution)/shard_map/ppermute | solution.py:485
  170.1 41.1 %collective-permute-start.19 = (bf16[128,2560]{1,0:T(8,128)(2,1)S(1)}, bf16[128,2560]{1,0:T(8,128)(2,1)S(1)}, u32[]{:S(2)}, u32[]{:S(2)}) collective-permute-start(bf16[128,2560]{1,0:T(8,128)(2,1)S(1)} %slice.432), channel_id=1, source_target_pairs={{0,8},{1,9},{2,10},{3,11},{4,12},{5,13},{6,14},{7,15},{8,0},{9,1},... | collective-permute-start | bytes 1966088 | tf_op jit(solution)/shard_map/ppermute | solution.py:485
  170.5 44.5 %collective-permute-start.20 = (bf16[128,2560]{1,0:T(8,128)(2,1)S(1)}, bf16[128,2560]{1,0:T(8,128)(2,1)S(1)}, u32[]{:S(2)}, u32[]{:S(2)}) collective-permute-start(bf16[128,2560]{1,0:T(8,128)(2,1)S(1)} %slice.433), channel_id=1, source_target_pairs={{0,16},{1,17},{2,18},{3,19},{4,20},{5,21},{6,22},{7,23},{8,24},{9,... | collective-permute-start | bytes 1966088 | tf_op jit(solution)/shard_map/ppermute | solution.py:485
  201.1 121.5 %collective-permute-start.22 = (bf16[640,1024]{0,1:T(8,128)(2,1)}, bf16[640,1024]{0,1:T(8,128)(2,1)}, u32[]{:S(2)}, u32[]{:S(2)}) collective-permute-start(bf16[640,1024]{0,1:T(8,128)(2,1)} %copy.59), channel_id=1, source_target_pairs={{2,5},{3,4},{4,3},{5,2},{10,13},{11,12},{12,11},{13,10},{18,21},{1... | collective-permute-start | bytes 3932168 | tf_op jit(solution)/shard_map/ppermute | solution.py:485
  216.0 137.1 %collective-permute-start.21 = (bf16[1024,2560]{1,0:T(8,128)(2,1)}, bf16[1024,2560]{1,0:T(8,128)(2,1)}, u32[]{:S(2)}, u32[]{:S(2)}) collective-permute-start(bf16[1024,2560]{1,0:T(8,128)(2,1)} %constant_dynamic-update-slice_fusion.11.g_ref), channel_id=1, source_target_pairs={{0,4},{1,5},{2,6},{3,7},{4,0},{5,1},{6,2},{7,3},{8,12},{9,13},{10,... | collective-permute-start | bytes 15728648 | tf_op jit(solution)/shard_map/ppermute | solution.py:485
  228.9 175.1 %collective-permute-start.31 = (bf16[1024,3072]{1,0:T(8,128)(2,1)}, bf16[1024,3072]{1,0:T(8,128)(2,1)}, u32[]{:S(2)}, u32[]{:S(2)}) collective-permute-start(bf16[1024,3072]{1,0:T(8,128)(2,1)} %constant_dynamic-update-slice_fusion.6.u_ref.d_ref), channel_id=1, source_target_pairs={{0,4},{1,5},{2,6},{3,7},{4,0},{5,1},{6,2},{7,3},{8,12},{9,13},{10,... | collective-permute-start | bytes 18874376 | tf_op jit(solution)/shard_map/ppermute | solution.py:485
  468.9 280.6 %collective-permute-start.54 = (bf16[1024,3072]{1,0:T(8,128)(2,1)}, bf16[1024,3072]{1,0:T(8,128)(2,1)}, u32[]{:S(2)}, u32[]{:S(2)}) collective-permute-start(bf16[1024,3072]{1,0:T(8,128)(2,1)} %pad_maximum_fusion), channel_id=1, source_target_pairs={{0,4},{1,5},{2,6},{3,7},{4,0},{5,1},{6,2},{7,3},{8,12},{9,13},{10,... | collective-permute-start | bytes 18874376 | tf_op jit(solution)/shard_map/ppermute | solution.py:485
  472.2 268.0 %collective-permute-start.45 = (bf16[1024,2560]{1,0:T(8,128)(2,1)}, bf16[1024,2560]{1,0:T(8,128)(2,1)}, u32[]{:S(2)}, u32[]{:S(2)}) collective-permute-start(bf16[1024,2560]{1,0:T(8,128)(2,1)} %pad_maximum_fusion.2), channel_id=1, source_target_pairs={{0,4},{1,5},{2,6},{3,7},{4,0},{5,1},{6,2},{7,3},{8,12},{9,13},{10,... | collective-permute-start | bytes 15728648 | tf_op jit(solution)/shard_map/ppermute | solution.py:485
  598.1 49.1 %collective-permute-start.36 = (bf16[1280,1024]{0,1:T(8,128)(2,1)S(1)}, bf16[1280,1024]{0,1:T(8,128)(2,1)}, u32[]{:S(2)}, u32[]{:S(2)}) collective-permute-start(bf16[1280,1024]{0,1:T(8,128)(2,1)S(1)} %concatenate.200), channel_id=1, source_target_pairs={{0,4},{1,5},{2,6},{3,7},{4,0},{5,1},{6,2},{7,3},{8,12},{9,13},{10,... | collective-permute-start | bytes 7864328 | tf_op jit(solution)/shard_map/ppermute | solution.py:485
  642.7 46.2 %collective-permute-start.32 = (bf16[640,1024]{0,1:T(8,128)(2,1)S(1)}, bf16[640,1024]{0,1:T(8,128)(2,1)S(1)}, u32[]{:S(2)}, u32[]{:S(2)}) collective-permute-start(bf16[640,1024]{0,1:T(8,128)(2,1)S(1)} %copy-done.5), channel_id=1, source_target_pairs={{2,5},{3,4},{4,3},{5,2},{10,13},{11,12},{12,11},{13,10},{18,21},{1... | collective-permute-start | bytes 3932168 | tf_op jit(solution)/shard_map/ppermute | solution.py:485
  645.2 42.2 %collective-permute-start.43 = (bf16[256,1024]{1,0:T(8,128)(2,1)S(1)}, bf16[256,1024]{1,0:T(8,128)(2,1)S(1)}, u32[]{:S(2)}, u32[]{:S(2)}) collective-permute-start(bf16[256,1024]{1,0:T(8,128)(2,1)S(1)} %add_convert_fusion.12), channel_id=1, source_target_pairs={{2,0},{3,1},{4,6},{5,7},{10,8},{11,9},{12,14},{13,15},{18,16},{19,... | collective-permute-start | bytes 1572872 | tf_op jit(solution)/shard_map/ppermute | solution.py:485
  650.3 45.9 %collective-permute-start.37 = (bf16[640,1024]{0,1:T(8,128)(2,1)}, bf16[640,1024]{0,1:T(8,128)(2,1)}, u32[]{:S(2)}, u32[]{:S(2)}) collective-permute-start(bf16[640,1024]{0,1:T(8,128)(2,1)} %add_convert_fusion.5), channel_id=1, source_target_pairs={{0,1},{1,0},{2,3},{3,2},{4,5},{5,4},{6,7},{7,6},{8,9},{9,8},{10,11... | collective-permute-start | bytes 3932168 | tf_op jit(solution)/shard_map/ppermute | solution.py:485
  766.5 44.5 %collective-permute-start.47 = (bf16[256,2560]{1,0:T(8,128)(2,1)S(1)}, bf16[256,2560]{1,0:T(8,128)(2,1)S(1)}, u32[]{:S(2)}, u32[]{:S(2)}) collective-permute-start(bf16[256,2560]{1,0:T(8,128)(2,1)S(1)} %pad_maximum_fusion.11), channel_id=1, source_target_pairs={{0,8},{1,9},{2,10},{3,11},{4,12},{5,13},{6,14},{7,15},{8,0},{9,1},... | collective-permute-start | bytes 3932168 | tf_op jit(solution)/shard_map/ppermute | solution.py:485
  767.8 43.2 %collective-permute-start.49 = (bf16[256,2560]{1,0:T(8,128)(2,1)S(1)}, bf16[256,2560]{1,0:T(8,128)(2,1)S(1)}, u32[]{:S(2)}, u32[]{:S(2)}) collective-permute-start(bf16[256,2560]{1,0:T(8,128)(2,1)S(1)} %pad_maximum_fusion.12), channel_id=1, source_target_pairs={{0,16},{1,17},{2,18},{3,19},{4,20},{5,21},{6,22},{7,23},{8,24},{9,... | collective-permute-start | bytes 3932168 | tf_op jit(solution)/shard_map/ppermute | solution.py:485
  783.6 68.0 %collective-permute-start.56 = (bf16[256,3072]{1,0:T(8,128)(2,1)S(1)}, bf16[256,3072]{1,0:T(8,128)(2,1)S(1)}, u32[]{:S(2)}, u32[]{:S(2)}) collective-permute-start(bf16[256,3072]{1,0:T(8,128)(2,1)S(1)} %pad_maximum_fusion.5), channel_id=1, source_target_pairs={{0,8},{1,9},{2,10},{3,11},{4,12},{5,13},{6,14},{7,15},{8,0},{9,1},... | collective-permute-start | bytes 4718600 | tf_op jit(solution)/shard_map/ppermute | solution.py:485
  784.9 66.6 %collective-permute-start.58 = (bf16[256,3072]{1,0:T(8,128)(2,1)S(1)}, bf16[256,3072]{1,0:T(8,128)(2,1)S(1)}, u32[]{:S(2)}, u32[]{:S(2)}) collective-permute-start(bf16[256,3072]{1,0:T(8,128)(2,1)S(1)} %pad_maximum_fusion.6), channel_id=1, source_target_pairs={{0,16},{1,17},{2,18},{3,19},{4,20},{5,21},{6,22},{7,23},{8,24},{9,... | collective-permute-start | bytes 4718600 | tf_op jit(solution)/shard_map/ppermute | solution.py:485
  822.9 41.5 %collective-permute-start.38 = (bf16[640,1024]{0,1:T(8,128)(2,1)S(1)}, bf16[640,1024]{0,1:T(8,128)(2,1)S(1)}, u32[]{:S(2)}, u32[]{:S(2)}) collective-permute-start(bf16[640,1024]{0,1:T(8,128)(2,1)S(1)} %fusion.6), channel_id=1, source_target_pairs={{2,5},{3,4},{4,3},{5,2},{10,13},{11,12},{12,11},{13,10},{18,21},{1... | collective-permute-start | bytes 3932168 | tf_op jit(solution)/shard_map/ppermute | solution.py:485
  (78 other events, 1333.7 us)

commit v2 on v1

v2 whole, which is shorter than its diff:
```python
import functools

import jax
import jax.numpy as jnp
from jax import lax
from jax.experimental.layout import Layout, with_layout_constraint
from jax.experimental import pallas as pl
from jax.experimental.pallas import tpu as pltpu
from jax.sharding import PartitionSpec as P

HEAD_SIZE = 128
EPSILON = 1e-06
THETA = 1000000.0
AXES = ("dp", "tensor")
BLOCK = 256
SCALE = HEAD_SIZE ** (-0.5)
LOG2E = 1.4426950408889634
VMEM_LIMIT = 56 * 1024 * 1024
F32 = jnp.float32
BF16 = jnp.bfloat16


def dot_nn(left, right):
    return lax.dot_general(left, right, (((1,), (0,)), ((), ())), preferred_element_type=F32)


def dot_nt(left, right):
    return lax.dot_general(left, right, (((1,), (1,)), ((), ())), preferred_element_type=F32)


def dot_tn(left, right):
    return lax.dot_general(left, right, (((0,), (0,)), ((), ())), preferred_element_type=F32)


def by_rows(x):
    return with_layout_constraint(x, Layout(major_to_minor=tuple(range(x.ndim))))


def row_scale(rows):
    return lax.rsqrt(jnp.mean(rows * rows, axis=-1, keepdims=True) + EPSILON)


def rotate(rows, cosine, sine):
    return rows * cosine + pltpu.roll(rows, HEAD_SIZE // 2, 1) * sine


def unrotate(rows, cosine, sine):
    return rows * cosine - pltpu.roll(rows, HEAD_SIZE // 2, 1) * sine


CHUNKS = 4


def first_kernel(
    pairs,
    span,
    tokens_ref,
    heads_ref,
    output_ref,
    gains_ref,
    facts_ref,
    tokens_out,
    heads_out,
    output_out,
    gains_out,
    facts_out,
    send_sems,
    recv_sems,
    local_sems,
):
    half = span // 2
    dp, t = lax.axis_index("dp"), lax.axis_index("tensor")
    p, c = dp // 2, lax.rem(dp, 2)
    q = t // half
    settled = c == q
    rows = tokens_ref.shape[0]
    piece = rows // CHUNKS
    shard = heads_ref.shape[0]
    small = gains_ref.shape[0]
    place = lambda pp, cc, tt: (pp * 2 + cc, tt)

    barrier = pltpu.get_barrier_semaphore()
    greeted = 0
    for k in range(1, 2 * span):
        pl.semaphore_signal(
            barrier,
            device_id=place(p, c ^ (k // span), t ^ (k % span)),
            device_id_type=pl.DeviceIdType.MESH,
        )
        greeted += 1
    for k in range(1, pairs):
        for cc in range(2):
            pl.semaphore_signal(
                barrier, device_id=place(p ^ k, c ^ cc, t), device_id_type=pl.DeviceIdType.MESH
            )
            greeted += 1
    pl.semaphore_wait(barrier, greeted)

    used = [0]

    def number(count=1):
        used[0] += count
        return used[0] - count

    def remote(src, dst, sem, to, arrival=None):
        return pltpu.make_async_remote_copy(
            src_ref=src,
            dst_ref=dst,
            send_sem=send_sems.at[sem],
            recv_sem=recv_sems.at[sem if arrival is None else arrival],
            device_id=to,
            device_id_type=pl.DeviceIdType.MESH,
        )

    def rows_of(i):
        return pl.ds(i * piece, piece)

    swap_sem = number(CHUNKS)
    line_sems = [[number() for _ in range(CHUNKS)] for _ in range(half)]
    side_sems = [[number() for _ in range(CHUNKS)] for _ in range(half)]
    near_sem, far_sem = number(), number(2)
    pair_sems = [number() for _ in range(pairs)]
    output_sems = [number() for _ in range(span)]
    gain_sems = [number() for _ in range(2 * pairs)]
    fact_sem = number()

    sibling = place(p, 1 - c, t)
    partner = place(p, 1 - c, span - 1 - t)
    swaps = [
        remote(tokens_ref.at[rows_of(i)], tokens_out.at[0, rows_of(i)], swap_sem + i, partner) for i in range(CHUNKS)
    ]
    own_rows = pl.ds(dp * shard, shard)
    far = lax.rem(t + half, span)
    near_copy = remote(heads_ref, heads_out.at[own_rows], near_sem, sibling)
    far_copy = remote(heads_ref, heads_out.at[own_rows], far_sem + c, place(p, q, far))
    local_tokens = pltpu.make_async_copy(tokens_ref, tokens_out.at[0], local_sems.at[0])
    local_heads = pltpu.make_async_copy(heads_ref, heads_out.at[own_rows], local_sems.at[1])
    local_output = pltpu.make_async_copy(output_ref, output_out.at[0], local_sems.at[2])
    local_gains = pltpu.make_async_copy(gains_ref, gains_out.at[pl.ds(dp * small, small)], local_sems.at[3])

    fact_copy = remote(facts_ref, facts_out, fact_sem, sibling)
    fact_copy.start()
    far_copy.start()

    @pl.when(settled)
    def _():
        local_heads.start()
        local_tokens.start()

    @pl.when(jnp.logical_not(settled))
    def _():
        near_copy.start()
        for copy in swaps:
            copy.start()

    gain_copies = []
    for k in range(1, 2 * pairs):
        to = (p ^ (k // 2), c ^ (k % 2))
        gain_copies.append(
            remote(gains_ref, gains_out.at[pl.ds(dp * small, small)], gain_sems[k], place(to[0], to[1], t))
        )
    local_gains.start()
    local_output.start()
    for copy in gain_copies:
        copy.start()

    def spread(i, source):
        copies = [remote(source, tokens_out.at[half, rows_of(i)], side_sems[0][i], sibling)]
        for k in range(1, half):
            copies.append(remote(source, tokens_out.at[k, rows_of(i)], line_sems[k][i], place(p, c, t ^ k)))
        return copies

    @pl.when(settled)
    def _():
        for i in range(CHUNKS):
            for copy in spread(i, tokens_ref.at[rows_of(i)]):
                copy.start()

    output_copies = [
        remote(output_ref, output_out.at[r], output_sems[r], place(p, c, t ^ r)) for r in range(1, span)
    ]

    @pl.when(settled)
    def _():
        local_heads.wait()
        near_copy.wait_recv()

    @pl.when(jnp.logical_not(settled))
    def _():
        near_copy.wait_send()
        for cc in range(2):
            remote(heads_ref, heads_out.at[own_rows], far_sem, sibling, far_sem + cc).wait_recv()

    both = heads_out.at[pl.ds(p * 2 * shard, 2 * shard)]
    pair_copies = [remote(both, both, pair_sems[k], place(p ^ k, c, t)) for k in range(1, pairs)]
    for copy in pair_copies:
        copy.start()

    @pl.when(jnp.logical_not(settled))
    def _():
        for i in range(CHUNKS):
            swaps[i].wait_recv()
            for copy in spread(i, tokens_out.at[0, rows_of(i)]):
                copy.start()

    for copy in output_copies:
        copy.start()

    forwards = []
    for i in range(CHUNKS):
        for k in range(1, half):
            block = tokens_out.at[k, rows_of(i)]
            remote(block, block, line_sems[k][i], sibling).wait_recv()
            copy = remote(block, tokens_out.at[half + k, rows_of(i)], side_sems[k][i], sibling)
            copy.start()
            forwards.append(copy)

    far_copy.wait_send()
    fact_copy.wait()
    local_output.wait()
    local_gains.wait()

    @pl.when(settled)
    def _():
        local_tokens.wait()

    @pl.when(jnp.logical_not(settled))
    def _():
        for copy in swaps:
            copy.wait_send()

    for i in range(CHUNKS):
        for index, copy in enumerate(spread(i, tokens_out.at[0, rows_of(i)])):
            copy.wait_send()
            if index == 0:
                copy.wait_recv()
    for copy in forwards + pair_copies + output_copies + gain_copies:
        copy.wait()


def first_transfers(pairs, span, tokens, heads, output, gains, facts):
    rows, width = tokens.shape
    shard = heads.shape[0]
    half = span // 2
    copies = CHUNKS * (1 + 2 * half) + 3 + pairs + span + 2 * pairs + 1
    any_ref = pl.BlockSpec(memory_space=pl.ANY)
    return pl.pallas_call(
        functools.partial(first_kernel, pairs, span),
        in_specs=[any_ref] * 5,
        out_specs=[any_ref] * 5,
        out_shape=[
            jax.ShapeDtypeStruct((span, rows, width), tokens.dtype),
            jax.ShapeDtypeStruct((2 * pairs * shard, heads.shape[1]), heads.dtype),
            jax.ShapeDtypeStruct((span, *output.shape), output.dtype),
            jax.ShapeDtypeStruct((2 * pairs * gains.shape[0], gains.shape[1]), gains.dtype),
            jax.ShapeDtypeStruct(facts.shape, facts.dtype),
        ],
        scratch_shapes=[
            pltpu.SemaphoreType.DMA((copies,)),
            pltpu.SemaphoreType.DMA((copies,)),
            pltpu.SemaphoreType.DMA((4,)),
        ],
        compiler_params=pltpu.CompilerParams(collective_id=0, has_side_effects=True),
        name="first_transfers",
    )(tokens, heads, output, gains, facts)


def project_kernel(
    query_heads, key_heads, x_ref, gain_ref, w_ref, gq_ref, gk_ref, cos_ref, sin_ref, normed_ref, qkv_ref, scale_ref
):
    x = x_ref[...].astype(F32)
    normed = (x * row_scale(x) * gain_ref[...]).astype(BF16)
    normed_ref[...] = normed
    raw = dot_nn(normed, w_ref[...])
    cosine, sine = cos_ref[...], sin_ref[...]
    lane = lax.broadcasted_iota(jnp.int32, (x.shape[0], HEAD_SIZE), 1)
    scales = jnp.zeros((x.shape[0], HEAD_SIZE), F32)
    for head in range(query_heads + key_heads):
        span = slice(head * HEAD_SIZE, (head + 1) * HEAD_SIZE)
        u = raw[:, span]
        r = row_scale(u)
        gain = gq_ref[...] if head < query_heads else gk_ref[...]
        qkv_ref[:, span] = rotate(u * r * gain, cosine, sine).astype(BF16)
        scales = jnp.where(lane == head, r, scales)
    span = slice((query_heads + key_heads) * HEAD_SIZE, None)
    qkv_ref[:, span] = raw[:, span].astype(BF16)
    scale_ref[...] = scales


def project(x, gain, weights, gain_query, gain_key, cosine, sine, query_heads, key_heads):
    rows, width = x.shape
    wide = weights.shape[1]
    whole = lambda shape: pl.BlockSpec(shape, lambda i: (0, 0))
    block = lambda cols: pl.BlockSpec((BLOCK, cols), lambda i: (i, 0))
    return pl.pallas_call(
        functools.partial(project_kernel, query_heads, key_heads),
        grid=(rows // BLOCK,),
        in_specs=[
            block(width),
            whole((1, width)),
            whole((width, wide)),
            whole((1, HEAD_SIZE)),
            whole((1, HEAD_SIZE)),
            block(HEAD_SIZE),
            block(HEAD_SIZE),
        ],
        out_specs=[block(width), block(wide), block(HEAD_SIZE)],
        out_shape=[
            jax.ShapeDtypeStruct((rows, width), BF16),
            jax.ShapeDtypeStruct((rows, wide), BF16),
            jax.ShapeDtypeStruct((rows, HEAD_SIZE), F32),
        ],
        compiler_params=pltpu.CompilerParams(vmem_limit_bytes=VMEM_LIMIT),
        name="project",
    )(x, gain, weights, gain_query, gain_key, cosine, sine)


def first_place(info_ref, blocks, docs, places):
    start = jnp.zeros_like(places)
    for doc in range(docs):
        begin = info_ref[2 * blocks + doc]
        start = jnp.maximum(start, jnp.where(places >= begin, begin, 0))
    return start


def forward_kernel(group, blocks, docs, info_ref, q_ref, k_ref, v_ref, o_ref, lse_ref, wide_ref, acc_ref):
    i = pl.program_id(0)

    @pl.when(i == 0)
    def _():
        wide_ref[:, :HEAD_SIZE] = v_ref[...]
        wide_ref[:, HEAD_SIZE:] = jnp.ones_like(v_ref)

    queries = jnp.concatenate([q_ref[:, h * HEAD_SIZE : (h + 1) * HEAD_SIZE] for h in range(group)], axis=0)
    acc_ref[...] = jnp.zeros_like(acc_ref)
    shape = (group * BLOCK, BLOCK)

    def step(j, masked):
        rows = pl.ds(pl.multiple_of(j * BLOCK, BLOCK), BLOCK)
        weights = jnp.exp2(dot_nt(queries, k_ref[rows, :]) * (SCALE * LOG2E))
        if masked:
            places = i * BLOCK + lax.rem(lax.broadcasted_iota(jnp.int32, (group * BLOCK, 1), 0), BLOCK)
            start = first_place(info_ref, blocks, docs, places)
            other = j * BLOCK + lax.broadcasted_iota(jnp.int32, shape, 1)
            weights = jnp.where((other <= places) & (other >= start), weights, 0.0)
        acc_ref[...] += dot_nn(weights.astype(BF16), wide_ref[rows, :])

    low, clear = info_ref[i], info_ref[blocks + i]

    def masked_step(j, carry):
        step(j, True)
        return carry

    def clear_step(j, carry):
        step(j, False)
        return carry

    lax.fori_loop(low, jnp.minimum(clear, i), masked_step, 0)
    lax.fori_loop(jnp.minimum(clear, i), i, clear_step, 0)
    step(i, True)
    total = acc_ref[:, HEAD_SIZE:]
    out = (acc_ref[:, :HEAD_SIZE] / total).astype(BF16)
    for h in range(group):
        o_ref[:, h * HEAD_SIZE : (h + 1) * HEAD_SIZE] = out[h * BLOCK : (h + 1) * BLOCK]
    lse_ref[0] = lax.dot_general(
        jnp.full((8, HEAD_SIZE), 1.0 / HEAD_SIZE, F32),
        jnp.log2(total),
        (((1,), (1,)), ((), ())),
        precision=lax.Precision.HIGHEST,
        preferred_element_type=F32,
    )


def attention_forward(info, qkv, query_heads, key_heads, docs, kv):
    rows = qkv.shape[0]
    blocks = rows // BLOCK
    group = query_heads // key_heads
    wide = group * HEAD_SIZE
    return pl.pallas_call(
        functools.partial(forward_kernel, group, blocks, docs),
        grid_spec=pltpu.PrefetchScalarGridSpec(
            num_scalar_prefetch=1,
            grid=(blocks,),
            in_specs=[
                pl.BlockSpec((BLOCK, wide), lambda i, s: (i, kv)),
                pl.BlockSpec((rows, HEAD_SIZE), lambda i, s: (0, query_heads + kv)),
                pl.BlockSpec((rows, HEAD_SIZE), lambda i, s: (0, query_heads + key_heads + kv)),
            ],
            out_specs=[
                pl.BlockSpec((BLOCK, wide), lambda i, s: (i, 0)),
                pl.BlockSpec((1, 8, group * BLOCK), lambda i, s: (i, 0, 0)),
            ],
            scratch_shapes=[
                pltpu.VMEM((rows, 2 * HEAD_SIZE), BF16),
                pltpu.VMEM((group * BLOCK, 2 * HEAD_SIZE), F32),
            ],
        ),
        out_shape=[
            jax.ShapeDtypeStruct((rows, wide), BF16),
            jax.ShapeDtypeStruct((blocks, 8, group * BLOCK), F32),
        ],
        compiler_params=pltpu.CompilerParams(vmem_limit_bytes=VMEM_LIMIT),
        name="attention_forward",
    )(info, qkv, qkv, qkv)


def backward_kernel(
    group,
    query_heads,
    kv,
    blocks,
    docs,
    info_ref,
    q_ref,
    k_ref,
    v_ref,
    o_ref,
    do_ref,
    lse_ref,
    cos_ref,
    sin_ref,
    scale_ref,
    gq_ref,
    gk_ref,
    grad_ref,
    dgain_ref,
    dk_acc,
    dv_acc,
    dq_acc,
):
    i = pl.program_id(0)

    @pl.when(i == 0)
    def _():
        dk_acc[...] = jnp.zeros_like(dk_acc)
        dv_acc[...] = jnp.zeros_like(dv_acc)
        dgain_ref[...] = jnp.zeros_like(dgain_ref)

    def stacked(ref):
        return jnp.concatenate([ref[:, h * HEAD_SIZE : (h + 1) * HEAD_SIZE] for h in range(group)], axis=0)

    queries, grads = stacked(q_ref), stacked(do_ref)
    product = stacked(o_ref).astype(F32) * grads.astype(F32)
    delta = lax.dot_general(
        jnp.ones((8, HEAD_SIZE), F32),
        product,
        (((1,), (1,)), ((), ())),
        precision=lax.Precision.HIGHEST,
        preferred_element_type=F32,
    )[:1]
    lse = lse_ref[0, :1]
    dq_acc[...] = jnp.zeros_like(dq_acc)
    shape = (BLOCK, group * BLOCK)

    def step(j, masked):
        rows = pl.ds(pl.multiple_of(j * BLOCK, BLOCK), BLOCK)
        keys, values = k_ref[rows, :], v_ref[rows, :]
        probs = jnp.exp2(dot_nt(keys, queries) * (SCALE * LOG2E) - lse)
        if masked:
            places = i * BLOCK + lax.rem(lax.broadcasted_iota(jnp.int32, (1, group * BLOCK), 1), BLOCK)
            start = first_place(info_ref, blocks, docs, places)
            other = j * BLOCK + lax.broadcasted_iota(jnp.int32, shape, 0)
            probs = jnp.where((other <= places) & (other >= start), probs, 0.0)
        score_grad = (probs * (dot_nt(values, grads) - delta)).astype(BF16)
        dv_acc[rows, :] += dot_nn(probs.astype(BF16), grads)
        dk_acc[rows, :] += dot_nn(score_grad, queries)
        dq_acc[...] += dot_tn(score_grad, keys)

    low, clear = info_ref[i], info_ref[blocks + i]

    def masked_step(j, carry):
        step(j, True)
        return carry

    def clear_step(j, carry):
        step(j, False)
        return carry

    lax.fori_loop(low, jnp.minimum(clear, i), masked_step, 0)
    lax.fori_loop(jnp.minimum(clear, i), i, clear_step, 0)
    step(i, True)

    lane = lax.broadcasted_iota(jnp.int32, (BLOCK, HEAD_SIZE), 1)

    def raw_grad(grad, rotated, rows, head, gain):
        cosine, sine = cos_ref[rows, :], sin_ref[rows, :]
        r = jnp.sum(jnp.where(lane == head, scale_ref[rows, :], 0.0), axis=1, keepdims=True)
        unit = unrotate(rotated.astype(F32), cosine, sine) / gain
        back = unrotate(grad * SCALE, cosine, sine)
        scaled = back * gain
        raw = r * (scaled - unit * jnp.mean(scaled * unit, axis=1, keepdims=True))
        return raw.astype(BF16), jnp.sum(back * unit, axis=0, keepdims=True)

    here = pl.ds(pl.multiple_of(i * BLOCK, BLOCK), BLOCK)
    for h in range(group):
        span = slice(h * HEAD_SIZE, (h + 1) * HEAD_SIZE)
        raw, gain_grad = raw_grad(
            dq_acc[h * BLOCK : (h + 1) * BLOCK, :], q_ref[:, span], here, kv * group + h, gq_ref[...]
        )
        grad_ref[here, span] = raw
        dgain_ref[0:1, :] += gain_grad

    @pl.when(i == blocks - 1)
    def _():
        grad_ref[:, (group + 1) * HEAD_SIZE :] = dv_acc[...].astype(BF16)

        def finish(b, carry):
            rows = pl.ds(pl.multiple_of(b * BLOCK, BLOCK), BLOCK)
            raw, gain_grad = raw_grad(dk_acc[rows, :], k_ref[rows, :], rows, query_heads + kv, gk_ref[...])
            grad_ref[rows, group * HEAD_SIZE : (group + 1) * HEAD_SIZE] = raw
            dgain_ref[1:2, :] += gain_grad
            return carry

        lax.fori_loop(0, blocks, finish, 0)


def attention_backward(
    info, qkv, attended, grads, lse, cosine, sine, scales, gain_query, gain_key, query_heads, key_heads, docs, kv
):
    rows = qkv.shape[0]
    blocks = rows // BLOCK
    group = query_heads // key_heads
    wide = group * HEAD_SIZE
    own = pl.BlockSpec((BLOCK, wide), lambda i, s: (i, 0))
    whole = lambda shape: pl.BlockSpec(shape, lambda i, s: (0, 0))
    return pl.pallas_call(
        functools.partial(backward_kernel, group, query_heads, kv, blocks, docs),
        grid_spec=pltpu.PrefetchScalarGridSpec(
            num_scalar_prefetch=1,
            grid=(blocks,),
            in_specs=[
                pl.BlockSpec((BLOCK, wide), lambda i, s: (i, kv)),
                pl.BlockSpec((rows, HEAD_SIZE), lambda i, s: (0, query_heads + kv)),
                pl.BlockSpec((rows, HEAD_SIZE), lambda i, s: (0, query_heads + key_heads + kv)),
                own,
                own,
                pl.BlockSpec((1, 8, group * BLOCK), lambda i, s: (i, 0, 0)),
                whole((rows, HEAD_SIZE)),
                whole((rows, HEAD_SIZE)),
                whole((rows, HEAD_SIZE)),
                whole((1, HEAD_SIZE)),
                whole((1, HEAD_SIZE)),
            ],
            out_specs=[whole((rows, wide + 2 * HEAD_SIZE)), whole((8, HEAD_SIZE))],
            scratch_shapes=[
                pltpu.VMEM((rows, HEAD_SIZE), F32),
                pltpu.VMEM((rows, HEAD_SIZE), F32),
                pltpu.VMEM((group * BLOCK, HEAD_SIZE), F32),
            ],
        ),
        out_shape=[
            jax.ShapeDtypeStruct((rows, wide + 2 * HEAD_SIZE), BF16),
            jax.ShapeDtypeStruct((8, HEAD_SIZE), F32),
        ],
        compiler_params=pltpu.CompilerParams(vmem_limit_bytes=VMEM_LIMIT),
        name="attention_backward",
    )(info, qkv, qkv, qkv, attended, grads, lse, cosine, sine, scales, gain_query, gain_key)


def wide_block(ref):
    value = ref[...]
    return value.reshape(value.shape[0] * value.shape[2], value.shape[3])


def output_kernel(a_ref, w_ref, tokens_ref, gain_ref, middle_ref, normed_ref):
    r = pl.program_id(0)

    @pl.when(r == 0)
    def _():
        middle_ref[...] = tokens_ref[...].astype(F32)

    middle_ref[...] += dot_nt(a_ref[0], wide_block(w_ref))

    @pl.when(r == pl.num_programs(0) - 1)
    def _():
        middle = middle_ref[...]
        normed_ref[...] = (middle * row_scale(middle) * gain_ref[...]).astype(BF16)


def output_project(mixed, weights, tokens, gain):
    span, rows, cols = mixed.shape
    devices, _, shard, _ = weights.shape
    width = devices * shard
    whole = lambda shape: pl.BlockSpec(shape, lambda r: (0, 0), pipeline_mode=pl.Buffered(1))
    return pl.pallas_call(
        output_kernel,
        grid=(span,),
        in_specs=[
            pl.BlockSpec((1, rows, cols), lambda r: (r, 0, 0)),
            pl.BlockSpec((devices, 1, shard, cols), lambda r: (0, r, 0, 0)),
            whole((rows, width)),
            whole((1, width)),
        ],
        out_specs=[whole((rows, width)), whole((rows, width))],
        out_shape=[jax.ShapeDtypeStruct((rows, width), F32), jax.ShapeDtypeStruct((rows, width), BF16)],
        compiler_params=pltpu.CompilerParams(vmem_limit_bytes=VMEM_LIMIT),
        name="output_project",
    )(mixed, weights, tokens, gain)


def output_back_kernel(b_ref, a_ref, w_ref, da_ref, dw_ref, bt_ref):
    @pl.when(pl.program_id(0) == 0)
    def _():
        bt_ref[...] = b_ref[...].T

    da_ref[0] = dot_nn(b_ref[...], wide_block(w_ref)).astype(BF16)
    dw_ref[...] = dot_nn(bt_ref[...], a_ref[0]).astype(BF16).reshape(dw_ref.shape)


def output_back(branch, mixed, weights):
    span, rows, cols = mixed.shape
    devices, _, shard, _ = weights.shape
    width = devices * shard
    chunk = pl.BlockSpec((1, rows, cols), lambda r: (r, 0, 0))
    wide = pl.BlockSpec((devices, 1, shard, cols), lambda r: (0, r, 0, 0))
    return pl.pallas_call(
        output_back_kernel,
        grid=(span,),
        in_specs=[
            pl.BlockSpec((rows, width), lambda r: (0, 0), pipeline_mode=pl.Buffered(1)),
            chunk,
            wide,
        ],
        out_specs=[chunk, wide],
        scratch_shapes=[pltpu.VMEM((width, rows), BF16)],
        out_shape=[
            jax.ShapeDtypeStruct((span, rows, cols), BF16),
            jax.ShapeDtypeStruct((devices, span, shard, cols), BF16),
        ],
        compiler_params=pltpu.CompilerParams(vmem_limit_bytes=VMEM_LIMIT),
        name="output_back",
    )(branch, mixed, weights)


def feed_kernel(last, x_ref, c_ref, w_ref, *refs):
    if last:
        (out_in, ng_in, middle_ref, gain_ref, result_ref, grad_ref, branch_ref, dgain_ref, dw_ref, out_s, ng_s) = refs[:11]
        act_s, gg_s, ug_s, xt_s, ct_s = refs[11:]
    else:
        out_s, ng_s, dw_ref, act_s, gg_s, ug_s, xt_s, ct_s = refs
    j = pl.program_id(0)
    rows_all, width = x_ref.shape
    hidden = act_s.shape[1]
    devices, _, shard, _ = w_ref.shape
    chunk = rows_all // 2

    @pl.when(j == 0)
    def _():
        xt_s[...] = x_ref[...].T
        ct_s[...] = c_ref[...].T
        out_s[...] = out_in[...] if last else jnp.zeros_like(out_s)
        ng_s[...] = ng_in[...] if last else jnp.zeros_like(ng_s)

    def part(k):
        return w_ref[:, 0, :, k * hidden : (k + 1) * hidden].reshape(width, hidden)

    def rows_step(m, carry):
        rows = pl.ds(pl.multiple_of(m * chunk, chunk), chunk)
        gate = dot_nn(x_ref[rows, :], part(0))
        upward = dot_nn(x_ref[rows, :], part(1))
        act_grad = dot_nn(c_ref[rows, :], part(2))
        sig = 1.0 / (1.0 + jnp.exp(-gate))
        silu = gate * sig
        act = (silu * upward).astype(BF16)
        up_grad = (act_grad * silu).astype(BF16)
        gate_grad = (act_grad * upward * sig * (1.0 + gate * (1.0 - sig))).astype(BF16)
        act_s[rows, :] = act
        ug_s[rows, :] = up_grad
        gg_s[rows, :] = gate_grad
        out_s[rows, :] += dot_nt(act, part(2))
        ng_s[rows, :] += dot_nt(gate_grad, part(0)) + dot_nt(up_grad, part(1))
        return carry

    lax.fori_loop(0, rows_all // chunk, rows_step, 0)

    group = BLOCK // shard

    def grad_step(m, carry):
        rows = pl.ds(pl.multiple_of(m * BLOCK, BLOCK), BLOCK)
        to = pl.ds(m * group, group)
        for k, left, right in ((0, xt_s, gg_s), (1, xt_s, ug_s), (2, ct_s, act_s)):
            value = dot_nn(left[rows, :], right[...]).astype(BF16)
            dw_ref[to, 0, :, k * hidden : (k + 1) * hidden] = value.reshape(group, shard, hidden)
        return carry

    lax.fori_loop(0, width // BLOCK, grad_step, 0)

    if not last:
        return

    @pl.when(j == pl.num_programs(0) - 1)
    def _():
        middle = middle_ref[...]
        result_ref[...] = (middle + out_s[...]).astype(BF16)
        r = row_scale(middle)
        unit = middle * r
        dgain_ref[...] = jnp.broadcast_to(jnp.sum(ng_s[...] * unit, axis=0, keepdims=True), dgain_ref.shape)
        scaled = ng_s[...] * gain_ref[...]
        grad = c_ref[...].astype(F32) + r * (scaled - unit * jnp.mean(scaled * unit, axis=-1, keepdims=True))
        grad_ref[...] = grad
        branch_ref[...] = grad.astype(BF16)


def feed(x, cot, weights, *rest):
    rows, width = x.shape
    devices, span, shard, cols = weights.shape
    hidden = cols // 3
    last = len(rest) > 0
    whole = lambda shape: pl.BlockSpec(shape, lambda j: (0, 0), pipeline_mode=pl.Buffered(1))
    chunk = pl.BlockSpec((devices, 1, shard, cols), lambda j: (0, j, 0, 0))
    full = whole((rows, width))
    grads = jax.ShapeDtypeStruct((devices, span, shard, cols), BF16)
    shape = lambda kind: jax.ShapeDtypeStruct((rows, width), kind)
    sums = [pltpu.VMEM((rows, width), F32)] * 2 if last else []
    return pl.pallas_call(
        functools.partial(feed_kernel, last),
        grid=(span,),
        in_specs=[full, full, chunk] + ([full, full, full, whole((1, width))] if last else []),
        out_specs=[full, full, full, whole((8, width)), chunk] if last else [full, full, chunk],
        out_shape=[shape(BF16), shape(F32), shape(BF16), jax.ShapeDtypeStruct((8, width), F32), grads]
        if last
        else [shape(F32), shape(F32), grads],
        scratch_shapes=sums + [pltpu.VMEM((rows, hidden), BF16)] * 3 + [pltpu.VMEM((width, rows), BF16)] * 2,
        compiler_params=pltpu.CompilerParams(vmem_limit_bytes=VMEM_LIMIT),
        name="feed_forward",
    )(x, cot, weights, *rest)


def local(
    tokens,
    lengths,
    row_order,
    attention_gain,
    query_gain,
    key_gain,
    query_weight,
    key_matrix,
    value_matrix,
    output_weight,
    feedforward_gain,
    gate_weight,
    up_weight,
    down_weight,
    cotangent,
):
    span = lax.axis_size("tensor")
    pairs = lax.axis_size("dp") // 2
    half = span // 2
    rows, width = tokens.shape
    group_rows = rows * span
    blocks = group_rows // BLOCK
    docs = lengths.shape[1]
    query_heads = query_weight.shape[1] // HEAD_SIZE
    key_heads = key_matrix.shape[1] // HEAD_SIZE
    head_columns = query_weight.shape[1]
    hidden_columns = gate_weight.shape[1]
    shard = query_weight.shape[0]

    dp, t = lax.axis_index("dp"), lax.axis_index("tensor")
    p, c = dp // 2, lax.rem(dp, 2)
    q = t // half
    settled = c == q

    def send(x, route):
        moves = []
        for pp in range(pairs):
            for cc in range(2):
                for tt in range(span):
                    to = route(pp, cc, tt)
                    if to is not None:
                        moves.append(((pp * 2 + cc) * span + tt, (to[0] * 2 + to[1]) * span + to[2]))
        return lax.ppermute(x, AXES, moves)

    def sibling(x):
        return send(x, lambda pp, cc, tt: (pp, 1 - cc, tt))

    def swap(x):
        moved = send(x, lambda pp, cc, tt: (pp, 1 - cc, span - 1 - tt) if cc != tt // half else None)
        return jnp.where(settled, x, moved)

    def ordered(mine, other, first):
        return jnp.where(first, mine, other), jnp.where(first, other, mine)

    def add(*terms):
        total = terms[0].astype(F32)
        for term in terms[1:]:
            total = total + term.astype(F32)
        return total.astype(BF16)

    one_off = lambda pp, cc, tt: (pp ^ 1, cc, tt)
    two_off = lambda pp, cc, tt: (pp ^ 2, cc, tt)

    def scatter_start(take):
        if pairs != 4:
            return ()
        cut = shard
        return send(take(p ^ 3, 0, cut), one_off), send(take(p ^ 3, cut, cut), two_off)

    def scatter_next(take, arrived):
        if pairs != 4:
            return ()
        cut = shard
        one = jnp.concatenate([take(p ^ 1, 0, cut), add(take(p ^ 1, cut, cut), arrived[1])], axis=0)
        two = jnp.concatenate([add(take(p ^ 2, 0, cut), arrived[0]), take(p ^ 2, cut, cut)], axis=0)
        return send(one, one_off), send(two, two_off)

    def scatter_end(take, later):
        size = 2 * shard
        if pairs == 4:
            return add(take(p, 0, size), *later)
        pieces = [take(p ^ k, 0, size) for k in range(pairs)]
        while len(pieces) > 1:
            keep = len(pieces) // 2
            moved = send(jnp.concatenate(pieces[keep:], axis=0), lambda pp, cc, tt: (pp ^ keep, cc, tt))
            pieces = [add(pieces[k], moved[k * size : (k + 1) * size]) for k in range(keep)]
        return pieces[0]

    def taker(parts):
        def take(at, shift, count):
            rows_of = lambda x: lax.dynamic_slice(x, (at * 2 * shard + shift, 0), (count, x.shape[1]))
            cols = [add(*[rows_of(x) for x in terms]) if len(terms) > 1 else rows_of(terms[0]) for terms in parts]
            return jnp.concatenate(cols, axis=1) if len(cols) > 1 else cols[0]

        return take

    never = row_order[0, 0] < 0

    def behind(x, other):
        return jnp.where(never, other[0, 0].astype(x.dtype), x)

    def line(x, steps):
        return [send(x, lambda pp, cc, tt: (pp, cc, tt ^ r)) for r in steps]

    def gather_wide(pieces):
        cols = pieces[0].shape[1]
        out = by_rows(lax.all_gather(by_rows(jnp.concatenate(pieces, axis=0)), "dp", axis=0, tiled=True))
        return out.reshape(2 * pairs, len(pieces), shard, cols)

    def scatter_wide(grads):
        devices, count, _, cols = grads.shape
        out = by_rows(grads.reshape(devices * count * shard, cols))
        out = by_rows(lax.psum_scatter(out, "dp", scatter_dimension=0, tiled=True))
        return [out[r * shard : (r + 1) * shard] for r in range(count)]

    def line_back(pieces, first):
        return [
            piece if r == 0 else send(piece, lambda pp, cc, tt: (pp, cc, tt ^ r))
            for r, piece in enumerate(pieces, start=first)
        ]

    heads_local = by_rows(jnp.concatenate([query_weight, key_matrix, value_matrix], axis=1))
    feed_local = by_rows(jnp.concatenate([gate_weight, up_weight, down_weight.T], axis=1))
    gains = jnp.concatenate([attention_gain, query_gain, key_gain, feedforward_gain])
    small, tiny = attention_gain.shape[0], query_gain.shape[0]
    few, lanes = gains.shape[0], -(-gains.shape[0] // 128) * 128
    gains = jnp.broadcast_to(jnp.pad(gains, (0, lanes - few))[None], (16, lanes))
    facts = jnp.concatenate([row_order[0], lengths[0]])
    fact_rows = -(-facts.shape[0] // 1024) * 8
    facts = jnp.pad(facts, (0, fact_rows * 128 - facts.shape[0])).reshape(fact_rows, 128)
    tokens_all, heads_weights, output_line, gains, facts_moved = first_transfers(
        pairs, span, tokens, heads_local, by_rows(output_weight.T), gains, facts
    )
    swapped = tokens_all[0]
    tokens_all = tokens_all.reshape(group_rows, width)
    feed_weights = [gather_wide([feed_local])]
    output_weights = gather_wide([output_line[r] for r in range(span)])
    feed_weights.append(gather_wide(line(behind(feed_local, swapped), range(1, span))))

    gains = gains.reshape(2 * pairs, 16, lanes)[:, 0, :few].astype(F32)
    gain_one = gains[:, :small].reshape(1, width)
    gain_query = gains[:, small : small + tiny].reshape(1, HEAD_SIZE)
    gain_key = gains[:, small + tiny : small + 2 * tiny].reshape(1, HEAD_SIZE)
    gain_two = gains[:, small + 2 * tiny : small + 2 * tiny + small].reshape(1, width)
    facts = jnp.where(settled, facts, facts_moved).reshape(-1)[: group_rows + docs]
    order, length = facts[:group_rows].reshape(span, rows), facts[group_rows:]
    places = []
    for k in range(span):
        tt, cc = t ^ (k % half), c ^ (k // half)
        places.append(lax.dynamic_index_in_dim(order, jnp.where(cc == tt // half, tt, span - 1 - tt), 0, False))
    places = jnp.concatenate(places)
    inverse = jnp.argsort(places)
    before = jnp.arange(docs)[None, :] < jnp.arange(docs)[:, None]
    starts = jnp.sum(jnp.where(before, length[None, :], 0), axis=1).astype(jnp.int32)

    def start_of(place):
        return jnp.max(jnp.where(place[:, None] >= starts[None, :], starts[None, :], 0), axis=1)

    index = jnp.arange(blocks, dtype=jnp.int32) * BLOCK
    low = start_of(index) // BLOCK
    clear = (start_of(index + BLOCK - 1) + BLOCK - 1) // BLOCK
    info = jnp.concatenate([low, clear, starts]).astype(jnp.int32)
    index = jnp.arange(group_rows, dtype=jnp.int32)
    position = (index - start_of(index)).astype(F32)
    inverse_rate = THETA ** (-(jnp.arange(HEAD_SIZE // 2, dtype=F32) * 2.0 / HEAD_SIZE))
    angle = position[:, None] * inverse_rate[None, :]
    cosine, sine = jnp.cos(angle), jnp.sin(angle)
    cosine = jnp.concatenate([cosine, cosine], axis=1)
    sine = jnp.concatenate([-sine, sine], axis=1)

    tokens_sorted = jnp.take(tokens_all, inverse, axis=0, mode="clip")
    cot_own = swap(cotangent)
    normed, qkv, scales = project(
        tokens_sorted, gain_one, heads_weights, gain_query, gain_key, cosine, sine, query_heads, key_heads
    )

    def exchange(parts):
        out = [parts[0]]
        for k in range(1, span):
            out.append(send(parts[k], lambda pp, cc, tt: (pp, cc ^ (k // half), tt ^ (k % half))))
        return out

    def by_chunk(parts):
        return [jnp.where(settled, parts[r], parts[(1 - r // half) * half + r % half]) for r in range(span)]

    attended, lse, chunks = [], [], []
    for kv in range(key_heads):
        out, total = attention_forward(info, qkv, query_heads, key_heads, docs, kv)
        attended.append(out)
        lse.append(total)
        out = jnp.take(out, places, axis=0, mode="clip")
        chunks.append(by_chunk(exchange([out[k * rows : (k + 1) * rows] for k in range(span)])))
    mixed = jnp.stack([jnp.concatenate([chunk[r] for chunk in chunks], axis=1) for r in range(span)])

    hidden = gate_weight.shape[1]
    middle, normed_two = output_project(mixed, output_weights, swapped, gain_two)
    out, normed_grad, first_grad = feed(normed_two, cot_own, feed_weights[0])
    result, middle_grad, branch, gain_two_grad, second_grad = feed(
        normed_two, cot_own, feed_weights[1], out, normed_grad, middle, gain_two
    )
    feed_back = line_back(scatter_wide(first_grad), 0) + line_back(scatter_wide(second_grad), 1)

    mixed_grad, output_grad = output_back(branch, mixed, output_weights)
    merged = by_chunk([mixed_grad[r] for r in range(span)])
    per_head = head_columns // key_heads
    grad_chunks = [exchange([x[:, kv * per_head : (kv + 1) * per_head] for x in merged]) for kv in range(key_heads)]
    output_sum = line_back(scatter_wide(output_grad), 0)
    layer_output = swap(result)

    head_grads, head_gains = [], 0.0
    for kv in range(key_heads):
        attended_grad = jnp.take(jnp.concatenate(grad_chunks[kv], axis=0), inverse, axis=0, mode="clip")
        grads, gains_of = attention_backward(
            info,
            qkv,
            attended[kv],
            attended_grad,
            lse[kv],
            cosine,
            sine,
            scales,
            gain_query,
            gain_key,
            query_heads,
            key_heads,
            docs,
            kv,
        )
        head_grads.append(grads)
        head_gains = head_gains + gains_of
    wide_q, wide_k = head_columns // key_heads, HEAD_SIZE
    qkv_grad = jnp.concatenate(
        [g[:, :wide_q] for g in head_grads]
        + [g[:, wide_q : wide_q + wide_k] for g in head_grads]
        + [g[:, wide_q + wide_k :] for g in head_grads],
        axis=1,
    )
    partial = dot_nt(jnp.take(qkv_grad, places, axis=0, mode="clip"), heads_weights).astype(BF16)
    parts = [partial[k * rows : (k + 1) * rows] for k in range(span)]
    moved = sibling(jnp.concatenate(parts[half:], axis=0))
    heads_grad = dot_tn(normed, qkv_grad).astype(BF16)
    heads = taker([(heads_grad,)])
    parts = [add(parts[k], moved[k * rows : (k + 1) * rows]) for k in range(half)]
    heads_arrived = scatter_start(heads)
    while len(parts) > 1:
        keep = len(parts) // 2
        moved = send(jnp.concatenate(parts[keep:], axis=0), lambda pp, cc, tt: (pp, cc, tt ^ keep))
        parts = [add(parts[k], moved[k * rows : (k + 1) * rows]) for k in range(keep)]
    heads_later = scatter_next(heads, heads_arrived)
    mine = scatter_end(heads, heads_later)
    moved = send(mine, lambda pp, cc, tt: (pp, cc, (tt + half) % span) if cc != tt // half else None)

    normed_grad = parts[0].astype(F32)
    inputs = swapped.astype(F32)
    r_one = row_scale(inputs)
    unit_one = inputs * r_one
    gain_one_grad = jnp.sum(normed_grad * unit_one, axis=0)
    scaled = normed_grad * gain_one
    input_grad = swap(
        (middle_grad + r_one * (scaled - unit_one * jnp.mean(scaled * unit_one, axis=-1, keepdims=True))).astype(BF16)
    )

    summed = mine.astype(F32) + moved.astype(F32)
    top, bottom = summed[:shard], summed[shard:]
    other = jnp.where(c == 0, bottom, top).astype(BF16)
    moved = send(other, lambda pp, cc, tt: (pp, 1 - cc, tt) if cc == tt // half else None).astype(F32)
    summed = jnp.where(settled, jnp.where(c == 0, top, bottom), moved)
    key_columns = key_heads * HEAD_SIZE

    def total(pieces):
        out = pieces[0].astype(F32)
        for piece in pieces[1:]:
            out = out + piece.astype(F32)
        return out

    wide_sum, output_sum = total(feed_back), total(output_sum)
    gain_sums = lax.psum(jnp.concatenate([gain_one_grad, head_gains[0], head_gains[1], gain_two_grad[0]]), AXES)
    cut = lambda at, size: lax.dynamic_slice(gain_sums, (at + dp * size,), (size,))
    return (
        layer_output,
        input_grad,
        cut(0, small),
        cut(width, tiny),
        cut(width + HEAD_SIZE, tiny),
        summed[:, :head_columns],
        summed[:, head_columns : head_columns + key_columns],
        summed[:, head_columns + key_columns :],
        output_sum.T,
        cut(width + 2 * HEAD_SIZE, small),
        wide_sum[:, :hidden],
        wide_sum[:, hidden : 2 * hidden],
        wide_sum[:, 2 * hidden :].T,
    )


def solution(mesh):
    placed = (
        P(AXES, None),
        P("dp", None),
        P("dp", None),
        P("dp"),
        P("dp"),
        P("dp"),
        P("dp", "tensor"),
        P("dp", "tensor"),
        P("dp", "tensor"),
        P("tensor", "dp"),
        P("dp"),
        P("dp", "tensor"),
        P("dp", "tensor"),
        P("tensor", "dp"),
        P(AXES, None),
    )
    return jax.shard_map(
        local,
        mesh=mesh,
        in_specs=placed,
        out_specs=(
            P(AXES, None),
            P(AXES, None),
            P("dp"),
            P("dp"),
            P("dp"),
            P("dp", "tensor"),
            P("dp", "tensor"),
            P("dp", "tensor"),
            P("tensor", "dp"),
            P("dp"),
            P("dp", "tensor"),
            P("dp", "tensor"),
            P("tensor", "dp"),
        ),
        check_vma=False,
    )
```

time: 914 us -> 749 us (0.82)
  waiting for transfers between devices: 313 us -> 195 us
  Pallas kernels: 179 us -> 279 us
  starting transfers between devices: 110 us -> 42.6 us
  other arithmetic: 79.7 us -> 44.6 us
  local copies, waits for them, and re-layouts: 126 us -> 99.8 us
  matrix products: 37.7 us -> 17.7 us
  between operations: 3.18 us -> 15.7 us
    ppermute x63 -> x32, waiting for transfers between devices: 313 us -> 195 us  [send(): return lax.ppermute(x, AXES, moves)]
    pallas_call x3 -> x7, Pallas kernels: 128 us -> 222 us  [the longest x2 73.7 us: attention_backward(): pl.pallas_call(functools.partial(backward_kernel, group, query_heads, kv,...]
    ppermute x63 -> x32, starting transfers between devices: 110 us -> 42.3 us  [send(): return lax.ppermute(x, AXES, moves)]
    convert_element_type x14 -> x5, other arithmetic: 28.3 us -> 4.05 us  [the longest x3 4 us: add(): return total.astype(BF16)]
    unnamed x1 -> x0, blocking collectives: 14.6 us -> none
    pallas_call x4 -> x0, local copies, waits for them, and re-layouts: 13 us -> none  [feed(): pl.pallas_call(feed_kernel, grid=(steps,), in_specs=[whole((rows, width))...]
    gather x2 -> x4, local copies, waits for them, and re-layouts: 18 us -> 30.7 us  [the longest x2 16.3 us: local(): jnp.take(jnp.concatenate(grad_chunks[kv], axis=0), inverse, axis=0, mode=...]
    dynamic_update_slice x14 -> x0, local copies, waits for them, and re-layouts: 11.2 us -> none  [gather_pairs(): lax.dynamic_update_slice(out, piece, (at * size + shift, 0))]
  transfers between devices with their start and end apart: 63 -> 38, of which waited for: 30 -> 16; matrix products, arithmetic and copies ran while one was open for 23% -> 20% of each run, Pallas kernels for 16% -> 21%
where the time goes in v2:
time: 749 us; the launch traced here: 743 us
  Pallas kernels  279 us (37%)
  waiting for transfers between devices  195 us (26%)
  local copies, waits for them, and re-layouts  99.8 us (13%)
  blocking collectives  48 us (6%)
  other arithmetic  44.6 us (6%)
  starting transfers between devices  42.6 us (6%)
  matrix products  17.7 us (2%)
  between operations  15.7 us (2%)
    ppermute x32, waiting for transfers between devices, send(): return lax.ppermute(x, AXES, moves)  195 us
    pallas_call x2, Pallas kernels, attention_backward(): pl.pallas_call(functools.partial(backward_kernel, group, query_heads, kv,...  73.7 us
    pallas_call x1, Pallas kernels, first_transfers(): pl.pallas_call(functools.partial(first_kernel, pairs, span), in_specs=[an...  65.8 us
    pallas_call x2, Pallas kernels, feed(): pl.pallas_call(functools.partial(feed_kernel, last), grid=(span,), in_spe...  62.8 us
    psum x1, blocking collectives, local(): lax.psum(jnp.concatenate([gain_one_grad, head_gains[0], head_gains[1], ga...  48 us
    pallas_call x2, Pallas kernels, attention_forward(): pl.pallas_call(functools.partial(forward_kernel, group, blocks, docs), gr...  42.6 us
    ppermute x32, starting transfers between devices, send(): return lax.ppermute(x, AXES, moves)  42.3 us
    gather x2, local copies, waits for them, and re-layouts, local(): jnp.take(jnp.concatenate(grad_chunks[kv], axis=0), inverse, axis=0, mode=...  16.3 us
  transfers between devices with their start and end apart: 38, of which 16 were waited for; matrix products, arithmetic and copies ran while one was open for 20% of the time, Pallas kernels for 21%

profile of v2, /device:TPU:0, one launch (start us, length us, event | category | flops | bytes accessed | tf_op | source)
XLA Modules:
  0.0 743.0 jit_solution(18088187646904475248)
XLA Ops:
  14.0 65.8 %first_transfers.1 = (bf16[4,640,1024]{2,1,0:T(8,128)(2,1)}, bf16[1024,1024]{1,0:T(8,128)(2,1)}, bf16[4,128,512]{2,1,0:T(8,128)(2,1)}, bf16[128,384]{1,0:T(8,128)(2,1)}, s32[24,128]{1,0:T(8,128)}) custom-call(bf16[640,1024]{1,0:T(8,128)(2,1)} %tokens_ref.1, bf16[128,1024]{1,0:T(8,128)(2,1)} %pad_maximum_fusion.10.heads_ref, bf16[128,512]{1,0:T(8,128)(2,1)} %bitcast.89, ...), custom_call_target="tpu_custom_call" | custom-call | tf_op jit(solution)/shard_map/first_transfers/pallas_call | solution.py:247
  91.9 19.0 %collective-permute-done.7 = bf16[128,2304]{1,0:T(8,128)(2,1)S(1)} collective-permute-done((bf16[128,2304]{1,0:T(8,128)(2,1)S(1)}, bf16[128,2304]{1,0:T(8,128)(2,1)S(1)}, u32[]{:S(2)}, u32[]{:S(2)}) %collective-permute-start.7) | collective-permute-done | bytes 589856 | tf_op jit(solution)/shard_map/ppermute | solution.py:772
  111.0 19.1 %collective-permute-done.8 = bf16[128,2304]{1,0:T(8,128)(2,1)S(1)} collective-permute-done((bf16[128,2304]{1,0:T(8,128)(2,1)S(1)}, bf16[128,2304]{1,0:T(8,128)(2,1)S(1)}, u32[]{:S(2)}, u32[]{:S(2)}) %collective-permute-start.8) | collective-permute-done | bytes 589856 | tf_op jit(solution)/shard_map/ppermute | solution.py:772
  139.5 15.8 %gather_fusion = bf16[2560,1024]{1,0:T(8,128)(2,1)} fusion(bf16[2560,1024]{1,0:T(8,128)(2,1)} %bitcast.78, s32[3072]{0:T(1024)S(1)} %get-tuple-element.170), kind=kCustom, calls=%fused_computation | custom fusion | bytes 10496000 | tf_op jit(solution)/shard_map/jit(_take)/gather | solution.py:900
  163.2 15.3 %project.1 = (bf16[2560,1024]{1,0:T(8,128)(2,1)}, bf16[2560,1024]{1,0:T(8,128)(2,1)}, f32[2560,128]{1,0:T(8,128)}) custom-call(bf16[2560,1024]{1,0:T(8,128)(2,1)} %gather_fusion, f32[1,1024]{1,0:T(1,128)} %bitcast.93, bf16[1024,1024]{1,0:T(8,128)(2,1)} %get-tuple-element.46.w_ref, f32[1,128]{1,0:T(1,128)} %reshape.127.gq_ref, f32[1,128]{1,0:T(1,128)} %reshape.128.gk_ref, ...), custom_call_target="tpu_custom_call" | custom-call | tf_op jit(solution)/shard_map/project/pallas_call | solution.py:295
  179.1 21.2 %attention_forward.2 = (bf16[2560,256]{1,0:T(8,128)(2,1)}, f32[10,8,512]{2,1,0:T(8,128)}) custom-call(s32[22]{0:T(128)} %pad_add_fusion.2.info_ref, bf16[2560,1024]{1,0:T(8,128)(2,1)} %get-tuple-element.47.q_ref.k_ref.v_ref, bf16[2560,1024]{1,0:T(8,128)(2,1)} %get-tuple-element.47.q_ref.k_ref.v_ref, bf16[2560,1024]{1,0:T(8,128)(2,1)} %get-tuple-element.47.q_ref.k_ref.v_ref), custom_call_target="tpu_custom_call" | custom-call | tf_op jit(solution)/shard_map/attention_forward/pallas_call | solution.py:379
  207.7 21.4 %attention_forward.3 = (bf16[2560,256]{1,0:T(8,128)(2,1)}, f32[10,8,512]{2,1,0:T(8,128)}) custom-call(s32[22]{0:T(128)} %pad_add_fusion.2.info_ref, bf16[2560,1024]{1,0:T(8,128)(2,1)} %get-tuple-element.47.q_ref.k_ref.v_ref, bf16[2560,1024]{1,0:T(8,128)(2,1)} %get-tuple-element.47.q_ref.k_ref.v_ref, bf16[2560,1024]{1,0:T(8,128)(2,1)} %get-tuple-element.47.q_ref.k_ref.v_ref), custom_call_target="tpu_custom_call" | custom-call | tf_op jit(solution)/shard_map/attention_forward/pallas_call | solution.py:379
  237.5 10.6 %collective-permute-start.2 = (bf16[640,256]{1,0:T(8,128)(2,1)S(1)}, bf16[640,256]{1,0:T(8,128)(2,1)S(1)}, u32[]{:S(2)}, u32[]{:S(2)}) collective-permute-start(bf16[640,256]{1,0:T(8,128)(2,1)S(1)} %get-tuple-element.123), channel_id=1, source_target_pairs={{0,1},{1,0},{2,3},{3,2},{4,5},{5,4},{6,7},{7,6},{8,9},{9,8},{10,11... | collective-permute-start | bytes 983048 | tf_op jit(solution)/shard_map/ppermute | solution.py:772
  252.5 12.1 %collective-permute-done.2 = bf16[640,256]{1,0:T(8,128)(2,1)S(1)} collective-permute-done((bf16[640,256]{1,0:T(8,128)(2,1)S(1)}, bf16[640,256]{1,0:T(8,128)(2,1)S(1)}, u32[]{:S(2)}, u32[]{:S(2)}) %collective-permute-start.2) | collective-permute-done | bytes 327712 | tf_op jit(solution)/shard_map/ppermute | solution.py:772
  289.2 9.0 %output_project.1 = (f32[640,1024]{1,0:T(8,128)}, bf16[640,1024]{1,0:T(8,128)(2,1)}) custom-call(bf16[4,640,512]{2,1,0:T(8,128)(2,1)} %pad_maximum_fusion.a_ref, bf16[8,4,128,512]{3,2,1,0:T(8,128)(2,1)} %bitcast.81, bf16[640,1024]{1,0:T(8,128)(2,1)} %copy-done, f32[1,1024]{1,0:T(1,128)} %bitcast.91), custom_call_target="tpu_custom_call" | custom-call | tf_op jit(solution)/shard_map/output_project/pallas_call | solution.py:585
  298.2 18.0 %feed_forward.2 = (f32[640,1024]{1,0:T(8,128)}, f32[640,1024]{1,0:T(8,128)}, bf16[8,1,128,2304]{3,2,1,0:T(8,128)(2,1)}) custom-call(bf16[640,1024]{1,0:T(8,128)(2,1)} %get-tuple-element.51.x_ref, bf16[640,1024]{1,0:T(8,128)(2,1)} %broadcast_select_fusion.2.c_ref, bf16[8,1,128,2304]{3,2,1,0:T(8,128)(2,1)} %bitcast.86), custom_call_target="tpu_custom_call" | custom-call | tf_op jit(solution)/shard_map/feed_forward/pallas_call | solution.py:715
  316.2 44.8 %feed_forward.3 = (bf16[640,1024]{1,0:T(8,128)(2,1)}, f32[640,1024]{1,0:T(8,128)}, bf16[640,1024]{1,0:T(8,128)(2,1)}, f32[8,1024]{1,0:T(8,128)}, bf16[8,3,128,2304]{3,2,1,0:T(8,128)(2,1)}) custom-call(bf16[640,1024]{1,0:T(8,128)(2,1)} %get-tuple-element.51.x_ref, bf16[640,1024]{1,0:T(8,128)(2,1)} %broadcast_select_fusion.2.c_ref, ...), custom_call_target="tpu_custom_call" | custom-call | tf_op jit(solution)/shard_map/feed_forward/pallas_call | solution.py:715
  361.0 10.3 %output_back.1 = (bf16[4,640,512]{2,1,0:T(8,128)(2,1)}, bf16[8,4,128,512]{3,2,1,0:T(8,128)(2,1)}) custom-call(bf16[640,1024]{1,0:T(8,128)(2,1)} %get-tuple-element.57.b_ref, bf16[4,640,512]{2,1,0:T(8,128)(2,1)} %pad_maximum_fusion.a_ref, bf16[8,4,128,512]{3,2,1,0:T(8,128)(2,1)} %bitcast.82), custom_call_target="tpu_custom_call" | custom-call | tf_op jit(solution)/shard_map/output_back/pallas_call | solution.py:616
  389.8 8.1 %gather_fusion.4 = bf16[2560,256]{1,0:T(8,128)(2,1)} fusion(bf16[2560,256]{1,0:T(8,128)(2,1)S(1)} %pad_maximum_fusion.5, s32[3072]{0:T(1024)S(1)} %get-tuple-element.170), kind=kCustom, calls=%fused_computation.4 | custom fusion | bytes 2631680 | tf_op jit(solution)/shard_map/jit(_take)/gather | solution.py:941
  404.1 8.1 %gather_fusion.3 = bf16[2560,256]{1,0:T(8,128)(2,1)} fusion(bf16[2560,256]{1,0:T(8,128)(2,1)S(1)} %pad_maximum_fusion.4, s32[3072]{0:T(1024)S(1)} %get-tuple-element.170), kind=kCustom, calls=%fused_computation.3 | custom fusion | bytes 2631680 | tf_op jit(solution)/shard_map/jit(_take)/gather | solution.py:941
  412.2 36.7 %attention_backward.2 = (bf16[2560,512]{1,0:T(8,128)(2,1)}, f32[8,128]{1,0:T(8,128)}) custom-call(s32[22]{0:T(128)} %pad_add_fusion.2.info_ref, bf16[2560,1024]{1,0:T(8,128)(2,1)} %get-tuple-element.47.q_ref.k_ref.v_ref, bf16[2560,1024]{1,0:T(8,128)(2,1)} %get-tuple-element.47.q_ref.k_ref.v_ref, bf16[2560,1024]{1,0:T(8,128)(2,1)} %get-tuple-element.47.q_ref.k_ref.v_ref, ...), custom_call_target="tpu_custom_call" | custom-call | tf_op jit(solution)/shard_map/attention_backward/pallas_call | solution.py:526
  451.6 37.0 %attention_backward.3 = (bf16[2560,512]{1,0:T(8,128)(2,1)}, f32[8,128]{1,0:T(8,128)}) custom-call(s32[22]{0:T(128)} %pad_add_fusion.2.info_ref, bf16[2560,1024]{1,0:T(8,128)(2,1)} %get-tuple-element.47.q_ref.k_ref.v_ref, bf16[2560,1024]{1,0:T(8,128)(2,1)} %get-tuple-element.47.q_ref.k_ref.v_ref, bf16[2560,1024]{1,0:T(8,128)(2,1)} %get-tuple-element.47.q_ref.k_ref.v_ref, ...), custom_call_target="tpu_custom_call" | custom-call | tf_op jit(solution)/shard_map/attention_backward/pallas_call | solution.py:526
  497.3 15.4 %gather_fusion.5 = bf16[2560,1024]{1,0:T(8,128)(2,1)} fusion(bf16[2560,1024]{1,0:T(8,128)(2,1)} %slice_dynamic-update-slice_fusion.2, s32[3072]{0:T(1024)S(1)} %get-tuple-element.169), kind=kCustom, calls=%fused_computation.5 | custom fusion | bytes 10496000 | tf_op jit(solution)/shard_map/jit(_take)/gather | solution.py:967
  512.7 8.6 %convolution_convert_fusion = bf16[2560,1024]{1,0:T(8,128)(2,1)S(1)} fusion(bf16[2560,1024]{1,0:T(8,128)(2,1)} %gather_fusion.5, bf16[1024,1024]{1,0:T(8,128)(2,1)S(1)} %copy-done.5), kind=kOutput, calls=%fused_computation.6 | convolution fusion | flops 5371330560 | bytes 12582912 | tf_op jit(solution)/shard_map/dot_general | solution.py:28
  526.8 9.1 %convolution_convert_fusion.1 = bf16[1024,1024]{1,0:T(8,128)(2,1)S(1)} fusion(bf16[2560,1024]{1,0:T(8,128)(2,1)} %get-tuple-element.67, bf16[2560,1024]{1,0:T(8,128)(2,1)} %slice_dynamic-update-slice_fusion.2), kind=kOutput, calls=%fused_computation.24 | convolution fusion | flops 5369757696 | bytes 12582912 | tf_op jit(solution)/shard_map/dot_general | solution.py:32
  553.1 15.9 %collective-permute-done.21 = bf16[256,1024]{1,0:T(8,128)(2,1)} collective-permute-done((bf16[256,1024]{1,0:T(8,128)(2,1)}, bf16[256,1024]{1,0:T(8,128)(2,1)}, u32[]{:S(2)}, u32[]{:S(2)}) %collective-permute-start.21) | collective-permute-done | bytes 524320 | tf_op jit(solution)/shard_map/ppermute | solution.py:772
  578.5 17.0 %collective-permute-done.24 = bf16[256,1024]{1,0:T(8,128)(2,1)S(1)} collective-permute-done((bf16[256,1024]{1,0:T(8,128)(2,1)S(1)}, bf16[256,1024]{1,0:T(8,128)(2,1)S(1)}, u32[]{:S(2)}, u32[]{:S(2)}) %collective-permute-start.24) | collective-permute-done | bytes 524320 | tf_op jit(solution)/shard_map/ppermute | solution.py:772
  613.2 48.0 %psum.7 = f32[2304]{0:T(1024)S(1)} all-reduce(f32[2304]{0:T(1024)S(1)} %pad_maximum_fusion.11), channel_id=1, replica_groups=mesh['dp'=8,'tensor'=4] {'dp','tensor'}, use_global_device_ids=true, to_apply=%region_8.9 | all-reduce | flops 2304 | bytes 18432 | tf_op jit(solution)/shard_map/psum | solution.py:1006
  675.7 55.0 %collective-permute-done.27 = bf16[128,512]{1,0:T(8,128)(2,1)S(1)} collective-permute-done((bf16[128,512]{1,0:T(8,128)(2,1)S(1)}, bf16[128,512]{1,0:T(8,128)(2,1)S(1)}, u32[]{:S(2)}, u32[]{:S(2)}) %collective-permute-start.27) | collective-permute-done | bytes 131104 | tf_op jit(solution)/shard_map/ppermute | solution.py:772
  (208 shorter events, 186.0 us)
Async XLA Ops:
  7.2 282.1 %all-gather.4.cloned.1.call-start = ((), (), s32[]{:S(2)}) async-start(), calls=%async_computation.3 | async-start | bytes 4718592 | tf_op jit(solution)/shard_map/all_gather | solution.py:836
  81.8 216.4 %all-gather.8.cloned.1.call-start = ((), (), s32[]{:S(2)}) async-start(), calls=%async_computation.5 | async-start | bytes 5308416 | tf_op jit(solution)/shard_map/all_gather | solution.py:836
  87.4 228.8 %all-gather.6.cloned.1.call-start = ((), (), s32[]{:S(2)}) async-start(), calls=%async_computation.4 | async-start | bytes 15925248 | tf_op jit(solution)/shard_map/all_gather | solution.py:836
  87.6 42.5 %collective-permute-start.8 = (bf16[128,2304]{1,0:T(8,128)(2,1)S(1)}, bf16[128,2304]{1,0:T(8,128)(2,1)S(1)}, u32[]{:S(2)}, u32[]{:S(2)}) collective-permute-start(bf16[128,2304]{1,0:T(8,128)(2,1)S(1)} %get-tuple-element.143), channel_id=1, source_target_pairs={{0,2},{1,3},{2,0},{3,1},{4,6},{5,7},{6,4},{7,5},{8,10},{9,11},{10,... | collective-permute-start | bytes 1769480 | tf_op jit(solution)/shard_map/ppermute | solution.py:772
  87.7 42.4 %collective-permute-start.9 = (bf16[128,2304]{1,0:T(8,128)(2,1)S(1)}, bf16[128,2304]{1,0:T(8,128)(2,1)S(1)}, u32[]{:S(2)}, u32[]{:S(2)}) collective-permute-start(bf16[128,2304]{1,0:T(8,128)(2,1)S(1)} %get-tuple-element.143), channel_id=1, source_target_pairs={{0,3},{1,2},{2,1},{3,0},{4,7},{5,6},{6,5},{7,4},{8,11},{9,10},{10,... | collective-permute-start | bytes 1769480 | tf_op jit(solution)/shard_map/ppermute | solution.py:772
  131.5 530.2 %reduce-scatter.4.cloned.1.call-start = ((), (), s32[]{:S(2)}) async-start(), calls=%async_computation.6 | async-start | bytes 4718592 | tf_op jit(solution)/shard_map/reduce_scatter | solution.py:842
  207.6 29.8 %collective-permute-start = (bf16[640,256]{1,0:T(8,128)(2,1)S(1)}, bf16[640,256]{1,0:T(8,128)(2,1)S(1)}, u32[]{:S(2)}, u32[]{:S(2)}) collective-permute-start(bf16[640,256]{1,0:T(8,128)(2,1)S(1)} %slice.274), channel_id=1, source_target_pairs={{0,4},{1,5},{2,6},{3,7},{4,0},{5,1},{6,2},{7,3},{8,12},{9,13},{10,... | collective-permute-start | bytes 983048 | tf_op jit(solution)/shard_map/ppermute | solution.py:772
  236.7 51.4 %collective-permute-start.6 = (bf16[640,1024]{1,0:T(8,128)(2,1)}, bf16[640,1024]{1,0:T(8,128)(2,1)S(1)}, u32[]{:S(2)}, u32[]{:S(2)}) collective-permute-start(bf16[640,1024]{1,0:T(8,128)(2,1)} %param.29), channel_id=1, source_target_pairs={{2,5},{3,4},{4,3},{5,2},{10,13},{11,12},{12,11},{13,10},{18,21},{1... | collective-permute-start | bytes 3932168 | tf_op jit(solution)/shard_map/ppermute | solution.py:772
  237.5 27.2 %collective-permute-start.2 = (bf16[640,256]{1,0:T(8,128)(2,1)S(1)}, bf16[640,256]{1,0:T(8,128)(2,1)S(1)}, u32[]{:S(2)}, u32[]{:S(2)}) collective-permute-start(bf16[640,256]{1,0:T(8,128)(2,1)S(1)} %get-tuple-element.123), channel_id=1, source_target_pairs={{0,1},{1,0},{2,3},{3,2},{4,5},{5,4},{6,7},{7,6},{8,9},{9,8},{10,11... | collective-permute-start | bytes 983048 | tf_op jit(solution)/shard_map/ppermute | solution.py:772
  248.1 24.2 %collective-permute-start.3 = (bf16[640,256]{1,0:T(8,128)(2,1)S(1)}, bf16[640,256]{1,0:T(8,128)(2,1)S(1)}, u32[]{:S(2)}, u32[]{:S(2)}) collective-permute-start(bf16[640,256]{1,0:T(8,128)(2,1)S(1)} %get-tuple-element.124), channel_id=1, source_target_pairs={{0,5},{1,4},{2,7},{3,6},{4,1},{5,0},{6,3},{7,2},{8,13},{9,12},{10,... | collective-permute-start | bytes 983048 | tf_op jit(solution)/shard_map/ppermute | solution.py:772
  250.7 28.1 %collective-permute-start.4 = (bf16[640,256]{1,0:T(8,128)(2,1)S(1)}, bf16[640,256]{1,0:T(8,128)(2,1)S(1)}, u32[]{:S(2)}, u32[]{:S(2)}) collective-permute-start(bf16[640,256]{1,0:T(8,128)(2,1)S(1)} %get-tuple-element.125), channel_id=1, source_target_pairs={{0,1},{1,0},{2,3},{3,2},{4,5},{5,4},{6,7},{7,6},{8,9},{9,8},{10,11... | collective-permute-start | bytes 983048 | tf_op jit(solution)/shard_map/ppermute | solution.py:772
  252.4 33.6 %collective-permute-start.5 = (bf16[640,256]{1,0:T(8,128)(2,1)S(1)}, bf16[640,256]{1,0:T(8,128)(2,1)S(1)}, u32[]{:S(2)}, u32[]{:S(2)}) collective-permute-start(bf16[640,256]{1,0:T(8,128)(2,1)S(1)} %get-tuple-element.126), channel_id=1, source_target_pairs={{0,5},{1,4},{2,7},{3,6},{4,1},{5,0},{6,3},{7,2},{8,13},{9,12},{10,... | collective-permute-start | bytes 983048 | tf_op jit(solution)/shard_map/ppermute | solution.py:772
  371.3 292.1 %reduce-scatter.8.cloned.1.call-start = ((), (), s32[]{:S(2)}) async-start(), calls=%async_computation.8 | async-start | bytes 15925248 | tf_op jit(solution)/shard_map/reduce_scatter | solution.py:842
  371.9 360.6 %reduce-scatter.6.cloned.1.call-start = ((), (), s32[]{:S(2)}) async-start(), calls=%async_computation.7 | async-start | bytes 5308416 | tf_op jit(solution)/shard_map/reduce_scatter | solution.py:842
  524.4 51.7 %collective-permute-start.17 = (bf16[1280,1024]{1,0:T(8,128)(2,1)}, bf16[1280,1024]{1,0:T(8,128)(2,1)}, u32[]{:S(2)}, u32[]{:S(2)}) collective-permute-start(bf16[1280,1024]{1,0:T(8,128)(2,1)} %concatenate.84), channel_id=1, source_target_pairs={{0,4},{1,5},{2,6},{3,7},{4,0},{5,1},{6,2},{7,3},{8,12},{9,13},{10,... | collective-permute-start | bytes 7864328 | tf_op jit(solution)/shard_map/ppermute | solution.py:772
  549.5 23.8 %collective-permute-start.23 = (bf16[256,1024]{1,0:T(8,128)(2,1)}, bf16[256,1024]{1,0:T(8,128)(2,1)}, u32[]{:S(2)}, u32[]{:S(2)}) collective-permute-start(bf16[256,1024]{1,0:T(8,128)(2,1)} %pad_maximum_fusion.9), channel_id=1, source_target_pairs={{0,16},{1,17},{2,18},{3,19},{4,20},{5,21},{6,22},{7,23},{8,24},{9,... | collective-permute-start | bytes 1572872 | tf_op jit(solution)/shard_map/ppermute | solution.py:772
  552.3 44.7 %collective-permute-start.10 = (bf16[640,1024]{1,0:T(8,128)(2,1)}, bf16[640,1024]{1,0:T(8,128)(2,1)S(1)}, u32[]{:S(2)}, u32[]{:S(2)}) collective-permute-start(bf16[640,1024]{1,0:T(8,128)(2,1)} %get-tuple-element.55), channel_id=1, source_target_pairs={{2,5},{3,4},{4,3},{5,2},{10,13},{11,12},{12,11},{13,10},{18,21},{1... | collective-permute-start | bytes 3932168 | tf_op jit(solution)/shard_map/ppermute | solution.py:772
  578.4 29.1 %collective-permute-start.18 = (bf16[640,1024]{1,0:T(8,128)(2,1)S(1)}, bf16[640,1024]{1,0:T(8,128)(2,1)S(1)}, u32[]{:S(2)}, u32[]{:S(2)}) collective-permute-start(bf16[640,1024]{1,0:T(8,128)(2,1)S(1)} %add_convert_fusion.1), channel_id=1, source_target_pairs={{0,1},{1,0},{2,3},{3,2},{4,5},{5,4},{6,7},{7,6},{8,9},{9,8},{10,11... | collective-permute-start | bytes 3932168 | tf_op jit(solution)/shard_map/ppermute | solution.py:772
  611.4 59.6 %collective-permute-start.19 = (bf16[640,1024]{1,0:T(8,128)(2,1)S(1)}, bf16[640,1024]{1,0:T(8,128)(2,1)}, u32[]{:S(2)}, u32[]{:S(2)}) collective-permute-start(bf16[640,1024]{1,0:T(8,128)(2,1)S(1)} %fusion.5), channel_id=1, source_target_pairs={{2,5},{3,4},{4,3},{5,2},{10,13},{11,12},{12,11},{13,10},{18,21},{1... | collective-permute-start | bytes 3932168 | tf_op jit(solution)/shard_map/ppermute | solution.py:772
  666.0 66.5 %collective-permute-start.29 = (bf16[128,2304]{1,0:T(8,128)(2,1)}, bf16[128,2304]{1,0:T(8,128)(2,1)S(1)}, u32[]{:S(2)}, u32[]{:S(2)}) collective-permute-start(bf16[128,2304]{1,0:T(8,128)(2,1)} %get-tuple-element.116), channel_id=1, source_target_pairs={{0,1},{1,0},{2,3},{3,2},{4,5},{5,4},{6,7},{7,6},{8,9},{9,8},{10,11... | collective-permute-start | bytes 1769480 | tf_op jit(solution)/shard_map/ppermute | solution.py:772
  668.0 64.4 %collective-permute-start.30 = (bf16[128,2304]{1,0:T(8,128)(2,1)}, bf16[128,2304]{1,0:T(8,128)(2,1)S(1)}, u32[]{:S(2)}, u32[]{:S(2)}) collective-permute-start(bf16[128,2304]{1,0:T(8,128)(2,1)} %get-tuple-element.117), channel_id=1, source_target_pairs={{0,2},{1,3},{2,0},{3,1},{4,6},{5,7},{6,4},{7,5},{8,10},{9,11},{10,... | collective-permute-start | bytes 1769480 | tf_op jit(solution)/shard_map/ppermute | solution.py:772
  668.9 63.6 %collective-permute-start.31 = (bf16[128,2304]{1,0:T(8,128)(2,1)S(1)}, bf16[128,2304]{1,0:T(8,128)(2,1)}, u32[]{:S(2)}, u32[]{:S(2)}) collective-permute-start(bf16[128,2304]{1,0:T(8,128)(2,1)S(1)} %get-tuple-element.118), channel_id=1, source_target_pairs={{0,3},{1,2},{2,1},{3,0},{4,7},{5,6},{6,5},{7,4},{8,11},{9,10},{10,... | collective-permute-start | bytes 1769480 | tf_op jit(solution)/shard_map/ppermute | solution.py:772
  671.0 59.7 %collective-permute-start.27 = (bf16[128,512]{1,0:T(8,128)(2,1)S(1)}, bf16[128,512]{1,0:T(8,128)(2,1)S(1)}, u32[]{:S(2)}, u32[]{:S(2)}) collective-permute-start(bf16[128,512]{1,0:T(8,128)(2,1)S(1)} %get-tuple-element.145), channel_id=1, source_target_pairs={{0,2},{1,3},{2,0},{3,1},{4,6},{5,7},{6,4},{7,5},{8,10},{9,11},{10,... | collective-permute-start | bytes 393224 | tf_op jit(solution)/shard_map/ppermute | solution.py:772
  673.0 57.7 %collective-permute-start.28 = (bf16[128,512]{1,0:T(8,128)(2,1)S(1)}, bf16[128,512]{1,0:T(8,128)(2,1)S(1)}, u32[]{:S(2)}, u32[]{:S(2)}) collective-permute-start(bf16[128,512]{1,0:T(8,128)(2,1)S(1)} %get-tuple-element.146), channel_id=1, source_target_pairs={{0,3},{1,2},{2,1},{3,0},{4,7},{5,6},{6,5},{7,4},{8,11},{9,10},{10,... | collective-permute-start | bytes 393224 | tf_op jit(solution)/shard_map/ppermute | solution.py:772
  (30 other events, 467.9 us)
Sparse Core Ops, SparseCore 0:
  81.9 35.1 all-gather.3
  119.1 38.9 all-gather.7
  159.9 79.1 all-gather.5
  371.4 49.0 reduce-scatter.3
  424.4 100.7 reduce-scatter.7
  528.8 59.6 reduce-scatter.5

commit v3 on v2

--- a/solution.py
+++ b/solution.py
@@ -12,7 +12,9 @@
 EPSILON = 1e-06
 THETA = 1000000.0
 AXES = ("dp", "tensor")
-BLOCK = 256
+ROWS = 256
+BLOCK = 512
+STEP = 512
 SCALE = HEAD_SIZE ** (-0.5)
 LOG2E = 1.4426950408889634
 VMEM_LIMIT = 56 * 1024 * 1024
@@ -261,6 +263,7 @@
             pltpu.SemaphoreType.DMA((4,)),
         ],
         compiler_params=pltpu.CompilerParams(collective_id=0, has_side_effects=True),
+        cost_estimate=pl.CostEstimate(flops=0, bytes_accessed=150_000_000, transcendentals=0),
         name="first_transfers",
     )(tokens, heads, output, gains, facts)
 
@@ -275,26 +278,30 @@
     cosine, sine = cos_ref[...], sin_ref[...]
     lane = lax.broadcasted_iota(jnp.int32, (x.shape[0], HEAD_SIZE), 1)
     scales = jnp.zeros((x.shape[0], HEAD_SIZE), F32)
-    for head in range(query_heads + key_heads):
-        span = slice(head * HEAD_SIZE, (head + 1) * HEAD_SIZE)
+    group = query_heads // key_heads
+    for at in range(query_heads + 2 * key_heads):
+        kv, kind = at // (group + 2), at % (group + 2)
+        span = slice(at * HEAD_SIZE, (at + 1) * HEAD_SIZE)
         u = raw[:, span]
+        if kind == group + 1:
+            qkv_ref[:, span] = u.astype(BF16)
+            continue
         r = row_scale(u)
-        gain = gq_ref[...] if head < query_heads else gk_ref[...]
+        gain = gq_ref[...] if kind < group else gk_ref[...]
         qkv_ref[:, span] = rotate(u * r * gain, cosine, sine).astype(BF16)
-        scales = jnp.where(lane == head, r, scales)
-    span = slice((query_heads + key_heads) * HEAD_SIZE, None)
-    qkv_ref[:, span] = raw[:, span].astype(BF16)
-    scale_ref[...] = scales
+        scales = jnp.where(lane == kind, r, scales) if kind else jnp.broadcast_to(r, scales.shape)
+        if kind == group:
+            scale_ref[kv] = scales
 
 
 def project(x, gain, weights, gain_query, gain_key, cosine, sine, query_heads, key_heads):
     rows, width = x.shape
     wide = weights.shape[1]
     whole = lambda shape: pl.BlockSpec(shape, lambda i: (0, 0))
-    block = lambda cols: pl.BlockSpec((BLOCK, cols), lambda i: (i, 0))
+    block = lambda cols: pl.BlockSpec((ROWS, cols), lambda i: (i, 0))
     return pl.pallas_call(
         functools.partial(project_kernel, query_heads, key_heads),
-        grid=(rows // BLOCK,),
+        grid=(rows // ROWS,),
         in_specs=[
             block(width),
             whole((1, width)),
@@ -304,11 +311,11 @@
             block(HEAD_SIZE),
             block(HEAD_SIZE),
         ],
-        out_specs=[block(width), block(wide), block(HEAD_SIZE)],
+        out_specs=[block(width), block(wide), pl.BlockSpec((key_heads, ROWS, HEAD_SIZE), lambda i: (0, i, 0))],
         out_shape=[
             jax.ShapeDtypeStruct((rows, width), BF16),
             jax.ShapeDtypeStruct((rows, wide), BF16),
-            jax.ShapeDtypeStruct((rows, HEAD_SIZE), F32),
+            jax.ShapeDtypeStruct((key_heads, rows, HEAD_SIZE), F32),
         ],
         compiler_params=pltpu.CompilerParams(vmem_limit_bytes=VMEM_LIMIT),
         name="project",
@@ -323,55 +330,66 @@
     return start
 
 
-def forward_kernel(group, blocks, docs, info_ref, q_ref, k_ref, v_ref, o_ref, lse_ref, wide_ref, acc_ref):
-    i = pl.program_id(0)
+def across(values, terms):
+    ones = jnp.ones((8, HEAD_SIZE), BF16)
+    total = None
+    for _ in range(terms):
+        part = values.astype(BF16)
+        values = values - part.astype(F32)
+        total = dot_nt(ones, part) if total is None else total + dot_nt(ones, part)
+    return total
+
+
+def keep_padded(pairs):
+    for ref, kept in pairs:
+        rows = ref.shape[0]
+        kept[:rows, : ref.shape[1]] = ref[...]
+        kept[rows:, : ref.shape[1]] = jnp.zeros((kept.shape[0] - rows, ref.shape[1]), BF16)
+
+
+def forward_kernel(group, blocks, docs, info_ref, q_ref, k_ref, v_ref, o_ref, lse_ref, keys_s, wide_s, acc_ref):
+    i = pl.program_id(1)
 
     @pl.when(i == 0)
     def _():
-        wide_ref[:, :HEAD_SIZE] = v_ref[...]
-        wide_ref[:, HEAD_SIZE:] = jnp.ones_like(v_ref)
-
-    queries = jnp.concatenate([q_ref[:, h * HEAD_SIZE : (h + 1) * HEAD_SIZE] for h in range(group)], axis=0)
+        keep_padded(((k_ref, keys_s), (v_ref, wide_s)))
+        wide_s[:, HEAD_SIZE:] = jnp.ones((wide_s.shape[0], HEAD_SIZE), BF16)
+
     acc_ref[...] = jnp.zeros_like(acc_ref)
-    shape = (group * BLOCK, BLOCK)
-
-    def step(j, masked):
-        rows = pl.ds(pl.multiple_of(j * BLOCK, BLOCK), BLOCK)
-        weights = jnp.exp2(dot_nt(queries, k_ref[rows, :]) * (SCALE * LOG2E))
-        if masked:
-            places = i * BLOCK + lax.rem(lax.broadcasted_iota(jnp.int32, (group * BLOCK, 1), 0), BLOCK)
-            start = first_place(info_ref, blocks, docs, places)
-            other = j * BLOCK + lax.broadcasted_iota(jnp.int32, shape, 1)
-            weights = jnp.where((other <= places) & (other >= start), weights, 0.0)
-        acc_ref[...] += dot_nn(weights.astype(BF16), wide_ref[rows, :])
-
-    low, clear = info_ref[i], info_ref[blocks + i]
-
-    def masked_step(j, carry):
-        step(j, True)
+    places = i * BLOCK + lax.broadcasted_iota(jnp.int32, (BLOCK, 1), 0)
+    start = first_place(info_ref, blocks, docs, places)
+    low = info_ref[i]
+
+    def step(m, carry):
+        base = (low + m * (STEP // BLOCK)) * BLOCK
+        rows = pl.ds(pl.multiple_of(base, BLOCK), STEP)
+        keys, values = keys_s[rows, :], wide_s[rows, :]
+        other = base + lax.broadcasted_iota(jnp.int32, (BLOCK, STEP), 1)
+        keep = (other <= places) & (other >= start)
+        scores = [dot_nt(q_ref[:, h * HEAD_SIZE : (h + 1) * HEAD_SIZE], keys) for h in range(group)]
+        for h in range(group):
+            weights = jnp.where(keep, jnp.exp2(scores[h] * (SCALE * LOG2E)), 0.0)
+            acc_ref[h * BLOCK : (h + 1) * BLOCK, :] += dot_nn(weights.astype(BF16), values)
         return carry
 
-    def clear_step(j, carry):
-        step(j, False)
-        return carry
-
-    lax.fori_loop(low, jnp.minimum(clear, i), masked_step, 0)
-    lax.fori_loop(jnp.minimum(clear, i), i, clear_step, 0)
-    step(i, True)
+    lax.fori_loop(0, (i - low) // (STEP // BLOCK) + 1, step, 0)
     total = acc_ref[:, HEAD_SIZE:]
     out = (acc_ref[:, :HEAD_SIZE] / total).astype(BF16)
     for h in range(group):
-        o_ref[:, h * HEAD_SIZE : (h + 1) * HEAD_SIZE] = out[h * BLOCK : (h + 1) * BLOCK]
-    lse_ref[0] = lax.dot_general(
-        jnp.full((8, HEAD_SIZE), 1.0 / HEAD_SIZE, F32),
-        jnp.log2(total),
-        (((1,), (1,)), ((), ())),
-        precision=lax.Precision.HIGHEST,
-        preferred_element_type=F32,
-    )
-
-
-def attention_forward(info, qkv, query_heads, key_heads, docs, kv):
+        o_ref[0, :, h * HEAD_SIZE : (h + 1) * HEAD_SIZE] = out[h * BLOCK : (h + 1) * BLOCK]
+    lse_ref[0, 0] = across(jnp.log2(total) * (1.0 / HEAD_SIZE), 3)
+
+
+def head_specs(rows, group, first):
+    wide = group * HEAD_SIZE
+    return [
+        pl.BlockSpec((BLOCK, wide), lambda h, i, s: (i, (first + h) * (group + 2) // group)),
+        pl.BlockSpec((rows, HEAD_SIZE), lambda h, i, s: (0, (first + h) * (group + 2) + group)),
+        pl.BlockSpec((rows, HEAD_SIZE), lambda h, i, s: (0, (first + h) * (group + 2) + group + 1)),
+    ]
+
+
+def attention_forward(info, qkv, query_heads, key_heads, docs):
     rows = qkv.shape[0]
     blocks = rows // BLOCK
     group = query_heads // key_heads
@@ -380,34 +398,30 @@
         functools.partial(forward_kernel, group, blocks, docs),
         grid_spec=pltpu.PrefetchScalarGridSpec(
             num_scalar_prefetch=1,
-            grid=(blocks,),
-            in_specs=[
-                pl.BlockSpec((BLOCK, wide), lambda i, s: (i, kv)),
-                pl.BlockSpec((rows, HEAD_SIZE), lambda i, s: (0, query_heads + kv)),
-                pl.BlockSpec((rows, HEAD_SIZE), lambda i, s: (0, query_heads + key_heads + kv)),
-            ],
+            grid=(key_heads, blocks),
+            in_specs=head_specs(rows, group, 0),
             out_specs=[
-                pl.BlockSpec((BLOCK, wide), lambda i, s: (i, 0)),
-                pl.BlockSpec((1, 8, group * BLOCK), lambda i, s: (i, 0, 0)),
+                pl.BlockSpec((1, BLOCK, wide), lambda h, i, s: (h, i, 0)),
+                pl.BlockSpec((1, 1, 8, group * BLOCK), lambda h, i, s: (h, i, 0, 0)),
             ],
             scratch_shapes=[
-                pltpu.VMEM((rows, 2 * HEAD_SIZE), BF16),
+                pltpu.VMEM((rows + STEP, HEAD_SIZE), BF16),
+                pltpu.VMEM((rows + STEP, 2 * HEAD_SIZE), BF16),
                 pltpu.VMEM((group * BLOCK, 2 * HEAD_SIZE), F32),
             ],
         ),
         out_shape=[
-            jax.ShapeDtypeStruct((rows, wide), BF16),
-            jax.ShapeDtypeStruct((blocks, 8, group * BLOCK), F32),
+            jax.ShapeDtypeStruct((key_heads, rows, wide), BF16),
+            jax.ShapeDtypeStruct((key_heads, blocks, 8, group * BLOCK), F32),
         ],
         compiler_params=pltpu.CompilerParams(vmem_limit_bytes=VMEM_LIMIT),
+        cost_estimate=pl.CostEstimate(flops=0, bytes_accessed=100_000_000, transcendentals=0),
         name="attention_forward",
     )(info, qkv, qkv, qkv)
 
 
 def backward_kernel(
     group,
-    query_heads,
-    kv,
     blocks,
     docs,
     info_ref,
@@ -427,65 +441,52 @@
     dk_acc,
     dv_acc,
     dq_acc,
+    keys_s,
+    values_s,
 ):
-    i = pl.program_id(0)
+    i = pl.program_id(1)
+    rows_all = k_ref.shape[0]
 
     @pl.when(i == 0)
     def _():
         dk_acc[...] = jnp.zeros_like(dk_acc)
         dv_acc[...] = jnp.zeros_like(dv_acc)
+        keep_padded(((k_ref, keys_s), (v_ref, values_s)))
+
+    @pl.when(i == 0)
+    def _():
         dgain_ref[...] = jnp.zeros_like(dgain_ref)
 
-    def stacked(ref):
-        return jnp.concatenate([ref[:, h * HEAD_SIZE : (h + 1) * HEAD_SIZE] for h in range(group)], axis=0)
-
-    queries, grads = stacked(q_ref), stacked(do_ref)
-    product = stacked(o_ref).astype(F32) * grads.astype(F32)
-    delta = lax.dot_general(
-        jnp.ones((8, HEAD_SIZE), F32),
-        product,
-        (((1,), (1,)), ((), ())),
-        precision=lax.Precision.HIGHEST,
-        preferred_element_type=F32,
-    )[:1]
-    lse = lse_ref[0, :1]
+    def stacked(value):
+        return jnp.concatenate([value[:, h * HEAD_SIZE : (h + 1) * HEAD_SIZE] for h in range(group)], axis=0)
+
+    queries, grads = stacked(q_ref[...]), stacked(do_ref[...])
+    delta = across(stacked(o_ref[0]).astype(F32) * grads.astype(F32), 2)[:1]
+    lse = lse_ref[0, 0, :1]
     dq_acc[...] = jnp.zeros_like(dq_acc)
-    shape = (BLOCK, group * BLOCK)
-
-    def step(j, masked):
-        rows = pl.ds(pl.multiple_of(j * BLOCK, BLOCK), BLOCK)
-        keys, values = k_ref[rows, :], v_ref[rows, :]
-        probs = jnp.exp2(dot_nt(keys, queries) * (SCALE * LOG2E) - lse)
-        if masked:
-            places = i * BLOCK + lax.rem(lax.broadcasted_iota(jnp.int32, (1, group * BLOCK), 1), BLOCK)
-            start = first_place(info_ref, blocks, docs, places)
-            other = j * BLOCK + lax.broadcasted_iota(jnp.int32, shape, 0)
-            probs = jnp.where((other <= places) & (other >= start), probs, 0.0)
+    places = i * BLOCK + lax.rem(lax.broadcasted_iota(jnp.int32, (1, group * BLOCK), 1), BLOCK)
+    start = first_place(info_ref, blocks, docs, places)
+    low = info_ref[i]
+
+    def step(m, carry):
+        base = (low + m * (STEP // BLOCK)) * BLOCK
+        rows = pl.ds(pl.multiple_of(base, BLOCK), STEP)
+        keys, values = keys_s[rows, :], values_s[rows, :]
+        other = base + lax.broadcasted_iota(jnp.int32, (STEP, group * BLOCK), 0)
+        keep = (other <= places) & (other >= start)
+        probs = jnp.where(keep, jnp.exp2(dot_nt(keys, queries) * (SCALE * LOG2E) - lse), 0.0)
         score_grad = (probs * (dot_nt(values, grads) - delta)).astype(BF16)
         dv_acc[rows, :] += dot_nn(probs.astype(BF16), grads)
         dk_acc[rows, :] += dot_nn(score_grad, queries)
         dq_acc[...] += dot_tn(score_grad, keys)
-
-    low, clear = info_ref[i], info_ref[blocks + i]
-
-    def masked_step(j, carry):
-        step(j, True)
         return carry
 
-    def clear_step(j, carry):
-        step(j, False)
-        return carry
-
-    lax.fori_loop(low, jnp.minimum(clear, i), masked_step, 0)
-    lax.fori_loop(jnp.minimum(clear, i), i, clear_step, 0)
-    step(i, True)
-
-    lane = lax.broadcasted_iota(jnp.int32, (BLOCK, HEAD_SIZE), 1)
-
-    def raw_grad(grad, rotated, rows, head, gain):
+    lax.fori_loop(0, (i - low) // (STEP // BLOCK) + 1, step, 0)
+
+    def raw_grad(grad, rotated, rows, kind, gain):
         cosine, sine = cos_ref[rows, :], sin_ref[rows, :]
-        r = jnp.sum(jnp.where(lane == head, scale_ref[rows, :], 0.0), axis=1, keepdims=True)
-        unit = unrotate(rotated.astype(F32), cosine, sine) / gain
+        r = scale_ref[0, rows, kind : kind + 1]
+        unit = unrotate(rotated.astype(F32), cosine, sine) * (1.0 / gain)
         back = unrotate(grad * SCALE, cosine, sine)
         scaled = back * gain
         raw = r * (scaled - unit * jnp.mean(scaled * unit, axis=1, keepdims=True))
@@ -494,19 +495,17 @@
     here = pl.ds(pl.multiple_of(i * BLOCK, BLOCK), BLOCK)
     for h in range(group):
         span = slice(h * HEAD_SIZE, (h + 1) * HEAD_SIZE)
-        raw, gain_grad = raw_grad(
-            dq_acc[h * BLOCK : (h + 1) * BLOCK, :], q_ref[:, span], here, kv * group + h, gq_ref[...]
-        )
+        raw, gain_grad = raw_grad(dq_acc[h * BLOCK : (h + 1) * BLOCK, :], q_ref[:, span], here, h, gq_ref[...])
         grad_ref[here, span] = raw
         dgain_ref[0:1, :] += gain_grad
 
     @pl.when(i == blocks - 1)
     def _():
-        grad_ref[:, (group + 1) * HEAD_SIZE :] = dv_acc[...].astype(BF16)
+        grad_ref[:, (group + 1) * HEAD_SIZE :] = dv_acc[:rows_all, :].astype(BF16)
 
         def finish(b, carry):
             rows = pl.ds(pl.multiple_of(b * BLOCK, BLOCK), BLOCK)
-            raw, gain_grad = raw_grad(dk_acc[rows, :], k_ref[rows, :], rows, query_heads + kv, gk_ref[...])
+            raw, gain_grad = raw_grad(dk_acc[rows, :], k_ref[rows, :], rows, group, gk_ref[...])
             grad_ref[rows, group * HEAD_SIZE : (group + 1) * HEAD_SIZE] = raw
             dgain_ref[1:2, :] += gain_grad
             return carry
@@ -521,31 +520,34 @@
     blocks = rows // BLOCK
     group = query_heads // key_heads
     wide = group * HEAD_SIZE
-    own = pl.BlockSpec((BLOCK, wide), lambda i, s: (i, 0))
-    whole = lambda shape: pl.BlockSpec(shape, lambda i, s: (0, 0))
+    own = pl.BlockSpec((1, BLOCK, wide), lambda h, i, s: (kv, i, 0))
+    whole = lambda shape: pl.BlockSpec(shape, lambda h, i, s: (0, 0), pipeline_mode=pl.Buffered(1))
     return pl.pallas_call(
-        functools.partial(backward_kernel, group, query_heads, kv, blocks, docs),
+        functools.partial(backward_kernel, group, blocks, docs),
         grid_spec=pltpu.PrefetchScalarGridSpec(
             num_scalar_prefetch=1,
-            grid=(blocks,),
+            grid=(1, blocks),
             in_specs=[
-                pl.BlockSpec((BLOCK, wide), lambda i, s: (i, kv)),
-                pl.BlockSpec((rows, HEAD_SIZE), lambda i, s: (0, query_heads + kv)),
-                pl.BlockSpec((rows, HEAD_SIZE), lambda i, s: (0, query_heads + key_heads + kv)),
+                *head_specs(rows, group, kv),
                 own,
-                own,
-                pl.BlockSpec((1, 8, group * BLOCK), lambda i, s: (i, 0, 0)),
+                pl.BlockSpec((BLOCK, wide), lambda h, i, s: (i, 0)),
+                pl.BlockSpec((1, 1, 8, group * BLOCK), lambda h, i, s: (kv, i, 0, 0)),
                 whole((rows, HEAD_SIZE)),
                 whole((rows, HEAD_SIZE)),
-                whole((rows, HEAD_SIZE)),
+                pl.BlockSpec((1, rows, HEAD_SIZE), lambda h, i, s: (kv, 0, 0), pipeline_mode=pl.Buffered(1)),
                 whole((1, HEAD_SIZE)),
                 whole((1, HEAD_SIZE)),
             ],
-            out_specs=[whole((rows, wide + 2 * HEAD_SIZE)), whole((8, HEAD_SIZE))],
+            out_specs=[
+                whole((rows, wide + 2 * HEAD_SIZE)),
+                pl.BlockSpec((8, HEAD_SIZE), lambda h, i, s: (0, 0)),
+            ],
             scratch_shapes=[
-                pltpu.VMEM((rows, HEAD_SIZE), F32),
-                pltpu.VMEM((rows, HEAD_SIZE), F32),
+                pltpu.VMEM((rows + STEP, HEAD_SIZE), F32),
+                pltpu.VMEM((rows + STEP, HEAD_SIZE), F32),
                 pltpu.VMEM((group * BLOCK, HEAD_SIZE), F32),
+                pltpu.VMEM((rows + STEP, HEAD_SIZE), BF16),
+                pltpu.VMEM((rows + STEP, HEAD_SIZE), BF16),
             ],
         ),
         out_shape=[
@@ -553,6 +555,7 @@
             jax.ShapeDtypeStruct((8, HEAD_SIZE), F32),
         ],
         compiler_params=pltpu.CompilerParams(vmem_limit_bytes=VMEM_LIMIT),
+        cost_estimate=pl.CostEstimate(flops=0, bytes_accessed=100_000_000, transcendentals=0),
         name="attention_backward",
     )(info, qkv, qkv, qkv, attended, grads, lse, cosine, sine, scales, gain_query, gain_key)
 
@@ -562,72 +565,184 @@
     return value.reshape(value.shape[0] * value.shape[2], value.shape[3])
 
 
-def output_kernel(a_ref, w_ref, tokens_ref, gain_ref, middle_ref, normed_ref):
-    r = pl.program_id(0)
-
-    @pl.when(r == 0)
-    def _():
-        middle_ref[...] = tokens_ref[...].astype(F32)
-
-    middle_ref[...] += dot_nt(a_ref[0], wide_block(w_ref))
-
-    @pl.when(r == pl.num_programs(0) - 1)
-    def _():
-        middle = middle_ref[...]
-        normed_ref[...] = (middle * row_scale(middle) * gain_ref[...]).astype(BF16)
-
-
-def output_project(mixed, weights, tokens, gain):
-    span, rows, cols = mixed.shape
-    devices, _, shard, _ = weights.shape
-    width = devices * shard
-    whole = lambda shape: pl.BlockSpec(shape, lambda r: (0, 0), pipeline_mode=pl.Buffered(1))
+def group_places(span):
+    half = span // 2
+    dp, t = lax.axis_index("dp"), lax.axis_index("tensor")
+    p, c = dp // 2, lax.rem(dp, 2)
+    aside = jnp.where(c == t // half, 0, 1)
+
+    def place(k):
+        return (p * 2 + (c ^ (k // half)), t ^ (k % half))
+
+    def chunk(k):
+        return ((k // half) ^ aside) * half + k % half
+
+    return place, chunk
+
+
+def group_barrier(span, place):
+    barrier = pltpu.get_barrier_semaphore()
+    for k in range(1, span):
+        pl.semaphore_signal(barrier, device_id=place(k), device_id_type=pl.DeviceIdType.MESH)
+    pl.semaphore_wait(barrier, span - 1)
+
+
+def remote_copy(src, dst, send_sem, recv_sem, to):
+    return pltpu.make_async_remote_copy(
+        src_ref=src,
+        dst_ref=dst,
+        send_sem=send_sem,
+        recv_sem=recv_sem,
+        device_id=to,
+        device_id_type=pl.DeviceIdType.MESH,
+    )
+
+
+def arrival_order(span):
+    half = span // 2
+    return [0, half] + [k for k in range(1, span) if k != half]
+
+
+def output_kernel(span, count, *refs):
+    heads = refs[:count]
+    w_hbm, tokens_ref, gain_ref, middle_ref, normed_ref, mixed_ref, w_ref, send_sems, recv_sems, local_sems = refs[count:]
+    place, chunk = group_places(span)
+    rows, width = tokens_ref.shape
+    wide = heads[0].shape[1]
+    load = pltpu.make_async_copy(w_hbm, w_ref, local_sems.at[count])
+    load.start()
+    group_barrier(span, place)
+    copies = {}
+    for h, ref in enumerate(heads):
+        to = pl.ds(h * wide, wide)
+        for k in range(1, span):
+            at = h * span + k
+            copies[h, k] = remote_copy(
+                ref.at[pl.ds(k * rows, rows)], mixed_ref.at[k, :, to], send_sems.at[at], recv_sems.at[at], place(k)
+            )
+            copies[h, k].start()
+        copies[h, 0] = pltpu.make_async_copy(ref.at[pl.ds(0, rows)], mixed_ref.at[0, :, to], local_sems.at[h])
+        copies[h, 0].start()
+    middle_ref[...] = tokens_ref[...].astype(F32)
+    load.wait()
+    piece = rows // 2
+    for k in arrival_order(span):
+        for h in range(count):
+            if k:
+                copies[h, k].wait_recv()
+            else:
+                copies[h, k].wait()
+        weights = w_ref[:, chunk(k)].reshape(width, w_ref.shape[3])
+
+        def step(m, carry, k=k, weights=weights):
+            at = pl.ds(pl.multiple_of(m * piece, piece), piece)
+            middle_ref[at, :] += dot_nt(mixed_ref[k, at, :], weights)
+            return carry
+
+        lax.fori_loop(0, rows // piece, step, 0)
+    middle = middle_ref[...]
+    normed_ref[...] = (middle * row_scale(middle) * gain_ref[...]).astype(BF16)
+    for k in range(1, span):
+        for h in range(count):
+            copies[h, k].wait_send()
+
+
+def output_project(heads, weights, tokens, gain):
+    devices, span, shard, cols = weights.shape
+    rows, width = tokens.shape
+    count = len(heads)
+    any_ref = pl.BlockSpec(memory_space=pl.ANY)
+    local_ref = pl.BlockSpec(memory_space=pltpu.VMEM)
     return pl.pallas_call(
-        output_kernel,
-        grid=(span,),
-        in_specs=[
-            pl.BlockSpec((1, rows, cols), lambda r: (r, 0, 0)),
-            pl.BlockSpec((devices, 1, shard, cols), lambda r: (0, r, 0, 0)),
-            whole((rows, width)),
-            whole((1, width)),
+        functools.partial(output_kernel, span, count),
+        in_specs=[any_ref] * (count + 1) + [local_ref] * 2,
+        out_specs=[local_ref] * 3,
+        out_shape=[
+            jax.ShapeDtypeStruct((rows, width), F32),
+            jax.ShapeDtypeStruct((rows, width), BF16),
+            jax.ShapeDtypeStruct((span, rows, cols), BF16),
         ],
-        out_specs=[whole((rows, width)), whole((rows, width))],
-        out_shape=[jax.ShapeDtypeStruct((rows, width), F32), jax.ShapeDtypeStruct((rows, width), BF16)],
-        compiler_params=pltpu.CompilerParams(vmem_limit_bytes=VMEM_LIMIT),
+        scratch_shapes=[
+            pltpu.VMEM(weights.shape, BF16),
+            pltpu.SemaphoreType.DMA((span * count,)),
+            pltpu.SemaphoreType.DMA((span * count,)),
+            pltpu.SemaphoreType.DMA((count + 1,)),
+        ],
+        compiler_params=pltpu.CompilerParams(
+            collective_id=1, has_side_effects=True, vmem_limit_bytes=VMEM_LIMIT
+        ),
+        cost_estimate=pl.CostEstimate(flops=0, bytes_accessed=100_000_000, transcendentals=0),
         name="output_project",
-    )(mixed, weights, tokens, gain)
-
-
-def output_back_kernel(b_ref, a_ref, w_ref, da_ref, dw_ref, bt_ref):
-    @pl.when(pl.program_id(0) == 0)
-    def _():
-        bt_ref[...] = b_ref[...].T
-
-    da_ref[0] = dot_nn(b_ref[...], wide_block(w_ref)).astype(BF16)
-    dw_ref[...] = dot_nn(bt_ref[...], a_ref[0]).astype(BF16).reshape(dw_ref.shape)
-
-
-def output_back(branch, mixed, weights):
-    span, rows, cols = mixed.shape
-    devices, _, shard, _ = weights.shape
-    width = devices * shard
-    chunk = pl.BlockSpec((1, rows, cols), lambda r: (r, 0, 0))
-    wide = pl.BlockSpec((devices, 1, shard, cols), lambda r: (0, r, 0, 0))
+    )(*heads, weights, tokens, gain)
+
+
+def output_back_kernel(span, count, b_ref, mixed_ref, w_hbm, *refs):
+    outs = refs[:count]
+    dw_hbm, w_ref, grad_ref, dw_ref, bt_ref, send_sems, recv_sems, local_sems = refs[count:]
+    place, chunk = group_places(span)
+    rows, width = b_ref.shape
+    wide = outs[0].shape[1]
+    cols = w_ref.shape[3]
+    load = pltpu.make_async_copy(w_hbm, w_ref, local_sems.at[0])
+    load.start()
+    group_barrier(span, place)
+    load.wait()
+    piece = rows // 2
+    copies = {}
+    for k in reversed(arrival_order(span)):
+        weights = w_ref[:, chunk(k)].reshape(width, cols)
+
+        def step(m, carry, k=k, weights=weights):
+            at = pl.ds(pl.multiple_of(m * piece, piece), piece)
+            grad_ref[k, at, :] = dot_nn(b_ref[at, :], weights).astype(BF16)
+            return carry
+
+        lax.fori_loop(0, rows // piece, step, 0)
+        for h, ref in enumerate(outs):
+            src, dst = grad_ref.at[k, :, pl.ds(h * wide, wide)], ref.at[pl.ds(k * rows, rows)]
+            at = h * span + k
+            if k:
+                copies[h, k] = remote_copy(src, dst, send_sems.at[at], recv_sems.at[at], place(k))
+            else:
+                copies[h, k] = pltpu.make_async_copy(src, dst, local_sems.at[1 + h])
+            copies[h, k].start()
+    bt_ref[...] = b_ref[...].T
+    stores = []
+    shard = w_ref.shape[2]
+    for k in range(span):
+        dw_ref[k] = dot_nn(bt_ref[...], mixed_ref[k]).astype(BF16).reshape(dw_ref.shape[1:])
+        stores.append(pltpu.make_async_copy(dw_ref.at[k], dw_hbm.at[:, chunk(k)], local_sems.at[1 + count + k]))
+        stores[-1].start()
+    for copy in stores:
+        copy.wait()
+    for key, copy in copies.items():
+        copy.wait()
+
+
+def output_back(branch, mixed, weights, count):
+    devices, span, shard, cols = weights.shape
+    rows, width = branch.shape
+    any_ref = pl.BlockSpec(memory_space=pl.ANY)
+    local_ref = pl.BlockSpec(memory_space=pltpu.VMEM)
     return pl.pallas_call(
-        output_back_kernel,
-        grid=(span,),
-        in_specs=[
-            pl.BlockSpec((rows, width), lambda r: (0, 0), pipeline_mode=pl.Buffered(1)),
-            chunk,
-            wide,
+        functools.partial(output_back_kernel, span, count),
+        in_specs=[local_ref, local_ref, any_ref],
+        out_specs=[any_ref] * (count + 1),
+        out_shape=[jax.ShapeDtypeStruct((span * rows, cols // count), BF16)] * count
+        + [jax.ShapeDtypeStruct(weights.shape, BF16)],
+        scratch_shapes=[
+            pltpu.VMEM(weights.shape, BF16),
+            pltpu.VMEM((span, rows, cols), BF16),
+            pltpu.VMEM((span, devices, shard, cols), BF16),
+            pltpu.VMEM((width, rows), BF16),
+            pltpu.SemaphoreType.DMA((span * count,)),
+            pltpu.SemaphoreType.DMA((span * count,)),
+            pltpu.SemaphoreType.DMA((1 + count + span,)),
         ],
-        out_specs=[chunk, wide],
-        scratch_shapes=[pltpu.VMEM((width, rows), BF16)],
-        out_shape=[
-            jax.ShapeDtypeStruct((span, rows, cols), BF16),
-            jax.ShapeDtypeStruct((devices, span, shard, cols), BF16),
-        ],
-        compiler_params=pltpu.CompilerParams(vmem_limit_bytes=VMEM_LIMIT),
+        compiler_params=pltpu.CompilerParams(
+            collective_id=2, has_side_effects=True, vmem_limit_bytes=VMEM_LIMIT
+        ),
+        cost_estimate=pl.CostEstimate(flops=0, bytes_accessed=100_000_000, transcendentals=0),
         name="output_back",
     )(branch, mixed, weights)
 
@@ -673,17 +788,17 @@
 
     lax.fori_loop(0, rows_all // chunk, rows_step, 0)
 
-    group = BLOCK // shard
+    group = ROWS // shard
 
     def grad_step(m, carry):
-        rows = pl.ds(pl.multiple_of(m * BLOCK, BLOCK), BLOCK)
+        rows = pl.ds(pl.multiple_of(m * ROWS, ROWS), ROWS)
         to = pl.ds(m * group, group)
         for k, left, right in ((0, xt_s, gg_s), (1, xt_s, ug_s), (2, ct_s, act_s)):
             value = dot_nn(left[rows, :], right[...]).astype(BF16)
             dw_ref[to, 0, :, k * hidden : (k + 1) * hidden] = value.reshape(group, shard, hidden)
         return carry
 
-    lax.fori_loop(0, width // BLOCK, grad_step, 0)
+    lax.fori_loop(0, width // ROWS, grad_step, 0)
 
     if not last:
         return
@@ -724,6 +839,322 @@
         compiler_params=pltpu.CompilerParams(vmem_limit_bytes=VMEM_LIMIT),
         name="feed_forward",
     )(x, cot, weights, *rest)
+
+
+def last_kernel(
+    pairs,
+    span,
+    count,
+    *refs,
+):
+    grads_hbm, sorted_hbm = refs[:count], refs[count : 2 * count]
+    last_body(pairs, span, grads_hbm, sorted_hbm, *refs[2 * count :])
+
+
+def last_body(
+    pairs,
+    span,
+    grads_hbm,
+    sorted_hbm,
+    normed_hbm,
+    w_ref,
+    middle_ref,
+    tokens_ref,
+    gain_ref,
+    gains_ref,
+    output_ref,
+    rows_out,
+    heads_out,
+    gains_out,
+    output_out,
+    grads,
+    sorted_s,
+    normed_s,
+    turned,
+    mine,
+    theirs,
+    from_sibling,
+    from_line,
+    heads_s,
+    heads_in,
+    far_in,
+    far_s,
+    near_in,
+    near_s,
+    final_s,
+    pass_s,
+    far_pass,
+    gains_one,
+    gains_two,
+    gains_s,
+    send_sems,
+    recv_sems,
+    local_sems,
+):
+    half = span // 2
+    dp, t = lax.axis_index("dp"), lax.axis_index("tensor")
+    p, c = dp // 2, lax.rem(dp, 2)
+    settled = c == t // half
+    rows, width = middle_ref.shape
+    shard = output_ref.shape[1]
+    place = lambda pp, cc, tt: (pp * 2 + cc, tt)
+    sibling = place(p, 1 - c, t)
+    used = [0]
+
+    def copy_to(src, dst, to):
+        used[0] += 1
+        at = used[0] - 1
+        return remote_copy(src, dst, send_sems.at[at], recv_sems.at[at], to)
+
+    count = len(grads_hbm)
+    wide = grads_hbm[0].shape[1]
+
+    def side_by_side(sources, rows_of, dst, sem):
+        return [
+            pltpu.make_async_copy(src.at[rows_of], dst.at[:, pl.ds(h * wide, wide)], local_sems.at[sem + h])
+            for h, src in enumerate(sources)
+        ]
+
+    loads = [side_by_side(grads_hbm, pl.ds(k * rows, rows), grads.at[k], k * count) for k in range(span)]
+    order = list(range(half, span)) + list(range(1, half)) + [0]
+    for k in order:
+        for load in loads[k]:
+            load.start()
+    more = [pltpu.make_async_copy(normed_hbm, normed_s, local_sems.at[span * count])]
+    more += side_by_side(sorted_hbm, pl.ds(0, span * rows), sorted_s, span * count + 1)
+    for load in more:
+        load.start()
+
+    barrier = pltpu.get_barrier_semaphore()
+    greeted = 0
+    for k in range(1, 2 * span):
+        pl.semaphore_signal(
+            barrier, device_id=place(p, c ^ (k // span), t ^ (k % span)), device_id_type=pl.DeviceIdType.MESH
+        )
+        greeted += 1
+    for k in range(1, pairs):
+        pl.semaphore_signal(barrier, device_id=place(p ^ k, c, t), device_id_type=pl.DeviceIdType.MESH)
+        greeted += 1
+    pl.semaphore_wait(barrier, greeted)
+
+    outputs = [copy_to(output_ref.at[r], output_out.at[r - 1], place(p, c, t ^ r)) for r in range(1, span)]
+
+    piece = rows // 2
+
+    def multiply(k, dst, slot):
+        def step(m, carry):
+            at = pl.ds(pl.multiple_of(m * piece, piece), piece)
+            dst[slot, at, :] = dot_nt(grads[k, at, :], w_ref[...]).astype(BF16)
+            return carry
+
+        lax.fori_loop(0, 2, step, 0)
+
+    sides = []
+    for k in range(half, span):
+        for load in loads[k]:
+            load.wait()
+        multiply(k, theirs, k - half)
+        sides.append(copy_to(theirs.at[k - half], from_sibling.at[k - half], sibling))
+        sides[-1].start()
+    for load in more:
+        load.wait()
+    turned[...] = normed_s[...].T
+    block = 2 * shard
+
+    def weights_step(m, carry):
+        at = pl.ds(pl.multiple_of(m * block, block), block)
+        heads_s[at, :] = dot_nn(turned[at, :], sorted_s[...]).astype(BF16)
+        return carry
+
+    lax.fori_loop(0, pairs, weights_step, 0)
+    heads_copies = []
+    for k in range(1, pairs):
+        there = pl.ds((p ^ k) * block, block)
+        heads_copies.append(copy_to(heads_s.at[there], heads_in.at[k - 1], place(p ^ k, c, t)))
+        heads_copies[-1].start()
+
+    hops = {}
+    for k in list(range(1, half)) + [0]:
+        for load in loads[k]:
+            load.wait()
+        multiply(k, mine, k)
+        sides[k].wait_recv()
+        mine[k] = (mine[k].astype(F32) + from_sibling[k].astype(F32)).astype(BF16)
+        if k:
+            for m in range(2):
+                at = pl.ds(m * piece, piece)
+                hops[k, m] = copy_to(mine.at[k, at], from_line.at[k - 1, at], place(p, c, t ^ k))
+                hops[k, m].start()
+    for copy in outputs:
+        copy.start()
+
+    for copy in heads_copies:
+        copy.wait_recv()
+    summed = heads_s[pl.ds(p * block, block), :].astype(F32)
+    for k in range(1, pairs):
+        summed = summed + heads_in[k - 1].astype(F32)
+    far_s[...] = summed.astype(BF16)
+    side = copy_to(far_s, far_pass, sibling)
+    far = copy_to(far_pass, far_in, place(p, 1 - c, lax.rem(t + half, span)))
+    near = copy_to(near_s, near_in, sibling)
+
+    @pl.when(jnp.logical_not(settled))
+    def _():
+        side.start()
+
+    swaps = []
+    gain_sum = jnp.zeros((1, width), F32)
+    for m in range(2):
+        at = pl.ds(m * piece, piece)
+        for k in range(1, half):
+            hops[k, m].wait_recv()
+        grad = mine[0, at, :].astype(F32)
+        for k in range(1, half):
+            grad = grad + from_line[k - 1, at, :].astype(F32)
+        inputs = tokens_ref[at, :].astype(F32)
+        r = row_scale(inputs)
+        unit = inputs * r
+        gain_sum = gain_sum + jnp.sum(grad * unit, axis=0, keepdims=True)
+        scaled = grad * gain_ref[...]
+        final_s[at, :] = (
+            middle_ref[at, :] + r * (scaled - unit * jnp.mean(scaled * unit, axis=-1, keepdims=True))
+        ).astype(BF16)
+        there = place(p, 1 - c, span - 1 - t)
+        swap = copy_to(final_s.at[at], rows_out.at[at] if m == 0 else pass_s, there if m == 0 else sibling)
+        keep = pltpu.make_async_copy(final_s.at[at], rows_out.at[at], local_sems.at[(span + 1) * count + 1 + m])
+        swaps.append((swap, keep))
+
+        @pl.when(settled)
+        def _():
+            keep.start()
+            if m == 0:
+                side.wait_recv()
+                far.start()
+
+        @pl.when(jnp.logical_not(settled))
+        def _():
+            swap.start()
+
+    gains_s[...] = gains_ref[...]
+    gains_s[0:1, :] = gain_sum
+    first_gains = [
+        copy_to(gains_s, gains_one.at[k - 1], place(p, c ^ (k // span), t ^ (k % span))) for k in range(1, 2 * span)
+    ]
+    for copy in first_gains:
+        copy.start()
+
+    at = pl.ds(piece, piece)
+    handed = swaps[1][0]
+    passed = copy_to(pass_s, rows_out.at[at], place(p, c, span - 1 - t))
+
+    @pl.when(settled)
+    def _():
+        handed.wait_recv()
+        passed.start()
+
+    for copy in first_gains:
+        copy.wait_recv()
+    total = gains_s[...]
+    for k in range(1, 2 * span):
+        total = total + gains_one[k - 1]
+    gains_out[...] = total
+    second_gains = [copy_to(gains_out, gains_two.at[k - 1], place(p ^ k, c, t)) for k in range(1, pairs)]
+    for copy in second_gains:
+        copy.start()
+
+    for copy in second_gains:
+        copy.wait()
+    for copy in first_gains:
+        copy.wait_send()
+    whole = gains_out[...]
+    for k in range(1, pairs):
+        whole = whole + gains_two[k - 1]
+    gains_out[...] = whole
+
+    @pl.when(settled)
+    def _():
+        far.wait_recv()
+        own = pl.ds(c * shard, shard)
+        other = pl.ds((1 - c) * shard, shard)
+        near_s[...] = (far_s[other, :].astype(F32) + far_in[other, :].astype(F32)).astype(BF16)
+        near.start()
+        far.wait_send()
+        heads_out[...] = far_s[own, :].astype(F32) + far_in[own, :].astype(F32)
+        near.wait_send()
+
+    @pl.when(jnp.logical_not(settled))
+    def _():
+        side.wait_send()
+        near.wait_recv()
+        heads_out[...] = near_in[...].astype(F32)
+
+    for copy in sides + list(hops.values()) + heads_copies:
+        copy.wait_send()
+    for copy in outputs:
+        copy.wait()
+    @pl.when(settled)
+    def _():
+        for swap, keep in swaps:
+            keep.wait()
+        passed.wait_send()
+
+    @pl.when(jnp.logical_not(settled))
+    def _():
+        for swap, keep in swaps:
+            swap.wait_send()
+        swaps[0][0].wait_recv()
+        passed.wait_recv()
+
+
+def last_transfers(pairs, span, grads, grads_sorted, normed, weights, middle_grad, tokens, gain, gains, output):
+    rows, width = tokens.shape
+    half = span // 2
+    shard = output.shape[1]
+    cols = weights.shape[1]
+    count = len(grads)
+    any_ref = pl.BlockSpec(memory_space=pl.ANY)
+    local_ref = pl.BlockSpec(memory_space=pltpu.VMEM)
+    copies = span - 1 + half + 2 * (half - 1) + 2 * (pairs - 1) + 2 + 2 * span - 1 + 4
+    return pl.pallas_call(
+        functools.partial(last_kernel, pairs, span, count),
+        in_specs=[any_ref] * (2 * count + 1) + [local_ref] * 5 + [any_ref],
+        out_specs=[any_ref, local_ref, local_ref, any_ref],
+        out_shape=[
+            jax.ShapeDtypeStruct((rows, width), BF16),
+            jax.ShapeDtypeStruct((shard, cols), F32),
+            jax.ShapeDtypeStruct((8, width), F32),
+            jax.ShapeDtypeStruct((span - 1, *output.shape[1:]), BF16),
+        ],
+        scratch_shapes=[
+            pltpu.VMEM((span, rows, cols), BF16),
+            pltpu.VMEM((span * rows, cols), BF16),
+            pltpu.VMEM((span * rows, width), BF16),
+            pltpu.VMEM((width, span * rows), BF16),
+            pltpu.VMEM((half, rows, width), BF16),
+            pltpu.VMEM((half, rows, width), BF16),
+            pltpu.VMEM((half, rows, width), BF16),
+            pltpu.VMEM((max(half - 1, 1), rows, width), BF16),
+            pltpu.VMEM((width, cols), BF16),
+            pltpu.VMEM((pairs - 1, 2 * shard, cols), BF16),
+            pltpu.VMEM((2 * shard, cols), BF16),
+            pltpu.VMEM((2 * shard, cols), BF16),
+            pltpu.VMEM((shard, cols), BF16),
+            pltpu.VMEM((shard, cols), BF16),
+            pltpu.VMEM((rows, width), BF16),
+            pltpu.VMEM((rows // 2, width), BF16),
+            pltpu.VMEM((2 * shard, cols), BF16),
+            pltpu.VMEM((2 * span - 1, 8, width), F32),
+            pltpu.VMEM((pairs - 1, 8, width), F32),
+            pltpu.VMEM((8, width), F32),
+            pltpu.SemaphoreType.DMA((copies,)),
+            pltpu.SemaphoreType.DMA((copies,)),
+            pltpu.SemaphoreType.DMA(((span + 1) * count + 3,)),
+        ],
+        compiler_params=pltpu.CompilerParams(
+            collective_id=3, has_side_effects=True, vmem_limit_bytes=VMEM_LIMIT
+        ),
+        name="last_transfers",
+    )(*grads, *grads_sorted, normed, weights, middle_grad, tokens, gain, gains, output)
 
 
 def local(
@@ -771,62 +1202,19 @@
                         moves.append(((pp * 2 + cc) * span + tt, (to[0] * 2 + to[1]) * span + to[2]))
         return lax.ppermute(x, AXES, moves)
 
-    def sibling(x):
-        return send(x, lambda pp, cc, tt: (pp, 1 - cc, tt))
-
     def swap(x):
         moved = send(x, lambda pp, cc, tt: (pp, 1 - cc, span - 1 - tt) if cc != tt // half else None)
         return jnp.where(settled, x, moved)
 
-    def ordered(mine, other, first):
-        return jnp.where(first, mine, other), jnp.where(first, other, mine)
-
-    def add(*terms):
-        total = terms[0].astype(F32)
-        for term in terms[1:]:
-            total = total + term.astype(F32)
-        return total.astype(BF16)
-
-    one_off = lambda pp, cc, tt: (pp ^ 1, cc, tt)
-    two_off = lambda pp, cc, tt: (pp ^ 2, cc, tt)
-
-    def scatter_start(take):
-        if pairs != 4:
-            return ()
-        cut = shard
-        return send(take(p ^ 3, 0, cut), one_off), send(take(p ^ 3, cut, cut), two_off)
-
-    def scatter_next(take, arrived):
-        if pairs != 4:
-            return ()
-        cut = shard
-        one = jnp.concatenate([take(p ^ 1, 0, cut), add(take(p ^ 1, cut, cut), arrived[1])], axis=0)
-        two = jnp.concatenate([add(take(p ^ 2, 0, cut), arrived[0]), take(p ^ 2, cut, cut)], axis=0)
-        return send(one, one_off), send(two, two_off)
-
-    def scatter_end(take, later):
-        size = 2 * shard
-        if pairs == 4:
-            return add(take(p, 0, size), *later)
-        pieces = [take(p ^ k, 0, size) for k in range(pairs)]
-        while len(pieces) > 1:
-            keep = len(pieces) // 2
-            moved = send(jnp.concatenate(pieces[keep:], axis=0), lambda pp, cc, tt: (pp ^ keep, cc, tt))
-            pieces = [add(pieces[k], moved[k * size : (k + 1) * size]) for k in range(keep)]
-        return pieces[0]
-
-    def taker(parts):
-        def take(at, shift, count):
-            rows_of = lambda x: lax.dynamic_slice(x, (at * 2 * shard + shift, 0), (count, x.shape[1]))
-            cols = [add(*[rows_of(x) for x in terms]) if len(terms) > 1 else rows_of(terms[0]) for terms in parts]
-            return jnp.concatenate(cols, axis=1) if len(cols) > 1 else cols[0]
-
-        return take
-
     never = row_order[0, 0] < 0
 
     def behind(x, other):
         return jnp.where(never, other[0, 0].astype(x.dtype), x)
+
+    def later(x, other):
+        at = (0,) * x.ndim
+        block = lax.slice(x, at, x.shape[:-2] and (1,) * (x.ndim - 2) + (8, 128) or (8, 128))
+        return lax.dynamic_update_slice(x, jnp.where(never, other[0, 0].astype(x.dtype), block), at)
 
     def line(x, steps):
         return [send(x, lambda pp, cc, tt: (pp, cc, tt ^ r)) for r in steps]
@@ -842,13 +1230,13 @@
         out = by_rows(lax.psum_scatter(out, "dp", scatter_dimension=0, tiled=True))
         return [out[r * shard : (r + 1) * shard] for r in range(count)]
 
-    def line_back(pieces, first):
-        return [
-            piece if r == 0 else send(piece, lambda pp, cc, tt: (pp, cc, tt ^ r))
-            for r, piece in enumerate(pieces, start=first)
-        ]
-
-    heads_local = by_rows(jnp.concatenate([query_weight, key_matrix, value_matrix], axis=1))
+    per_query, per_key = head_columns // key_heads, HEAD_SIZE
+    heads_local = []
+    for kv in range(key_heads):
+        heads_local.append(query_weight[:, kv * per_query : (kv + 1) * per_query])
+        heads_local.append(key_matrix[:, kv * per_key : (kv + 1) * per_key])
+        heads_local.append(value_matrix[:, kv * per_key : (kv + 1) * per_key])
+    heads_local = by_rows(jnp.concatenate(heads_local, axis=1))
     feed_local = by_rows(jnp.concatenate([gate_weight, up_weight, down_weight.T], axis=1))
     gains = jnp.concatenate([attention_gain, query_gain, key_gain, feedforward_gain])
     small, tiny = attention_gain.shape[0], query_gain.shape[0]
@@ -862,9 +1250,9 @@
     )
     swapped = tokens_all[0]
     tokens_all = tokens_all.reshape(group_rows, width)
-    feed_weights = [gather_wide([feed_local])]
+    own_weights = gather_wide([feed_local])
     output_weights = gather_wide([output_line[r] for r in range(span)])
-    feed_weights.append(gather_wide(line(behind(feed_local, swapped), range(1, span))))
+    feed_line = line(behind(feed_local, swapped), range(1, span))
 
     gains = gains.reshape(2 * pairs, 16, lanes)[:, 0, :few].astype(F32)
     gain_one = gains[:, :small].reshape(1, width)
@@ -903,48 +1291,33 @@
         tokens_sorted, gain_one, heads_weights, gain_query, gain_key, cosine, sine, query_heads, key_heads
     )
 
-    def exchange(parts):
-        out = [parts[0]]
-        for k in range(1, span):
-            out.append(send(parts[k], lambda pp, cc, tt: (pp, cc ^ (k // half), tt ^ (k % half))))
-        return out
-
-    def by_chunk(parts):
-        return [jnp.where(settled, parts[r], parts[(1 - r // half) * half + r % half]) for r in range(span)]
-
-    attended, lse, chunks = [], [], []
-    for kv in range(key_heads):
-        out, total = attention_forward(info, qkv, query_heads, key_heads, docs, kv)
-        attended.append(out)
-        lse.append(total)
-        out = jnp.take(out, places, axis=0, mode="clip")
-        chunks.append(by_chunk(exchange([out[k * rows : (k + 1) * rows] for k in range(span)])))
-    mixed = jnp.stack([jnp.concatenate([chunk[r] for chunk in chunks], axis=1) for r in range(span)])
+    line_weights = gather_wide([behind(piece, qkv) for piece in feed_line])
+
+    attended, lse = attention_forward(info, qkv, query_heads, key_heads, docs)
+    unsorted = [jnp.take(attended[kv], places, axis=0, mode="clip") for kv in range(key_heads)]
 
     hidden = gate_weight.shape[1]
-    middle, normed_two = output_project(mixed, output_weights, swapped, gain_two)
-    out, normed_grad, first_grad = feed(normed_two, cot_own, feed_weights[0])
-    result, middle_grad, branch, gain_two_grad, second_grad = feed(
-        normed_two, cot_own, feed_weights[1], out, normed_grad, middle, gain_two
+    middle, normed_two, mixed = output_project(unsorted, output_weights, swapped, gain_two)
+    out, normed_grad, line_grad = feed(normed_two, cot_own, line_weights)
+    result, middle_grad, branch, gain_two_grad, own_grad = feed(
+        normed_two, cot_own, own_weights, out, normed_grad, middle, gain_two
     )
-    feed_back = line_back(scatter_wide(first_grad), 0) + line_back(scatter_wide(second_grad), 1)
-
-    mixed_grad, output_grad = output_back(branch, mixed, output_weights)
-    merged = by_chunk([mixed_grad[r] for r in range(span)])
-    per_head = head_columns // key_heads
-    grad_chunks = [exchange([x[:, kv * per_head : (kv + 1) * per_head] for x in merged]) for kv in range(key_heads)]
-    output_sum = line_back(scatter_wide(output_grad), 0)
+    line_sum = scatter_wide(line_grad)
+
+    *head_rows, output_grad = output_back(branch, mixed, output_weights, key_heads)
     layer_output = swap(result)
 
     head_grads, head_gains = [], 0.0
     for kv in range(key_heads):
-        attended_grad = jnp.take(jnp.concatenate(grad_chunks[kv], axis=0), inverse, axis=0, mode="clip")
+        attended_grad = jnp.take(head_rows[kv], inverse, axis=0, mode="clip")
+        if kv > 0:
+            attended_grad = behind(attended_grad, grads)
         grads, gains_of = attention_backward(
             info,
             qkv,
-            attended[kv],
+            attended,
             attended_grad,
-            lse[kv],
+            lse,
             cosine,
             sine,
             scales,
@@ -955,67 +1328,61 @@
             docs,
             kv,
         )
+        if kv == 0:
+            output_sum = scatter_wide(later(later(output_grad, line_sum[0]), grads))
+            own_sum = scatter_wide(later(own_grad, grads))
+            line_in = [
+                send(piece, lambda pp, cc, tt: (pp, cc, tt ^ r)) for r, piece in enumerate(line_sum, start=1)
+            ]
         head_grads.append(grads)
         head_gains = head_gains + gains_of
-    wide_q, wide_k = head_columns // key_heads, HEAD_SIZE
-    qkv_grad = jnp.concatenate(
-        [g[:, :wide_q] for g in head_grads]
-        + [g[:, wide_q : wide_q + wide_k] for g in head_grads]
-        + [g[:, wide_q + wide_k :] for g in head_grads],
-        axis=1,
+    qkv_rows = [jnp.take(grads, places, axis=0, mode="clip") for grads in head_grads]
+    gain_rows = jnp.concatenate(
+        [
+            jnp.zeros((1, width), F32),
+            gain_two_grad[:1],
+            jnp.pad(head_gains[:2].reshape(1, 2 * HEAD_SIZE), ((0, 0), (0, width - 2 * HEAD_SIZE))),
+            jnp.zeros((5, width), F32),
+        ]
     )
-    partial = dot_nt(jnp.take(qkv_grad, places, axis=0, mode="clip"), heads_weights).astype(BF16)
-    parts = [partial[k * rows : (k + 1) * rows] for k in range(span)]
-    moved = sibling(jnp.concatenate(parts[half:], axis=0))
-    heads_grad = dot_tn(normed, qkv_grad).astype(BF16)
-    heads = taker([(heads_grad,)])
-    parts = [add(parts[k], moved[k * rows : (k + 1) * rows]) for k in range(half)]
-    heads_arrived = scatter_start(heads)
-    while len(parts) > 1:
-        keep = len(parts) // 2
-        moved = send(jnp.concatenate(parts[keep:], axis=0), lambda pp, cc, tt: (pp, cc, tt ^ keep))
-        parts = [add(parts[k], moved[k * rows : (k + 1) * rows]) for k in range(keep)]
-    heads_later = scatter_next(heads, heads_arrived)
-    mine = scatter_end(heads, heads_later)
-    moved = send(mine, lambda pp, cc, tt: (pp, cc, (tt + half) % span) if cc != tt // half else None)
-
-    normed_grad = parts[0].astype(F32)
-    inputs = swapped.astype(F32)
-    r_one = row_scale(inputs)
-    unit_one = inputs * r_one
-    gain_one_grad = jnp.sum(normed_grad * unit_one, axis=0)
-    scaled = normed_grad * gain_one
-    input_grad = swap(
-        (middle_grad + r_one * (scaled - unit_one * jnp.mean(scaled * unit_one, axis=-1, keepdims=True))).astype(BF16)
+    input_grad, heads_sum, gain_sums, output_in = last_transfers(
+        pairs,
+        span,
+        qkv_rows,
+        head_grads,
+        normed,
+        heads_weights,
+        middle_grad,
+        swapped,
+        gain_one,
+        gain_rows,
+        jnp.stack(output_sum),
     )
 
-    summed = mine.astype(F32) + moved.astype(F32)
-    top, bottom = summed[:shard], summed[shard:]
-    other = jnp.where(c == 0, bottom, top).astype(BF16)
-    moved = send(other, lambda pp, cc, tt: (pp, 1 - cc, tt) if cc == tt // half else None).astype(F32)
-    summed = jnp.where(settled, jnp.where(c == 0, top, bottom), moved)
-    key_columns = key_heads * HEAD_SIZE
-
-    def total(pieces):
-        out = pieces[0].astype(F32)
-        for piece in pieces[1:]:
-            out = out + piece.astype(F32)
+    def total(first, others):
+        out = first.astype(F32)
+        for other in others:
+            out = out + other.astype(F32)
         return out
 
-    wide_sum, output_sum = total(feed_back), total(output_sum)
-    gain_sums = lax.psum(jnp.concatenate([gain_one_grad, head_gains[0], head_gains[1], gain_two_grad[0]]), AXES)
-    cut = lambda at, size: lax.dynamic_slice(gain_sums, (at + dp * size,), (size,))
+    wide_sum = total(own_sum[0], line_in)
+    output_sum = total(output_sum[0], [output_in[k] for k in range(span - 1)])
+    stride = per_query + 2 * per_key
+    columns = lambda at, size: jnp.concatenate(
+        [heads_sum[:, kv * stride + at : kv * stride + at + size] for kv in range(key_heads)], axis=1
+    )
+    cut = lambda row, at, size: lax.dynamic_slice(gain_sums[row], (at + dp * size,), (size,))
     return (
         layer_output,
         input_grad,
-        cut(0, small),
-        cut(width, tiny),
-        cut(width + HEAD_SIZE, tiny),
-        summed[:, :head_columns],
-        summed[:, head_columns : head_columns + key_columns],
-        summed[:, head_columns + key_columns :],
+        cut(0, 0, small),
+        cut(2, 0, tiny),
+        cut(2, HEAD_SIZE, tiny),
+        columns(0, per_query),
+        columns(per_query, per_key),
+        columns(per_query + per_key, per_key),
         output_sum.T,
-        cut(width + 2 * HEAD_SIZE, small),
+        cut(1, 0, small),
         wide_sum[:, :hidden],
         wide_sum[:, hidden : 2 * hidden],
         wide_sum[:, 2 * hidden :].T,

time: 749 us -> 624 us (0.83)
  waiting for transfers between devices: 195 us -> 20.5 us
  Pallas kernels: 279 us -> 405 us
  blocking collectives: 48 us -> 0 us
  starting transfers between devices: 42.6 us -> 24 us
  matrix products: 17.7 us -> 0 us
    ppermute x32 -> x8, waiting for transfers between devices: 195 us -> 13.9 us  [send(): return lax.ppermute(x, AXES, moves)]
    pallas_call x4 -> x5, Pallas kernels: 92.9 us -> 232 us  [the longest x1 94.5 us: last_transfers(): pl.pallas_call(functools.partial(last_kernel, pairs, span, count), in_spe...]
    psum x1 -> x0, blocking collectives: 48 us -> none  [local(): lax.psum(jnp.concatenate([gain_one_grad, head_gains[0], head_gains[1], ga...]
    ppermute x32 -> x8, starting transfers between devices: 42.3 us -> 12.6 us  [send(): return lax.ppermute(x, AXES, moves)]
    dot_general x2 -> x0, matrix products: 17.7 us -> none  [the longest x1 9.13 us: dot_tn(): lax.dot_general(left, right, (((0,), (0,)), ((), ())), preferred_element_...]
    pallas_call x2 -> x1, Pallas kernels: 42.6 us -> 25.3 us  [attention_forward(): pl.pallas_call(functools.partial(forward_kernel, group, blocks, docs), gr...]
    reduce_scatter x3, starting transfers between devices: 0.12 us -> 11.3 us  [scatter_wide(): out = by_rows(lax.psum_scatter(out, 'dp', scatter_dimension=0, tiled=True))]
    gather x5 -> x6, local copies, waits for them, and re-layouts: 46.1 us -> 51.5 us  [the longest x2 18.9 us: local(): jnp.take(grads, places, axis=0, mode='clip')]
  transfers between devices with their start and end apart: 38 -> 14, of which waited for: 16 -> 2; matrix products, arithmetic and copies ran while one was open for 20% -> 20% of each run, Pallas kernels for 21% -> 40%
where the time goes in v3:
time: 624 us; the launch traced here: 613 us
  Pallas kernels  405 us (65%)
  local copies, waits for them, and re-layouts  106 us (17%)
  other arithmetic  40.9 us (7%)
  starting transfers between devices  24 us (4%)
  waiting for transfers between devices  20.5 us (3%)
  between operations  15.5 us (2%)
    pallas_call x1, Pallas kernels, last_transfers(): pl.pallas_call(functools.partial(last_kernel, pairs, span, count), in_spe...  94.5 us
    pallas_call x2, Pallas kernels, feed(): pl.pallas_call(functools.partial(feed_kernel, last), grid=(span,), in_spe...  66.3 us
    pallas_call x1, Pallas kernels, first_transfers(): pl.pallas_call(functools.partial(first_kernel, pairs, span), in_specs=[an...  65.8 us
    pallas_call x2, Pallas kernels, attention_backward(): pl.pallas_call(functools.partial(backward_kernel, group, blocks, docs), g...  64.8 us
    pallas_call x1, Pallas kernels, output_project(): pl.pallas_call(functools.partial(output_kernel, span, count), in_specs=[a...  36.6 us
    pallas_call x1, Pallas kernels, output_back(): pl.pallas_call(functools.partial(output_back_kernel, span, count), in_spe...  36.4 us
    pallas_call x1, Pallas kernels, attention_forward(): pl.pallas_call(functools.partial(forward_kernel, group, blocks, docs), gr...  25.3 us
    gather x2, local copies, waits for them, and re-layouts, local(): jnp.take(grads, places, axis=0, mode='clip')  18.9 us
  transfers between devices with their start and end apart: 14, of which 2 were waited for; matrix products, arithmetic and copies ran while one was open for 20% of the time, Pallas kernels for 40%

profile of v3, /device:TPU:0, one launch (start us, length us, event | category | flops | bytes accessed | tf_op | source)
XLA Modules:
  0.0 612.9 jit_solution(6346223216780094561)
XLA Ops:
  17.2 65.8 %first_transfers.1 = (bf16[4,640,1024]{2,1,0:T(8,128)(2,1)}, bf16[1024,1024]{1,0:T(8,128)(2,1)}, bf16[4,128,512]{2,1,0:T(8,128)(2,1)}, bf16[128,384]{1,0:T(8,128)(2,1)}, s32[24,128]{1,0:T(8,128)}) custom-call(bf16[640,1024]{1,0:T(8,128)(2,1)} %tokens_ref.1, bf16[128,1024]{1,0:T(8,128)(2,1)} %copy-done.7, bf16[128,512]{1,0:T(8,128)(2,1)} %bitcast.85, ...), custom_call_target="tpu_custom_call" | custom-call | bytes 150000000 | tf_op jit(solution)/shard_map/first_transfers/pallas_call | solution.py:249
  92.3 3.8 collective-permute-start.1
  98.3 5.7 sort.17
  104.0 16.0 %gather_fusion = bf16[2560,1024]{1,0:T(8,128)(2,1)} fusion(bf16[2560,1024]{1,0:T(8,128)(2,1)} %bitcast.77, s32[3072]{0:T(1024)S(1)} %pad_clamp_fusion.1), kind=kCustom, calls=%fused_computation | custom fusion | bytes 10496000 | tf_op jit(solution)/shard_map/jit(_take)/gather | solution.py:1288
  120.3 4.6 fusion
  127.8 15.5 %project.1 = (bf16[2560,1024]{1,0:T(8,128)(2,1)}, bf16[2560,1024]{1,0:T(8,128)(2,1)}, f32[2,2560,128]{2,1,0:T(8,128)}) custom-call(bf16[2560,1024]{1,0:T(8,128)(2,1)} %gather_fusion, f32[1,1024]{1,0:T(1,128)} %bitcast.89, bf16[1024,1024]{1,0:T(8,128)(2,1)} %get-tuple-element.50.w_ref.refs_5_, f32[1,128]{1,0:T(1,128)} %reshape.119.gq_ref, ...), custom_call_target="tpu_custom_call" | custom-call | tf_op jit(solution)/shard_map/project/pallas_call | solution.py:302
  151.5 25.3 %attention_forward.1 = (bf16[2,2560,256]{2,1,0:T(8,128)(2,1)}, f32[2,5,8,1024]{3,2,1,0:T(8,128)}) custom-call(s32[12]{0:T(128)} %pad_add_fusion.2.info_ref, bf16[2560,1024]{1,0:T(8,128)(2,1)} %get-tuple-element.51.q_ref.k_ref.v_ref, bf16[2560,1024]{1,0:T(8,128)(2,1)} %get-tuple-element.51.q_ref.k_ref.v_ref, ...), custom_call_target="tpu_custom_call" | custom-call | bytes 100000000 | tf_op jit(solution)/shard_map/attention_forward/pallas_call | solution.py:397
  178.7 8.1 %gather_fusion.2 = bf16[2560,256]{1,0:T(8,128)(2,1)} fusion(bf16[2560,256]{1,0:T(8,128)(2,1)S(1)} %get-tuple-element.111, s32[3072]{0:T(1024)S(1)} %pad_clamp_fusion), kind=kCustom, calls=%fused_computation.2 | custom fusion | bytes 2631680 | tf_op jit(solution)/shard_map/jit(_take)/gather | solution.py:1297
  186.8 8.1 %gather_fusion.1 = bf16[2560,256]{1,0:T(8,128)(2,1)} fusion(bf16[2560,256]{1,0:T(8,128)(2,1)S(1)} %get-tuple-element.112, s32[3072]{0:T(1024)S(1)} %pad_clamp_fusion), kind=kCustom, calls=%fused_computation.1 | custom fusion | bytes 2631680 | tf_op jit(solution)/shard_map/jit(_take)/gather | solution.py:1297
  197.5 36.6 %output_project.1 = (f32[640,1024]{1,0:T(8,128)}, bf16[640,1024]{1,0:T(8,128)(2,1)}, bf16[4,640,512]{2,1,0:T(8,128)(2,1)}) custom-call(bf16[2560,256]{1,0:T(8,128)(2,1)} %gather_fusion.1, bf16[2560,256]{1,0:T(8,128)(2,1)} %gather_fusion.2, bf16[8,4,128,512]{3,2,1,0:T(8,128)(2,1)} %bitcast.79, bf16[640,1024]{1,0:T(8,128)(2,1)} %copy-done.2, f32[1,1024]{1,0:T(1,128)} %bitcast.87), custom_call_target="tpu_custom_call" | custom-call | bytes 100000000 | tf_op jit(solution)/shard_map/output_project/pallas_call | solution.py:656
  234.2 40.9 %feed_forward.2 = (f32[640,1024]{1,0:T(8,128)}, f32[640,1024]{1,0:T(8,128)}, bf16[8,3,128,2304]{3,2,1,0:T(8,128)(2,1)}) custom-call(bf16[640,1024]{1,0:T(8,128)(2,1)} %get-tuple-element.54.x_ref, bf16[640,1024]{1,0:T(8,128)(2,1)} %broadcast_select_fusion.2.c_ref, bf16[8,3,128,2304]{3,2,1,0:T(8,128)(2,1)} %bitcast.82), custom_call_target="tpu_custom_call" | custom-call | tf_op jit(solution)/shard_map/feed_forward/pallas_call | solution.py:830
  275.2 11.3 %reduce-scatter.8.cloned.1.call-start = ((), (), s32[]{:S(2)}) async-start(), calls=%async_computation.8 | async-start | bytes 5308416 | tf_op jit(solution)/shard_map/reduce_scatter | solution.py:1230
  286.4 25.4 %feed_forward.3 = (bf16[640,1024]{1,0:T(8,128)(2,1)}, f32[640,1024]{1,0:T(8,128)}, bf16[640,1024]{1,0:T(8,128)(2,1)}, f32[8,1024]{1,0:T(8,128)}, bf16[8,1,128,2304]{3,2,1,0:T(8,128)(2,1)}) custom-call(bf16[640,1024]{1,0:T(8,128)(2,1)} %get-tuple-element.54.x_ref, bf16[640,1024]{1,0:T(8,128)(2,1)} %broadcast_select_fusion.2.c_ref, ...), custom_call_target="tpu_custom_call" | custom-call | tf_op jit(solution)/shard_map/feed_forward/pallas_call | solution.py:830
  311.8 36.4 %output_back.1 = (bf16[2560,256]{1,0:T(8,128)(2,1)}, bf16[2560,256]{1,0:T(8,128)(2,1)}, bf16[8,4,128,512]{3,2,1,0:T(8,128)(2,1)}) custom-call(bf16[640,1024]{1,0:T(8,128)(2,1)} %get-tuple-element.59.b_ref, bf16[4,640,512]{2,1,0:T(8,128)(2,1)} %get-tuple-element.60.mixed_ref, bf16[8,4,128,512]{3,2,1,0:T(8,128)(2,1)} %bitcast.80), custom_call_target="tpu_custom_call" | custom-call | bytes 100000000 | tf_op jit(solution)/shard_map/output_back/pallas_call | solution.py:727
  348.2 8.3 %gather_fusion.3 = bf16[2560,256]{1,0:T(8,128)(2,1)} fusion(bf16[2560,256]{1,0:T(8,128)(2,1)} %get-tuple-element.61, s32[3072]{0:T(1024)S(1)} %pad_clamp_fusion.1), kind=kCustom, calls=%fused_computation.3 | custom fusion | bytes 2631680 | tf_op jit(solution)/shard_map/jit(_take)/gather | solution.py:1312
  356.5 32.3 %attention_backward.2 = (bf16[2560,512]{1,0:T(8,128)(2,1)}, f32[8,128]{1,0:T(8,128)}) custom-call(s32[12]{0:T(128)} %pad_add_fusion.2.info_ref, bf16[2560,1024]{1,0:T(8,128)(2,1)} %get-tuple-element.51.q_ref.k_ref.v_ref, bf16[2560,1024]{1,0:T(8,128)(2,1)} %get-tuple-element.51.q_ref.k_ref.v_ref, bf16[2560,1024]{1,0:T(8,128)(2,1)} %get-tuple-element.51.q_ref.k_ref.v_ref, ...), custom_call_target="tpu_custom_call" | custom-call | bytes 100000000 | tf_op jit(solution)/shard_map/attention_backward/pallas_call | solution.py:525
  391.9 4.6 copy.47
  403.6 8.1 %gather_fusion.5 = bf16[2560,256]{1,0:T(8,128)(2,1)} fusion(bf16[2560,256]{1,0:T(8,128)(2,1)S(1)} %copy-done.1, s32[3072]{0:T(1024)S(1)} %pad_clamp_fusion.1), kind=kCustom, calls=%fused_computation.5 | custom fusion | bytes 2631680 | tf_op jit(solution)/shard_map/jit(_take)/gather | solution.py:1312
  421.2 8.4 %gather_fusion.4 = bf16[2560,512]{1,0:T(8,128)(2,1)} fusion(bf16[2560,512]{1,0:T(8,128)(2,1)S(1)} %copy-done, s32[3072]{0:T(1024)S(1)} %pad_clamp_fusion), kind=kCustom, calls=%fused_computation.4 | custom fusion | bytes 5253120 | tf_op jit(solution)/shard_map/jit(_take)/gather | solution.py:1339
  429.6 32.5 %attention_backward.3 = (bf16[2560,512]{1,0:T(8,128)(2,1)}, f32[8,128]{1,0:T(8,128)}) custom-call(s32[12]{0:T(128)} %pad_add_fusion.2.info_ref, bf16[2560,1024]{1,0:T(8,128)(2,1)} %get-tuple-element.51.q_ref.k_ref.v_ref, bf16[2560,1024]{1,0:T(8,128)(2,1)} %get-tuple-element.51.q_ref.k_ref.v_ref, bf16[2560,1024]{1,0:T(8,128)(2,1)} %get-tuple-element.51.q_ref.k_ref.v_ref, ...), custom_call_target="tpu_custom_call" | custom-call | bytes 100000000 | tf_op jit(solution)/shard_map/attention_backward/pallas_call | solution.py:525
  463.5 10.5 %gather_fusion.6 = bf16[2560,512]{1,0:T(8,128)(2,1)} fusion(bf16[2560,512]{1,0:T(8,128)(2,1)} %get-tuple-element.66.refs_3_, s32[3072]{0:T(1024)S(1)} %pad_clamp_fusion), kind=kCustom, calls=%fused_computation.6 | custom fusion | bytes 5253120 | tf_op jit(solution)/shard_map/jit(_take)/gather | solution.py:1339
  475.9 13.9 %collective-permute-done.6 = bf16[128,2304]{1,0:T(8,128)(2,1)} collective-permute-done((bf16[128,2304]{1,0:T(8,128)(2,1)}, bf16[128,2304]{1,0:T(8,128)(2,1)}, u32[]{:S(2)}, u32[]{:S(2)}) %collective-permute-start.6) | collective-permute-done | bytes 589856 | tf_op jit(solution)/shard_map/ppermute | solution.py:1203
  493.7 5.8 reduce-scatter.6.cloned.1.call-done
  501.5 94.5 %last_transfers.1 = (bf16[640,1024]{1,0:T(8,128)(2,1)}, f32[128,1024]{1,0:T(8,128)}, f32[8,1024]{1,0:T(8,128)}, bf16[3,128,512]{2,1,0:T(8,128)(2,1)}) custom-call(bf16[2560,512]{1,0:T(8,128)(2,1)} %gather_fusion.4, bf16[2560,512]{1,0:T(8,128)(2,1)} %gather_fusion.6, bf16[2560,512]{1,0:T(8,128)(2,1)} %get-tuple-element.64.refs_2_, ...), custom_call_target="tpu_custom_call" | custom-call | tf_op jit(solution)/shard_map/last_transfers/pallas_call | solution.py:1118
  (141 shorter events, 74.7 us)
Async XLA Ops:
  7.2 190.3 %all-gather.4.cloned.1.call-start = ((), (), s32[]{:S(2)}) async-start(), calls=%async_computation.3 | async-start | bytes 4718592 | tf_op jit(solution)/shard_map/all_gather | solution.py:1224
  14.0 3.2 copy-start.7
  85.0 149.2 %all-gather.8.cloned.1.call-start = ((), (), s32[]{:S(2)}) async-start(), calls=%async_computation.5 | async-start | bytes 15925248 | tf_op jit(solution)/shard_map/all_gather | solution.py:1224
  86.2 3.1 copy-start.11
  86.2 3.9 copy-start.9
  86.2 3.9 copy-start.10
  88.8 7.3 %copy-start.12 = (s32[24,128]{1,0:T(8,128)S(1)}, s32[24,128]{1,0:T(8,128)}, u32[]{:S(2)}) copy-start(s32[24,128]{1,0:T(8,128)} %get-tuple-element.46) | copy-start | bytes 36868
  91.7 52.8 %collective-permute-start.3 = (bf16[128,2304]{1,0:T(8,128)(2,1)S(1)}, bf16[128,2304]{1,0:T(8,128)(2,1)S(1)}, u32[]{:S(2)}, u32[]{:S(2)}) collective-permute-start(bf16[128,2304]{1,0:T(8,128)(2,1)S(1)} %get-tuple-element.119), channel_id=1, source_target_pairs={{0,3},{1,2},{2,1},{3,0},{4,7},{5,6},{6,5},{7,4},{8,11},{9,10},{10,... | collective-permute-start | bytes 1769480 | tf_op jit(solution)/shard_map/ppermute | solution.py:1203
  91.7 53.5 %collective-permute-start.2 = (bf16[128,2304]{1,0:T(8,128)(2,1)S(1)}, bf16[128,2304]{1,0:T(8,128)(2,1)S(1)}, u32[]{:S(2)}, u32[]{:S(2)}) collective-permute-start(bf16[128,2304]{1,0:T(8,128)(2,1)S(1)} %get-tuple-element.119), channel_id=1, source_target_pairs={{0,2},{1,3},{2,0},{3,1},{4,6},{5,7},{6,4},{7,5},{8,10},{9,11},{10,... | collective-permute-start | bytes 1769480 | tf_op jit(solution)/shard_map/ppermute | solution.py:1203
  92.3 53.6 %collective-permute-start.1 = (bf16[128,2304]{1,0:T(8,128)(2,1)S(1)}, bf16[128,2304]{1,0:T(8,128)(2,1)S(1)}, u32[]{:S(2)}, u32[]{:S(2)}) collective-permute-start(bf16[128,2304]{1,0:T(8,128)(2,1)S(1)} %get-tuple-element.119), channel_id=1, source_target_pairs={{0,1},{1,0},{2,3},{3,2},{4,5},{5,4},{6,7},{7,6},{8,9},{9,8},{10,11... | collective-permute-start | bytes 1769480 | tf_op jit(solution)/shard_map/ppermute | solution.py:1203
  148.0 138.4 %all-gather.6.cloned.1.call-start = ((), (), s32[]{:S(2)}) async-start(), calls=%async_computation.4 | async-start | bytes 5308416 | tf_op jit(solution)/shard_map/all_gather | solution.py:1224
  148.7 247.9 %reduce-scatter.4.cloned.1.call-start = ((), (), s32[]{:S(2)}) async-start(), calls=%async_computation.6 | async-start | bytes 15925248 | tf_op jit(solution)/shard_map/reduce_scatter | solution.py:1230
  148.8 46.2 %collective-permute-start = (bf16[640,1024]{1,0:T(8,128)(2,1)}, bf16[640,1024]{1,0:T(8,128)(2,1)}, u32[]{:S(2)}, u32[]{:S(2)}) collective-permute-start(bf16[640,1024]{1,0:T(8,128)(2,1)} %param.29), channel_id=1, source_target_pairs={{2,5},{3,4},{4,3},{5,2},{10,13},{11,12},{12,11},{13,10},{18,21},{1... | collective-permute-start | bytes 3932168 | tf_op jit(solution)/shard_map/ppermute | solution.py:1203
  275.2 200.8 %reduce-scatter.8.cloned.1.call-start = ((), (), s32[]{:S(2)}) async-start(), calls=%async_computation.8 | async-start | bytes 5308416 | tf_op jit(solution)/shard_map/reduce_scatter | solution.py:1230
  391.9 107.6 %reduce-scatter.6.cloned.1.call-start = ((), (), s32[]{:S(2)}) async-start(), calls=%async_computation.7 | async-start | bytes 4718592 | tf_op jit(solution)/shard_map/reduce_scatter | solution.py:1230
  403.6 10.0 %copy-start.4 = (bf16[384,2304]{1,0:T(8,128)(2,1)S(1)}, bf16[384,2304]{1,0:T(8,128)(2,1)}, u32[]{:S(2)}) copy-start(bf16[384,2304]{1,0:T(8,128)(2,1)} %reduce-scatter.4.cloned.1.call-done) | copy-start | bytes 5308420
  411.8 7.5 %copy-start.3 = (bf16[2560,256]{1,0:T(8,128)(2,1)S(1)}, bf16[2560,256]{1,0:T(8,128)(2,1)}, u32[]{:S(2)}) copy-start(bf16[2560,256]{1,0:T(8,128)(2,1)} %gather_fusion.5) | copy-start | bytes 3932164
  411.8 62.9 %collective-permute-start.4 = (bf16[640,1024]{1,0:T(8,128)(2,1)}, bf16[640,1024]{1,0:T(8,128)(2,1)}, u32[]{:S(2)}, u32[]{:S(2)}) collective-permute-start(bf16[640,1024]{1,0:T(8,128)(2,1)} %get-tuple-element.58), channel_id=1, source_target_pairs={{2,5},{3,4},{4,3},{5,2},{10,13},{11,12},{12,11},{13,10},{18,21},{1... | collective-permute-start | bytes 3932168 | tf_op jit(solution)/shard_map/ppermute | solution.py:1203
  414.9 61.1 %collective-permute-start.5 = (bf16[128,2304]{1,0:T(8,128)(2,1)}, bf16[128,2304]{1,0:T(8,128)(2,1)S(1)}, u32[]{:S(2)}, u32[]{:S(2)}) collective-permute-start(bf16[128,2304]{1,0:T(8,128)(2,1)} %get-tuple-element.113), channel_id=1, source_target_pairs={{0,1},{1,0},{2,3},{3,2},{4,5},{5,4},{6,7},{7,6},{8,9},{9,8},{10,11... | collective-permute-start | bytes 1769480 | tf_op jit(solution)/shard_map/ppermute | solution.py:1203
  415.8 74.0 %collective-permute-start.6 = (bf16[128,2304]{1,0:T(8,128)(2,1)}, bf16[128,2304]{1,0:T(8,128)(2,1)}, u32[]{:S(2)}, u32[]{:S(2)}) collective-permute-start(bf16[128,2304]{1,0:T(8,128)(2,1)} %get-tuple-element.114), channel_id=1, source_target_pairs={{0,2},{1,3},{2,0},{3,1},{4,6},{5,7},{6,4},{7,5},{8,10},{9,11},{10,... | collective-permute-start | bytes 1769480 | tf_op jit(solution)/shard_map/ppermute | solution.py:1203
  419.0 70.8 %collective-permute-start.7 = (bf16[128,2304]{1,0:T(8,128)(2,1)}, bf16[128,2304]{1,0:T(8,128)(2,1)}, u32[]{:S(2)}, u32[]{:S(2)}) collective-permute-start(bf16[128,2304]{1,0:T(8,128)(2,1)} %get-tuple-element.115), channel_id=1, source_target_pairs={{0,3},{1,2},{2,1},{3,0},{4,7},{5,6},{6,5},{7,4},{8,11},{9,10},{10,... | collective-permute-start | bytes 1769480 | tf_op jit(solution)/shard_map/ppermute | solution.py:1203
  429.6 32.5 %copy-start.13 = (f32[8,128]{1,0:T(8,128)S(1)}, f32[8,128]{1,0:T(8,128)}, u32[]{:S(2)}) copy-start(f32[8,128]{1,0:T(8,128)} %get-tuple-element.70) | copy-start | bytes 12292
  463.5 11.2 %copy-start.5 = (bf16[640,1024]{1,0:T(8,128)(2,1)S(1)}, bf16[640,1024]{1,0:T(8,128)(2,1)}, u32[]{:S(2)}) copy-start(bf16[640,1024]{1,0:T(8,128)(2,1)} %get-tuple-element.58) | copy-start | bytes 3932164
  598.1 6.5 %copy-start.6 = (bf16[640,1024]{1,0:T(8,128)(2,1)S(1)}, bf16[640,1024]{1,0:T(8,128)(2,1)}, u32[]{:S(2)}) copy-start(bf16[640,1024]{1,0:T(8,128)(2,1)} %get-tuple-element.165) | copy-start | bytes 3932164
  (4 other events, 6.8 us)
Sparse Core Ops, SparseCore 0:
  85.1 35.1 all-gather.3
  148.1 75.6 all-gather.7
  225.8 38.9 all-gather.5
  275.3 99.4 reduce-scatter.3
  392.0 52.5 reduce-scatter.7
  448.2 51.3 reduce-scatter.5

commit v4 on v3

--- a/solution.py
+++ b/solution.py
@@ -2,6 +2,7 @@
 
 import jax
 import jax.numpy as jnp
+import numpy as np
 from jax import lax
 from jax.experimental.layout import Layout, with_layout_constraint
 from jax.experimental import pallas as pl
@@ -13,6 +14,7 @@
 THETA = 1000000.0
 AXES = ("dp", "tensor")
 ROWS = 256
+PROJECTED = 512
 BLOCK = 512
 STEP = 512
 SCALE = HEAD_SIZE ** (-0.5)
@@ -268,10 +270,15 @@
     )(tokens, heads, output, gains, facts)
 
 
+def sorting(places, first, count):
+    index = first + lax.broadcasted_iota(jnp.int32, (count, places.shape[1]), 0)
+    return jnp.where(places == index, 1.0, 0.0).astype(BF16)
+
+
 def project_kernel(
-    query_heads, key_heads, x_ref, gain_ref, w_ref, gq_ref, gk_ref, cos_ref, sin_ref, normed_ref, qkv_ref, scale_ref
+    query_heads, key_heads, x_ref, places_ref, gain_ref, w_ref, gq_ref, gk_ref, cos_ref, sin_ref, normed_ref, qkv_ref, scale_ref
 ):
-    x = x_ref[...].astype(F32)
+    x = dot_nn(sorting(places_ref[...], pl.program_id(0) * PROJECTED, PROJECTED), x_ref[...])
     normed = (x * row_scale(x) * gain_ref[...]).astype(BF16)
     normed_ref[...] = normed
     raw = dot_nn(normed, w_ref[...])
@@ -294,16 +301,17 @@
             scale_ref[kv] = scales
 
 
-def project(x, gain, weights, gain_query, gain_key, cosine, sine, query_heads, key_heads):
+def project(x, places, gain, weights, gain_query, gain_key, cosine, sine, query_heads, key_heads):
     rows, width = x.shape
     wide = weights.shape[1]
     whole = lambda shape: pl.BlockSpec(shape, lambda i: (0, 0))
-    block = lambda cols: pl.BlockSpec((ROWS, cols), lambda i: (i, 0))
+    block = lambda cols: pl.BlockSpec((PROJECTED, cols), lambda i: (i, 0))
     return pl.pallas_call(
         functools.partial(project_kernel, query_heads, key_heads),
-        grid=(rows // ROWS,),
+        grid=(rows // PROJECTED,),
         in_specs=[
-            block(width),
+            pl.BlockSpec((rows, width), lambda i: (0, 0), pipeline_mode=pl.Buffered(1)),
+            whole((1, rows)),
             whole((1, width)),
             whole((width, wide)),
             whole((1, HEAD_SIZE)),
@@ -311,7 +319,7 @@
             block(HEAD_SIZE),
             block(HEAD_SIZE),
         ],
-        out_specs=[block(width), block(wide), pl.BlockSpec((key_heads, ROWS, HEAD_SIZE), lambda i: (0, i, 0))],
+        out_specs=[block(width), block(wide), pl.BlockSpec((key_heads, PROJECTED, HEAD_SIZE), lambda i: (0, i, 0))],
         out_shape=[
             jax.ShapeDtypeStruct((rows, width), BF16),
             jax.ShapeDtypeStruct((rows, wide), BF16),
@@ -319,7 +327,7 @@
         ],
         compiler_params=pltpu.CompilerParams(vmem_limit_bytes=VMEM_LIMIT),
         name="project",
-    )(x, gain, weights, gain_query, gain_key, cosine, sine)
+    )(x, places, gain, weights, gain_query, gain_key, cosine, sine)
 
 
 def first_place(info_ref, blocks, docs, places):
@@ -376,7 +384,7 @@
     total = acc_ref[:, HEAD_SIZE:]
     out = (acc_ref[:, :HEAD_SIZE] / total).astype(BF16)
     for h in range(group):
-        o_ref[0, :, h * HEAD_SIZE : (h + 1) * HEAD_SIZE] = out[h * BLOCK : (h + 1) * BLOCK]
+        o_ref[:, h * HEAD_SIZE : (h + 1) * HEAD_SIZE] = out[h * BLOCK : (h + 1) * BLOCK]
     lse_ref[0, 0] = across(jnp.log2(total) * (1.0 / HEAD_SIZE), 3)
 
 
@@ -401,7 +409,7 @@
             grid=(key_heads, blocks),
             in_specs=head_specs(rows, group, 0),
             out_specs=[
-                pl.BlockSpec((1, BLOCK, wide), lambda h, i, s: (h, i, 0)),
+                pl.BlockSpec((BLOCK, wide), lambda h, i, s: (i, h)),
                 pl.BlockSpec((1, 1, 8, group * BLOCK), lambda h, i, s: (h, i, 0, 0)),
             ],
             scratch_shapes=[
@@ -411,7 +419,7 @@
             ],
         ),
         out_shape=[
-            jax.ShapeDtypeStruct((key_heads, rows, wide), BF16),
+            jax.ShapeDtypeStruct((rows, key_heads * wide), BF16),
             jax.ShapeDtypeStruct((key_heads, blocks, 8, group * BLOCK), F32),
         ],
         compiler_params=pltpu.CompilerParams(vmem_limit_bytes=VMEM_LIMIT),
@@ -461,7 +469,7 @@
         return jnp.concatenate([value[:, h * HEAD_SIZE : (h + 1) * HEAD_SIZE] for h in range(group)], axis=0)
 
     queries, grads = stacked(q_ref[...]), stacked(do_ref[...])
-    delta = across(stacked(o_ref[0]).astype(F32) * grads.astype(F32), 2)[:1]
+    delta = across(stacked(o_ref[...]).astype(F32) * grads.astype(F32), 2)[:1]
     lse = lse_ref[0, 0, :1]
     dq_acc[...] = jnp.zeros_like(dq_acc)
     places = i * BLOCK + lax.rem(lax.broadcasted_iota(jnp.int32, (1, group * BLOCK), 1), BLOCK)
@@ -520,7 +528,7 @@
     blocks = rows // BLOCK
     group = query_heads // key_heads
     wide = group * HEAD_SIZE
-    own = pl.BlockSpec((1, BLOCK, wide), lambda h, i, s: (kv, i, 0))
+    own = pl.BlockSpec((BLOCK, wide), lambda h, i, s: (i, kv))
     whole = lambda shape: pl.BlockSpec(shape, lambda h, i, s: (0, 0), pipeline_mode=pl.Buffered(1))
     return pl.pallas_call(
         functools.partial(backward_kernel, group, blocks, docs),
@@ -530,7 +538,7 @@
             in_specs=[
                 *head_specs(rows, group, kv),
                 own,
-                pl.BlockSpec((BLOCK, wide), lambda h, i, s: (i, 0)),
+                own,
                 pl.BlockSpec((1, 1, 8, group * BLOCK), lambda h, i, s: (kv, i, 0, 0)),
                 whole((rows, HEAD_SIZE)),
                 whole((rows, HEAD_SIZE)),
@@ -580,11 +588,11 @@
     return place, chunk
 
 
-def group_barrier(span, place):
+def group_barrier(span, place, *others):
     barrier = pltpu.get_barrier_semaphore()
-    for k in range(1, span):
-        pl.semaphore_signal(barrier, device_id=place(k), device_id_type=pl.DeviceIdType.MESH)
-    pl.semaphore_wait(barrier, span - 1)
+    for to in [place(k) for k in range(1, span)] + list(others):
+        pl.semaphore_signal(barrier, device_id=to, device_id_type=pl.DeviceIdType.MESH)
+    pl.semaphore_wait(barrier, span - 1 + len(others))
 
 
 def remote_copy(src, dst, send_sem, recv_sem, to):
@@ -603,59 +611,59 @@
     return [0, half] + [k for k in range(1, span) if k != half]
 
 
-def output_kernel(span, count, *refs):
-    heads = refs[:count]
-    w_hbm, tokens_ref, gain_ref, middle_ref, normed_ref, mixed_ref, w_ref, send_sems, recv_sems, local_sems = refs[count:]
+def output_kernel(
+    span,
+    heads_ref,
+    places_ref,
+    w_hbm,
+    tokens_ref,
+    gain_ref,
+    middle_ref,
+    normed_ref,
+    mixed_ref,
+    w_ref,
+    out_s,
+    send_sems,
+    recv_sems,
+    local_sem,
+):
     place, chunk = group_places(span)
     rows, width = tokens_ref.shape
-    wide = heads[0].shape[1]
-    load = pltpu.make_async_copy(w_hbm, w_ref, local_sems.at[count])
+    load = pltpu.make_async_copy(w_hbm, w_ref, local_sem)
     load.start()
     group_barrier(span, place)
     copies = {}
-    for h, ref in enumerate(heads):
-        to = pl.ds(h * wide, wide)
-        for k in range(1, span):
-            at = h * span + k
-            copies[h, k] = remote_copy(
-                ref.at[pl.ds(k * rows, rows)], mixed_ref.at[k, :, to], send_sems.at[at], recv_sems.at[at], place(k)
-            )
-            copies[h, k].start()
-        copies[h, 0] = pltpu.make_async_copy(ref.at[pl.ds(0, rows)], mixed_ref.at[0, :, to], local_sems.at[h])
-        copies[h, 0].start()
+    index = lax.broadcasted_iota(jnp.int32, (rows, heads_ref.shape[0]), 1)
+    for k in reversed(arrival_order(span)):
+        picks = jnp.where(places_ref[k * rows : (k + 1) * rows, :] == index, 1.0, 0.0).astype(BF16)
+        block = dot_nn(picks, heads_ref[...]).astype(BF16)
+        if k:
+            out_s[k] = block
+            copies[k] = remote_copy(out_s.at[k], mixed_ref.at[k], send_sems.at[k], recv_sems.at[k], place(k))
+            copies[k].start()
+        else:
+            mixed_ref[0] = block
     middle_ref[...] = tokens_ref[...].astype(F32)
     load.wait()
-    piece = rows // 2
     for k in arrival_order(span):
-        for h in range(count):
-            if k:
-                copies[h, k].wait_recv()
-            else:
-                copies[h, k].wait()
+        if k:
+            copies[k].wait_recv()
         weights = w_ref[:, chunk(k)].reshape(width, w_ref.shape[3])
-
-        def step(m, carry, k=k, weights=weights):
-            at = pl.ds(pl.multiple_of(m * piece, piece), piece)
-            middle_ref[at, :] += dot_nt(mixed_ref[k, at, :], weights)
-            return carry
-
-        lax.fori_loop(0, rows // piece, step, 0)
+        middle_ref[...] += dot_nt(mixed_ref[k], weights)
     middle = middle_ref[...]
     normed_ref[...] = (middle * row_scale(middle) * gain_ref[...]).astype(BF16)
     for k in range(1, span):
-        for h in range(count):
-            copies[h, k].wait_send()
-
-
-def output_project(heads, weights, tokens, gain):
+        copies[k].wait_send()
+
+
+def output_project(heads, places, weights, tokens, gain):
     devices, span, shard, cols = weights.shape
     rows, width = tokens.shape
-    count = len(heads)
     any_ref = pl.BlockSpec(memory_space=pl.ANY)
     local_ref = pl.BlockSpec(memory_space=pltpu.VMEM)
     return pl.pallas_call(
-        functools.partial(output_kernel, span, count),
-        in_specs=[any_ref] * (count + 1) + [local_ref] * 2,
+        functools.partial(output_kernel, span),
+        in_specs=[local_ref] * 2 + [any_ref] + [local_ref] * 2,
         out_specs=[local_ref] * 3,
         out_shape=[
             jax.ShapeDtypeStruct((rows, width), F32),
@@ -664,87 +672,136 @@
         ],
         scratch_shapes=[
             pltpu.VMEM(weights.shape, BF16),
-            pltpu.SemaphoreType.DMA((span * count,)),
-            pltpu.SemaphoreType.DMA((span * count,)),
-            pltpu.SemaphoreType.DMA((count + 1,)),
+            pltpu.VMEM((span, rows, cols), BF16),
+            pltpu.SemaphoreType.DMA((span,)),
+            pltpu.SemaphoreType.DMA((span,)),
+            pltpu.SemaphoreType.DMA,
         ],
         compiler_params=pltpu.CompilerParams(
             collective_id=1, has_side_effects=True, vmem_limit_bytes=VMEM_LIMIT
         ),
         cost_estimate=pl.CostEstimate(flops=0, bytes_accessed=100_000_000, transcendentals=0),
         name="output_project",
-    )(*heads, weights, tokens, gain)
-
-
-def output_back_kernel(span, count, b_ref, mixed_ref, w_hbm, *refs):
-    outs = refs[:count]
-    dw_hbm, w_ref, grad_ref, dw_ref, bt_ref, send_sems, recv_sems, local_sems = refs[count:]
+    )(heads, places, weights, tokens, gain)
+
+
+def output_back_kernel(
+    span,
+    b_ref,
+    mixed_ref,
+    places_ref,
+    w_hbm,
+    result_hbm,
+    feed_hbm,
+    out_ref,
+    dw_hbm,
+    result_out,
+    w_ref,
+    grad_s,
+    in_s,
+    dw_ref,
+    bt_ref,
+    send_sems,
+    recv_sems,
+    local_sems,
+):
     place, chunk = group_places(span)
     rows, width = b_ref.shape
-    wide = outs[0].shape[1]
     cols = w_ref.shape[3]
-    load = pltpu.make_async_copy(w_hbm, w_ref, local_sems.at[0])
+    load = pltpu.make_async_copy(w_hbm, w_ref, local_sems.at[span])
     load.start()
-    group_barrier(span, place)
+    dp, t = lax.axis_index("dp"), lax.axis_index("tensor")
+    p, c = dp // 2, lax.rem(dp, 2)
+    settled = c == t // (span // 2)
+    partner = (p * 2 + 1 - c, span - 1 - t)
+    group_barrier(span, place, partner)
     load.wait()
-    piece = rows // 2
+    swap = remote_copy(result_hbm, result_out, send_sems.at[0], recv_sems.at[0], partner)
+    keep = pltpu.make_async_copy(result_hbm, result_out, local_sems.at[span + 1])
     copies = {}
     for k in reversed(arrival_order(span)):
-        weights = w_ref[:, chunk(k)].reshape(width, cols)
-
-        def step(m, carry, k=k, weights=weights):
-            at = pl.ds(pl.multiple_of(m * piece, piece), piece)
-            grad_ref[k, at, :] = dot_nn(b_ref[at, :], weights).astype(BF16)
-            return carry
-
-        lax.fori_loop(0, rows // piece, step, 0)
-        for h, ref in enumerate(outs):
-            src, dst = grad_ref.at[k, :, pl.ds(h * wide, wide)], ref.at[pl.ds(k * rows, rows)]
-            at = h * span + k
-            if k:
-                copies[h, k] = remote_copy(src, dst, send_sems.at[at], recv_sems.at[at], place(k))
-            else:
-                copies[h, k] = pltpu.make_async_copy(src, dst, local_sems.at[1 + h])
-            copies[h, k].start()
+        block = dot_nn(b_ref[...], w_ref[:, chunk(k)].reshape(width, cols)).astype(BF16)
+        if k:
+            grad_s[k] = block
+            copies[k] = remote_copy(grad_s.at[k], in_s.at[k], send_sems.at[k], recv_sems.at[k], place(k))
+            copies[k].start()
+        else:
+            in_s[0] = block
+    @pl.when(settled)
+    def _():
+        keep.start()
+
+    @pl.when(jnp.logical_not(settled))
+    def _():
+        swap.start()
+
     bt_ref[...] = b_ref[...].T
     stores = []
-    shard = w_ref.shape[2]
+    base = dw_hbm.shape[3] - span * cols
     for k in range(span):
         dw_ref[k] = dot_nn(bt_ref[...], mixed_ref[k]).astype(BF16).reshape(dw_ref.shape[1:])
-        stores.append(pltpu.make_async_copy(dw_ref.at[k], dw_hbm.at[:, chunk(k)], local_sems.at[1 + count + k]))
+        to = pl.ds(pl.multiple_of(base + chunk(k) * cols, 128), cols)
+        stores.append(pltpu.make_async_copy(dw_ref.at[k], dw_hbm.at[:, 0, :, to], local_sems.at[k]))
         stores[-1].start()
+    for k in arrival_order(span):
+        if k:
+            copies[k].wait_recv()
+
+        def sort_step(m, carry, k=k):
+            at = pl.ds(pl.multiple_of(m * rows, rows), rows)
+            block = dot_nn(sorting(places_ref[k], m * rows, rows), in_s[k]).astype(BF16)
+            if k:
+                out_ref[at, :] += block
+            else:
+                out_ref[at, :] = block
+            return carry
+
+        lax.fori_loop(0, span, sort_step, 0)
     for copy in stores:
         copy.wait()
-    for key, copy in copies.items():
-        copy.wait()
-
-
-def output_back(branch, mixed, weights, count):
+    for copy in copies.values():
+        copy.wait_send()
+
+    @pl.when(settled)
+    def _():
+        keep.wait()
+
+    @pl.when(jnp.logical_not(settled))
+    def _():
+        swap.wait()
+
+
+def output_back(branch, mixed, places, weights, result, feed_grads):
     devices, span, shard, cols = weights.shape
     rows, width = branch.shape
     any_ref = pl.BlockSpec(memory_space=pl.ANY)
     local_ref = pl.BlockSpec(memory_space=pltpu.VMEM)
     return pl.pallas_call(
-        functools.partial(output_back_kernel, span, count),
-        in_specs=[local_ref, local_ref, any_ref],
-        out_specs=[any_ref] * (count + 1),
-        out_shape=[jax.ShapeDtypeStruct((span * rows, cols // count), BF16)] * count
-        + [jax.ShapeDtypeStruct(weights.shape, BF16)],
+        functools.partial(output_back_kernel, span),
+        in_specs=[local_ref, local_ref, local_ref, any_ref, any_ref, any_ref],
+        out_specs=[local_ref, any_ref, any_ref],
+        input_output_aliases={5: 1},
+        out_shape=[
+            jax.ShapeDtypeStruct((span * rows, cols), BF16),
+            jax.ShapeDtypeStruct(feed_grads.shape, BF16),
+            jax.ShapeDtypeStruct(result.shape, BF16),
+        ],
         scratch_shapes=[
             pltpu.VMEM(weights.shape, BF16),
             pltpu.VMEM((span, rows, cols), BF16),
+            pltpu.VMEM((span, rows, cols), BF16),
             pltpu.VMEM((span, devices, shard, cols), BF16),
             pltpu.VMEM((width, rows), BF16),
-            pltpu.SemaphoreType.DMA((span * count,)),
-            pltpu.SemaphoreType.DMA((span * count,)),
-            pltpu.SemaphoreType.DMA((1 + count + span,)),
+            pltpu.SemaphoreType.DMA((span,)),
+            pltpu.SemaphoreType.DMA((span,)),
+            pltpu.SemaphoreType.DMA((span + 2,)),
         ],
         compiler_params=pltpu.CompilerParams(
             collective_id=2, has_side_effects=True, vmem_limit_bytes=VMEM_LIMIT
         ),
         cost_estimate=pl.CostEstimate(flops=0, bytes_accessed=100_000_000, transcendentals=0),
         name="output_back",
-    )(branch, mixed, weights)
+    )(branch, mixed, places, weights, result, feed_grads)
 
 
 def feed_kernel(last, x_ref, c_ref, w_ref, *refs):
@@ -757,7 +814,7 @@
     rows_all, width = x_ref.shape
     hidden = act_s.shape[1]
     devices, _, shard, _ = w_ref.shape
-    chunk = rows_all // 2
+    chunk = rows_all
 
     @pl.when(j == 0)
     def _():
@@ -816,7 +873,7 @@
         branch_ref[...] = grad.astype(BF16)
 
 
-def feed(x, cot, weights, *rest):
+def feed(x, cot, weights, *rest, room=0):
     rows, width = x.shape
     devices, span, shard, cols = weights.shape
     hidden = cols // 3
@@ -824,7 +881,7 @@
     whole = lambda shape: pl.BlockSpec(shape, lambda j: (0, 0), pipeline_mode=pl.Buffered(1))
     chunk = pl.BlockSpec((devices, 1, shard, cols), lambda j: (0, j, 0, 0))
     full = whole((rows, width))
-    grads = jax.ShapeDtypeStruct((devices, span, shard, cols), BF16)
+    grads = jax.ShapeDtypeStruct((devices, span, shard, cols + room), BF16)
     shape = lambda kind: jax.ShapeDtypeStruct((rows, width), kind)
     sums = [pltpu.VMEM((rows, width), F32)] * 2 if last else []
     return pl.pallas_call(
@@ -884,6 +941,7 @@
     final_s,
     pass_s,
     far_pass,
+    wt_s,
     gains_one,
     gains_two,
     gains_s,
@@ -916,7 +974,7 @@
         ]
 
     loads = [side_by_side(grads_hbm, pl.ds(k * rows, rows), grads.at[k], k * count) for k in range(span)]
-    order = list(range(half, span)) + list(range(1, half)) + [0]
+    order = list(range(half + 1, span)) + list(range(1, half)) + [half, 0]
     for k in order:
         for load in loads[k]:
             load.start()
@@ -937,6 +995,7 @@
         greeted += 1
     pl.semaphore_wait(barrier, greeted)
 
+    wt_s[...] = w_ref[...].T
     outputs = [copy_to(output_ref.at[r], output_out.at[r - 1], place(p, c, t ^ r)) for r in range(1, span)]
 
     piece = rows // 2
@@ -944,18 +1003,38 @@
     def multiply(k, dst, slot):
         def step(m, carry):
             at = pl.ds(pl.multiple_of(m * piece, piece), piece)
-            dst[slot, at, :] = dot_nt(grads[k, at, :], w_ref[...]).astype(BF16)
+            dst[slot, at, :] = dot_nn(grads[k, at, :], wt_s[...]).astype(BF16)
             return carry
 
         lax.fori_loop(0, 2, step, 0)
 
-    sides = []
-    for k in range(half, span):
+    sides, hops = {}, {}
+    away = list(range(1, half))
+
+    def product_for_sibling(k):
+        for load in loads[half + k]:
+            load.wait()
+        multiply(half + k, theirs, k)
+        sides[k] = copy_to(theirs.at[k], from_sibling.at[k], sibling)
+        sides[k].start()
+
+    def own_sum(k):
         for load in loads[k]:
             load.wait()
-        multiply(k, theirs, k - half)
-        sides.append(copy_to(theirs.at[k - half], from_sibling.at[k - half], sibling))
-        sides[-1].start()
+        multiply(k, mine, k)
+        sides[k].wait_recv()
+        mine[k] = (mine[k].astype(F32) + from_sibling[k].astype(F32)).astype(BF16)
+
+    for k in away:
+        product_for_sibling(k)
+    for k in away:
+        own_sum(k)
+        for m in range(2):
+            at = pl.ds(m * piece, piece)
+            hops[k, m] = copy_to(mine.at[k, at], from_line.at[k - 1, at], place(p, c, t ^ k))
+            hops[k, m].start()
+    product_for_sibling(0)
+    own_sum(0)
     for load in more:
         load.wait()
     turned[...] = normed_s[...].T
@@ -973,34 +1052,8 @@
         heads_copies.append(copy_to(heads_s.at[there], heads_in.at[k - 1], place(p ^ k, c, t)))
         heads_copies[-1].start()
 
-    hops = {}
-    for k in list(range(1, half)) + [0]:
-        for load in loads[k]:
-            load.wait()
-        multiply(k, mine, k)
-        sides[k].wait_recv()
-        mine[k] = (mine[k].astype(F32) + from_sibling[k].astype(F32)).astype(BF16)
-        if k:
-            for m in range(2):
-                at = pl.ds(m * piece, piece)
-                hops[k, m] = copy_to(mine.at[k, at], from_line.at[k - 1, at], place(p, c, t ^ k))
-                hops[k, m].start()
     for copy in outputs:
         copy.start()
-
-    for copy in heads_copies:
-        copy.wait_recv()
-    summed = heads_s[pl.ds(p * block, block), :].astype(F32)
-    for k in range(1, pairs):
-        summed = summed + heads_in[k - 1].astype(F32)
-    far_s[...] = summed.astype(BF16)
-    side = copy_to(far_s, far_pass, sibling)
-    far = copy_to(far_pass, far_in, place(p, 1 - c, lax.rem(t + half, span)))
-    near = copy_to(near_s, near_in, sibling)
-
-    @pl.when(jnp.logical_not(settled))
-    def _():
-        side.start()
 
     swaps = []
     gain_sum = jnp.zeros((1, width), F32)
@@ -1027,9 +1080,6 @@
         @pl.when(settled)
         def _():
             keep.start()
-            if m == 0:
-                side.wait_recv()
-                far.start()
 
         @pl.when(jnp.logical_not(settled))
         def _():
@@ -1052,12 +1102,31 @@
         handed.wait_recv()
         passed.start()
 
+    for copy in heads_copies:
+        copy.wait_recv()
+    summed = heads_s[pl.ds(p * block, block), :].astype(F32)
+    for k in range(1, pairs):
+        summed = summed + heads_in[k - 1].astype(F32)
+    far_s[...] = summed.astype(BF16)
+    side = copy_to(far_s, far_pass, sibling)
+    far = copy_to(far_pass, far_in, place(p, 1 - c, lax.rem(t + half, span)))
+    near = copy_to(near_s, near_in, sibling)
+
+    @pl.when(jnp.logical_not(settled))
+    def _():
+        side.start()
+
     for copy in first_gains:
         copy.wait_recv()
     total = gains_s[...]
     for k in range(1, 2 * span):
         total = total + gains_one[k - 1]
     gains_out[...] = total
+    @pl.when(settled)
+    def _():
+        side.wait_recv()
+        far.start()
+
     second_gains = [copy_to(gains_out, gains_two.at[k - 1], place(p ^ k, c, t)) for k in range(1, pairs)]
     for copy in second_gains:
         copy.start()
@@ -1088,7 +1157,7 @@
         near.wait_recv()
         heads_out[...] = near_in[...].astype(F32)
 
-    for copy in sides + list(hops.values()) + heads_copies:
+    for copy in list(sides.values()) + list(hops.values()) + heads_copies:
         copy.wait_send()
     for copy in outputs:
         copy.wait()
@@ -1143,6 +1212,7 @@
             pltpu.VMEM((rows, width), BF16),
             pltpu.VMEM((rows // 2, width), BF16),
             pltpu.VMEM((2 * shard, cols), BF16),
+            pltpu.VMEM((cols, width), BF16),
             pltpu.VMEM((2 * span - 1, 8, width), F32),
             pltpu.VMEM((pairs - 1, 8, width), F32),
             pltpu.VMEM((8, width), F32),
@@ -1211,11 +1281,6 @@
     def behind(x, other):
         return jnp.where(never, other[0, 0].astype(x.dtype), x)
 
-    def later(x, other):
-        at = (0,) * x.ndim
-        block = lax.slice(x, at, x.shape[:-2] and (1,) * (x.ndim - 2) + (8, 128) or (8, 128))
-        return lax.dynamic_update_slice(x, jnp.where(never, other[0, 0].astype(x.dtype), block), at)
-
     def line(x, steps):
         return [send(x, lambda pp, cc, tt: (pp, cc, tt ^ r)) for r in steps]
 
@@ -1266,7 +1331,6 @@
         tt, cc = t ^ (k % half), c ^ (k // half)
         places.append(lax.dynamic_index_in_dim(order, jnp.where(cc == tt // half, tt, span - 1 - tt), 0, False))
     places = jnp.concatenate(places)
-    inverse = jnp.argsort(places)
     before = jnp.arange(docs)[None, :] < jnp.arange(docs)[:, None]
     starts = jnp.sum(jnp.where(before, length[None, :], 0), axis=1).astype(jnp.int32)
 
@@ -1277,41 +1341,43 @@
     low = start_of(index) // BLOCK
     clear = (start_of(index + BLOCK - 1) + BLOCK - 1) // BLOCK
     info = jnp.concatenate([low, clear, starts]).astype(jnp.int32)
-    index = jnp.arange(group_rows, dtype=jnp.int32)
-    position = (index - start_of(index)).astype(F32)
-    inverse_rate = THETA ** (-(jnp.arange(HEAD_SIZE // 2, dtype=F32) * 2.0 / HEAD_SIZE))
-    angle = position[:, None] * inverse_rate[None, :]
-    cosine, sine = jnp.cos(angle), jnp.sin(angle)
-    cosine = jnp.concatenate([cosine, cosine], axis=1)
-    sine = jnp.concatenate([-sine, sine], axis=1)
-
-    tokens_sorted = jnp.take(tokens_all, inverse, axis=0, mode="clip")
+    rate = np.float32(THETA) ** (-(np.arange(HEAD_SIZE // 2, dtype=np.float32) * np.float32(2.0) / HEAD_SIZE))
+    angle = np.arange(group_rows, dtype=np.float32)[:, None] * rate.astype(np.float32)[None, :]
+    turn_c, turn_s = np.cos(angle), np.sin(angle)
+    tables = np.concatenate([turn_c, turn_c, -turn_s, turn_s], axis=1).astype(np.float32)
+    turned, index = jnp.asarray(tables), jnp.arange(group_rows, dtype=jnp.int32)[:, None]
+    for doc in range(1, docs):
+        moved = lax.dynamic_slice(jnp.asarray(np.concatenate([tables, tables])), (group_rows - starts[doc], 0), tables.shape)
+        turned = jnp.where(index >= starts[doc], moved, turned)
+    cosine, sine = turned[:, :HEAD_SIZE], turned[:, HEAD_SIZE:]
+
     cot_own = swap(cotangent)
     normed, qkv, scales = project(
-        tokens_sorted, gain_one, heads_weights, gain_query, gain_key, cosine, sine, query_heads, key_heads
+        tokens_all, places[None], gain_one, heads_weights, gain_query, gain_key, cosine, sine, query_heads, key_heads
     )
 
     line_weights = gather_wide([behind(piece, qkv) for piece in feed_line])
 
     attended, lse = attention_forward(info, qkv, query_heads, key_heads, docs)
-    unsorted = [jnp.take(attended[kv], places, axis=0, mode="clip") for kv in range(key_heads)]
 
     hidden = gate_weight.shape[1]
-    middle, normed_two, mixed = output_project(unsorted, output_weights, swapped, gain_two)
+    middle, normed_two, mixed = output_project(attended, places[:, None], output_weights, swapped, gain_two)
     out, normed_grad, line_grad = feed(normed_two, cot_own, line_weights)
     result, middle_grad, branch, gain_two_grad, own_grad = feed(
-        normed_two, cot_own, own_weights, out, normed_grad, middle, gain_two
+        normed_two, cot_own, own_weights, out, normed_grad, middle, gain_two, room=span * head_columns
     )
     line_sum = scatter_wide(line_grad)
 
-    *head_rows, output_grad = output_back(branch, mixed, output_weights, key_heads)
-    layer_output = swap(result)
+    attended_grad, own_grad, layer_output = output_back(
+        branch, mixed, places.reshape(span, 1, rows), output_weights, result, own_grad
+    )
+    [both_sum] = scatter_wide(own_grad)
+    own_sum = both_sum[:, : 3 * hidden]
 
     head_grads, head_gains = [], 0.0
     for kv in range(key_heads):
-        attended_grad = jnp.take(head_rows[kv], inverse, axis=0, mode="clip")
         if kv > 0:
-            attended_grad = behind(attended_grad, grads)
+            info = jnp.where(never, behind(line_sum[0], head_grads[0])[0, 0].astype(jnp.int32), info)
         grads, gains_of = attention_backward(
             info,
             qkv,
@@ -1329,14 +1395,20 @@
             kv,
         )
         if kv == 0:
-            output_sum = scatter_wide(later(later(output_grad, line_sum[0]), grads))
-            own_sum = scatter_wide(later(own_grad, grads))
             line_in = [
-                send(piece, lambda pp, cc, tt: (pp, cc, tt ^ r)) for r, piece in enumerate(line_sum, start=1)
+                send(behind(piece, grads), lambda pp, cc, tt: (pp, cc, tt ^ r))
+                for r, piece in enumerate(line_sum, start=1)
             ]
         head_grads.append(grads)
         head_gains = head_gains + gains_of
-    qkv_rows = [jnp.take(grads, places, axis=0, mode="clip") for grads in head_grads]
+    arrived = sum(piece[0, 0].astype(jnp.int32) for piece in line_in)
+    tied = jnp.where(never, arrived, places)
+    qkv_rows = [
+        jnp.take(grads, places if kv + 1 < key_heads else tied, axis=0, mode="clip")
+        for kv, grads in enumerate(head_grads)
+    ]
+    output_sum = behind(both_sum, qkv_rows[-1])[:, 3 * hidden :]
+    output_sum = output_sum.reshape(shard, span, head_columns).transpose(1, 0, 2)
     gain_rows = jnp.concatenate(
         [
             jnp.zeros((1, width), F32),
@@ -1356,7 +1428,7 @@
         swapped,
         gain_one,
         gain_rows,
-        jnp.stack(output_sum),
+        output_sum,
     )
 
     def total(first, others):
@@ -1365,7 +1437,7 @@
             out = out + other.astype(F32)
         return out
 
-    wide_sum = total(own_sum[0], line_in)
+    wide_sum = total(behind(own_sum, gain_sums), [behind(piece, gain_sums) for piece in line_in])
     output_sum = total(output_sum[0], [output_in[k] for k in range(span - 1)])
     stride = per_query + 2 * per_key
     columns = lambda at, size: jnp.concatenate(

time: 624 us -> 570 us (0.913)
  local copies, waits for them, and re-layouts: 106 us -> 60.2 us
  Pallas kernels: 405 us -> 428 us
  other arithmetic: 40.9 us -> 28.1 us
  starting transfers between devices: 24 us -> 13.8 us
  waiting for transfers between devices: 20.5 us -> 13.3 us
    gather x7 -> x2, local copies, waits for them, and re-layouts: 67.5 us -> 18.4 us  [local(): jnp.take(grads, places if kv + 1 < key_heads else tied, axis=0, mode='clip')]
    pallas_call x2, Pallas kernels: 73.1 us -> 95.7 us  [the longest x1 51.4 us: output_back(): pl.pallas_call(functools.partial(output_back_kernel, span), in_specs=[loc...]
    pallas_call x1, Pallas kernels: 15.5 us -> 32 us  [project(): pl.pallas_call(functools.partial(project_kernel, query_heads, key_heads),...]
    ppermute x8 -> x7, waiting for transfers between devices: 13.9 us -> 0.02 us  [send(): return lax.ppermute(x, AXES, moves)]
    reduce_scatter x3 -> x2, starting transfers between devices: 11.3 us -> 0.08 us  [scatter_wide(): out = by_rows(lax.psum_scatter(out, 'dp', scatter_dimension=0, tiled=True))]
    pallas_call x2, Pallas kernels: 64.8 us -> 57.9 us  [attention_backward(): pl.pallas_call(functools.partial(backward_kernel, group, blocks, docs), g...]
    dynamic_update_slice x3 -> x0, other arithmetic: 6.33 us -> none  [later(): lax.dynamic_update_slice(x, jnp.where(never, other[0, 0].astype(x.dtype),...]
    unnamed x39 -> x45, local copies, waits for them, and re-layouts: 15.8 us -> 10.3 us
  transfers between devices with their start and end apart: 14 -> 12, of which waited for: 2 -> 2; matrix products, arithmetic and copies ran while one was open for 20% -> 10% of each run, Pallas kernels for 40% -> 48%
where the time goes in v4:
time: 570 us; the launch traced here: 562 us
  Pallas kernels  428 us (75%)
  local copies, waits for them, and re-layouts  60.2 us (11%)
  other arithmetic  28.1 us (5%)
  between operations  18.9 us (3%)
  starting transfers between devices  13.8 us (2%)
  waiting for transfers between devices  13.3 us (2%)
    pallas_call x1, Pallas kernels, last_transfers(): pl.pallas_call(functools.partial(last_kernel, pairs, span, count), in_spe...  90.9 us
    pallas_call x1, Pallas kernels, first_transfers(): pl.pallas_call(functools.partial(first_kernel, pairs, span), in_specs=[an...  65.8 us
    pallas_call x2, Pallas kernels, feed(): pl.pallas_call(functools.partial(feed_kernel, last), grid=(span,), in_spe...  63.2 us
    pallas_call x2, Pallas kernels, attention_backward(): pl.pallas_call(functools.partial(backward_kernel, group, blocks, docs), g...  57.9 us
    pallas_call x1, Pallas kernels, output_back(): pl.pallas_call(functools.partial(output_back_kernel, span), in_specs=[loc...  51.4 us
    pallas_call x1, Pallas kernels, output_project(): pl.pallas_call(functools.partial(output_kernel, span), in_specs=[local_re...  44.3 us
    pallas_call x1, Pallas kernels, project(): pl.pallas_call(functools.partial(project_kernel, query_heads, key_heads),...  32 us
    pallas_call x1, Pallas kernels, attention_forward(): pl.pallas_call(functools.partial(forward_kernel, group, blocks, docs), gr...  22.5 us
  transfers between devices with their start and end apart: 12, of which 2 were waited for; matrix products, arithmetic and copies ran while one was open for 10% of the time, Pallas kernels for 48%

profile of v4, /device:TPU:0, one launch (start us, length us, event | category | flops | bytes accessed | tf_op | source)
XLA Modules:
  0.0 562.2 jit_solution(16577831765605287087)
XLA Ops:
  14.0 1.8 copy.44
  17.2 65.8 %first_transfers.1 = (bf16[4,640,1024]{2,1,0:T(8,128)(2,1)}, bf16[1024,1024]{1,0:T(8,128)(2,1)}, bf16[4,128,512]{2,1,0:T(8,128)(2,1)}, bf16[128,384]{1,0:T(8,128)(2,1)}, s32[24,128]{1,0:T(8,128)}) custom-call(bf16[640,1024]{1,0:T(8,128)(2,1)} %tokens_ref.1, bf16[128,1024]{1,0:T(8,128)(2,1)} %copy-done.9, bf16[128,512]{1,0:T(8,128)(2,1)} %bitcast.91, ...), custom_call_target="tpu_custom_call" | custom-call | bytes 150000000 | tf_op jit(solution)/shard_map/first_transfers/pallas_call | solution.py:251
  91.3 3.8 collective-permute-start.1
  101.2 3.2 dynamic-slice_select_fusion
  106.1 32.0 %project.1 = (bf16[2560,1024]{1,0:T(8,128)(2,1)}, bf16[2560,1024]{1,0:T(8,128)(2,1)}, f32[2,2560,128]{2,1,0:T(8,128)}) custom-call(bf16[2560,1024]{1,0:T(8,128)(2,1)} %bitcast.85, s32[1,2560]{1,0:T(1,128)} %broadcast_in_dim.102.places_ref, f32[1,1024]{1,0:T(1,128)} %bitcast.93, bf16[1024,1024]{1,0:T(8,128)(2,1)} %get-tuple-element.48.w_ref.refs_5_, ...), custom_call_target="tpu_custom_call" | custom-call | tf_op jit(solution)/shard_map/project/pallas_call | solution.py:309
  139.2 1.8 broadcast_select_fusion.1
  146.3 2.0 broadcast_in_dim.114.places_ref
  149.0 22.5 %attention_forward.1 = (bf16[2560,512]{1,0:T(8,128)(2,1)}, f32[2,5,8,1024]{3,2,1,0:T(8,128)}) custom-call(s32[12]{0:T(128)} %pad_add_fusion.3.info_ref, bf16[2560,1024]{1,0:T(8,128)(2,1)} %get-tuple-element.49.q_ref.k_ref.v_ref, bf16[2560,1024]{1,0:T(8,128)(2,1)} %get-tuple-element.49.q_ref.k_ref.v_ref, bf16[2560,1024]{1,0:T(8,128)(2,1)} %get-tuple-element.49.q_ref.k_ref.v_ref), custom_call_target="tpu_custom_call" | custom-call | bytes 100000000 | tf_op jit(solution)/shard_map/attention_forward/pallas_call | solution.py:405
  172.7 44.3 %output_project.1 = (f32[640,1024]{1,0:T(8,128)}, bf16[640,1024]{1,0:T(8,128)(2,1)}, bf16[4,640,512]{2,1,0:T(8,128)(2,1)}) custom-call(bf16[2560,512]{1,0:T(8,128)(2,1)} %get-tuple-element.50.heads_ref.o_ref, s32[2560,1]{1,0:T(8,128)} %broadcast_in_dim.114.places_ref, bf16[8,4,128,512]{3,2,1,0:T(8,128)(2,1)} %bitcast.81, bf16[640,1024]{1,0:T(8,128)(2,1)} %copy-done.1, ...), custom_call_target="tpu_custom_call" | custom-call | bytes 100000000 | tf_op jit(solution)/shard_map/output_project/pallas_call | solution.py:664
  217.0 4.5 all-gather.8.cloned.1.call-done
  221.5 40.5 %feed_forward.2 = (f32[640,1024]{1,0:T(8,128)}, f32[640,1024]{1,0:T(8,128)}, bf16[8,3,128,2304]{3,2,1,0:T(8,128)(2,1)}) custom-call(bf16[640,1024]{1,0:T(8,128)(2,1)} %get-tuple-element.52.x_ref, bf16[640,1024]{1,0:T(8,128)(2,1)} %broadcast_select_fusion.c_ref, bf16[8,3,128,2304]{3,2,1,0:T(8,128)(2,1)} %bitcast.84), custom_call_target="tpu_custom_call" | custom-call | tf_op jit(solution)/shard_map/feed_forward/pallas_call | solution.py:887
  262.7 22.7 %feed_forward.3 = (bf16[640,1024]{1,0:T(8,128)(2,1)}, f32[640,1024]{1,0:T(8,128)}, bf16[640,1024]{1,0:T(8,128)(2,1)}, f32[8,1024]{1,0:T(8,128)}, bf16[8,1,128,4352]{3,2,1,0:T(8,128)(2,1)}) custom-call(bf16[640,1024]{1,0:T(8,128)(2,1)} %get-tuple-element.52.x_ref, bf16[640,1024]{1,0:T(8,128)(2,1)} %broadcast_select_fusion.c_ref, ...), custom_call_target="tpu_custom_call" | custom-call | tf_op jit(solution)/shard_map/feed_forward/pallas_call | solution.py:887
  285.4 51.4 %output_back.1 = (bf16[2560,512]{1,0:T(8,128)(2,1)}, bf16[8,1,128,4352]{3,2,1,0:T(8,128)(2,1)}, bf16[640,1024]{1,0:T(8,128)(2,1)}) custom-call(bf16[640,1024]{1,0:T(8,128)(2,1)} %get-tuple-element.56.b_ref, bf16[4,640,512]{2,1,0:T(8,128)(2,1)} %get-tuple-element.57.mixed_ref, ...), custom_call_target="tpu_custom_call", output_to_operand_aliasing={{1}: (5, {})} | custom-call | bytes 100000000 | tf_op jit(solution)/shard_map/output_back/pallas_call | solution.py:779
  336.8 28.9 %attention_backward.2 = (bf16[2560,512]{1,0:T(8,128)(2,1)}, f32[8,128]{1,0:T(8,128)}) custom-call(s32[12]{0:T(128)} %pad_add_fusion.3.info_ref, bf16[2560,1024]{1,0:T(8,128)(2,1)} %get-tuple-element.49.q_ref.k_ref.v_ref, bf16[2560,1024]{1,0:T(8,128)(2,1)} %get-tuple-element.49.q_ref.k_ref.v_ref, bf16[2560,1024]{1,0:T(8,128)(2,1)} %get-tuple-element.49.q_ref.k_ref.v_ref, ...), custom_call_target="tpu_custom_call" | custom-call | bytes 100000000 | tf_op jit(solution)/shard_map/attention_backward/pallas_call | solution.py:533
  366.9 3.5 slice_select_fusion.1
  371.6 6.7 %collective-permute-start.5 = (bf16[128,2304]{1,0:T(8,128)(2,1)}, bf16[128,2304]{1,0:T(8,128)(2,1)}, u32[]{:S(2)}, u32[]{:S(2)}) collective-permute-start(bf16[128,2304]{1,0:T(8,128)(2,1)} %get-tuple-element.125), channel_id=1, source_target_pairs={{0,2},{1,3},{2,0},{3,1},{4,6},{5,7},{6,4},{7,5},{8,10},{9,11},{10,... | collective-permute-start | bytes 1769480 | tf_op jit(solution)/shard_map/ppermute | solution.py:1273
  379.2 8.6 %gather_fusion = bf16[2560,512]{1,0:T(8,128)(2,1)} fusion(bf16[2560,512]{1,0:T(8,128)(2,1)S(1)} %copy-done, s32[3072]{0:T(1024)S(1)} %pad_clamp_fusion.1), kind=kCustom, calls=%fused_computation | custom fusion | bytes 5253120 | tf_op jit(solution)/shard_map/jit(_take)/gather | solution.py:1407
  390.2 29.0 %attention_backward.3 = (bf16[2560,512]{1,0:T(8,128)(2,1)}, f32[8,128]{1,0:T(8,128)}) custom-call(s32[12]{0:T(128)} %broadcast_select_fusion.7.info_ref, bf16[2560,1024]{1,0:T(8,128)(2,1)} %get-tuple-element.49.q_ref.k_ref.v_ref, bf16[2560,1024]{1,0:T(8,128)(2,1)} %get-tuple-element.49.q_ref.k_ref.v_ref, ...), custom_call_target="tpu_custom_call" | custom-call | bytes 100000000 | tf_op jit(solution)/shard_map/attention_backward/pallas_call | solution.py:533
  425.5 9.8 %gather_fusion.1 = bf16[2560,512]{1,0:T(8,128)(2,1)S(1)} fusion(bf16[2560,512]{1,0:T(8,128)(2,1)} %get-tuple-element.66.refs_3_, s32[3072]{0:T(1024)S(1)} %pad_clamp_fusion), kind=kCustom, calls=%fused_computation.1 | custom fusion | bytes 5253120 | tf_op jit(solution)/shard_map/jit(_take)/gather | solution.py:1407
  435.9 8.0 %reduce-scatter.5.cloned.1.call-done = bf16[128,4352]{1,0:T(8,128)(2,1)} async-done(((bf16[1024,4352]{1,0:T(8,128)(2,1)}), bf16[128,4352]{1,0:T(8,128)(2,1)}) %reduce-scatter.5.cloned.1.call-update) | async-done | bytes 1114128 | tf_op jit(solution)/shard_map/reduce_scatter | solution.py:1295
  443.9 1.7 slice_select_fusion.4
  446.6 2.1 copy.49
  448.7 90.9 %last_transfers.1 = (bf16[640,1024]{1,0:T(8,128)(2,1)}, f32[128,1024]{1,0:T(8,128)}, f32[8,1024]{1,0:T(8,128)}, bf16[3,128,512]{2,1,0:T(8,128)(2,1)}) custom-call(bf16[2560,512]{1,0:T(8,128)(2,1)} %gather_fusion, bf16[2560,512]{1,0:T(8,128)(2,1)} %copy-done.2, bf16[2560,512]{1,0:T(8,128)(2,1)} %get-tuple-element.64.refs_2_, ...), custom_call_target="tpu_custom_call" | custom-call | tf_op jit(solution)/shard_map/last_transfers/pallas_call | solution.py:1187
  543.6 2.3 convert_add_fusion
  (139 shorter events, 55.6 us)
Async XLA Ops:
  7.2 165.6 %all-gather.4.cloned.1.call-start = ((), (), s32[]{:S(2)}) async-start(), calls=%async_computation.2 | async-start | bytes 4718592 | tf_op jit(solution)/shard_map/all_gather | solution.py:1289
  85.0 4.1 copy-start.11
  85.0 4.1 copy-start.12
  85.0 136.5 %all-gather.8.cloned.1.call-start = ((), (), s32[]{:S(2)}) async-start(), calls=%async_computation.4 | async-start | bytes 15925248 | tf_op jit(solution)/shard_map/all_gather | solution.py:1289
  87.7 16.7 %copy-start.1 = (bf16[640,1024]{1,0:T(8,128)(2,1)}, bf16[640,1024]{1,0:T(8,128)(2,1)S(1)}, u32[]{:S(2)}) copy-start(bf16[640,1024]{1,0:T(8,128)(2,1)S(1)} %slice_bitcast_fusion.tokens_ref.refs_7_) | copy-start | bytes 3932164
  87.8 7.3 %copy-start.14 = (s32[24,128]{1,0:T(8,128)S(1)}, s32[24,128]{1,0:T(8,128)}, u32[]{:S(2)}) copy-start(s32[24,128]{1,0:T(8,128)} %get-tuple-element.45) | copy-start | bytes 36868
  90.7 48.5 %collective-permute-start.3 = (bf16[128,2304]{1,0:T(8,128)(2,1)S(1)}, bf16[128,2304]{1,0:T(8,128)(2,1)}, u32[]{:S(2)}, u32[]{:S(2)}) collective-permute-start(bf16[128,2304]{1,0:T(8,128)(2,1)S(1)} %get-tuple-element.130), channel_id=1, source_target_pairs={{0,3},{1,2},{2,1},{3,0},{4,7},{5,6},{6,5},{7,4},{8,11},{9,10},{10,... | collective-permute-start | bytes 1769480 | tf_op jit(solution)/shard_map/ppermute | solution.py:1273
  90.7 50.3 %collective-permute-start.2 = (bf16[128,2304]{1,0:T(8,128)(2,1)S(1)}, bf16[128,2304]{1,0:T(8,128)(2,1)S(1)}, u32[]{:S(2)}, u32[]{:S(2)}) collective-permute-start(bf16[128,2304]{1,0:T(8,128)(2,1)S(1)} %get-tuple-element.130), channel_id=1, source_target_pairs={{0,2},{1,3},{2,0},{3,1},{4,6},{5,7},{6,4},{7,5},{8,10},{9,11},{10,... | collective-permute-start | bytes 1769480 | tf_op jit(solution)/shard_map/ppermute | solution.py:1273
  91.3 50.4 %collective-permute-start.1 = (bf16[128,2304]{1,0:T(8,128)(2,1)S(1)}, bf16[128,2304]{1,0:T(8,128)(2,1)S(1)}, u32[]{:S(2)}, u32[]{:S(2)}) collective-permute-start(bf16[128,2304]{1,0:T(8,128)(2,1)S(1)} %get-tuple-element.130), channel_id=1, source_target_pairs={{0,1},{1,0},{2,3},{3,2},{4,5},{5,4},{6,7},{7,6},{8,9},{9,8},{10,11... | collective-permute-start | bytes 1769480 | tf_op jit(solution)/shard_map/ppermute | solution.py:1273
  143.8 118.9 %all-gather.6.cloned.1.call-start = ((), (), s32[]{:S(2)}) async-start(), calls=%async_computation.3 | async-start | bytes 5308416 | tf_op jit(solution)/shard_map/all_gather | solution.py:1289
  144.5 222.4 %reduce-scatter.3.cloned.1.call-start = ((), (), s32[]{:S(2)}) async-start(), calls=%async_computation.5 | async-start | bytes 15925248 | tf_op jit(solution)/shard_map/reduce_scatter | solution.py:1295
  145.0 26.5 %collective-permute-start = (bf16[640,1024]{1,0:T(8,128)(2,1)S(1)}, bf16[640,1024]{1,0:T(8,128)(2,1)S(1)}, u32[]{:S(2)}, u32[]{:S(2)}) collective-permute-start(bf16[640,1024]{1,0:T(8,128)(2,1)S(1)} %copy-done.3), channel_id=1, source_target_pairs={{2,5},{3,4},{4,3},{5,2},{10,13},{11,12},{12,11},{13,10},{18,21},{1... | collective-permute-start | bytes 3932168 | tf_op jit(solution)/shard_map/ppermute | solution.py:1273
  262.0 181.9 %reduce-scatter.5.cloned.1.call-start = ((), (), s32[]{:S(2)}) async-start(), calls=%async_computation.6 | async-start | bytes 10027008 | tf_op jit(solution)/shard_map/reduce_scatter | solution.py:1295
  366.9 12.3 %copy-start = (bf16[2560,512]{1,0:T(8,128)(2,1)S(1)}, bf16[2560,512]{1,0:T(8,128)(2,1)}, u32[]{:S(2)}) copy-start(bf16[2560,512]{1,0:T(8,128)(2,1)} %get-tuple-element.64.refs_2_) | copy-start | bytes 7864324
  370.4 50.2 %collective-permute-start.4 = (bf16[128,2304]{1,0:T(8,128)(2,1)}, bf16[128,2304]{1,0:T(8,128)(2,1)S(1)}, u32[]{:S(2)}, u32[]{:S(2)}) collective-permute-start(bf16[128,2304]{1,0:T(8,128)(2,1)} %get-tuple-element.126), channel_id=1, source_target_pairs={{0,1},{1,0},{2,3},{3,2},{4,5},{5,4},{6,7},{7,6},{8,9},{9,8},{10,11... | collective-permute-start | bytes 1769480 | tf_op jit(solution)/shard_map/ppermute | solution.py:1273
  371.6 50.2 %collective-permute-start.5 = (bf16[128,2304]{1,0:T(8,128)(2,1)}, bf16[128,2304]{1,0:T(8,128)(2,1)}, u32[]{:S(2)}, u32[]{:S(2)}) collective-permute-start(bf16[128,2304]{1,0:T(8,128)(2,1)} %get-tuple-element.125), channel_id=1, source_target_pairs={{0,2},{1,3},{2,0},{3,1},{4,6},{5,7},{6,4},{7,5},{8,10},{9,11},{10,... | collective-permute-start | bytes 1769480 | tf_op jit(solution)/shard_map/ppermute | solution.py:1273
  378.3 45.3 %collective-permute-start.6 = (bf16[128,2304]{1,0:T(8,128)(2,1)}, bf16[128,2304]{1,0:T(8,128)(2,1)}, u32[]{:S(2)}, u32[]{:S(2)}) collective-permute-start(bf16[128,2304]{1,0:T(8,128)(2,1)} %get-tuple-element.124), channel_id=1, source_target_pairs={{0,3},{1,2},{2,1},{3,0},{4,7},{5,6},{6,5},{7,4},{8,11},{9,10},{10,... | collective-permute-start | bytes 1769480 | tf_op jit(solution)/shard_map/ppermute | solution.py:1273
  379.2 10.5 %copy-start.15 = (s32[12]{0:T(128)S(1)}, s32[12]{0:T(128)}, u32[]{:S(2)}) copy-start(s32[12]{0:T(128)} %pad_add_fusion.3.info_ref) | copy-start | bytes 148
  390.2 29.0 %copy-start.16 = (f32[8,128]{1,0:T(8,128)S(1)}, f32[8,128]{1,0:T(8,128)}, u32[]{:S(2)}) copy-start(f32[8,128]{1,0:T(8,128)} %get-tuple-element.70) | copy-start | bytes 12292
  420.5 14.8 %copy-start.7 = (bf16[128,2304]{1,0:T(8,128)(2,1)}, bf16[128,2304]{1,0:T(8,128)(2,1)S(1)}, u32[]{:S(2)}) copy-start(bf16[128,2304]{1,0:T(8,128)(2,1)S(1)} %collective-permute-done.4) | copy-start | bytes 1769476
  435.3 13.4 %copy-start.2 = (bf16[2560,512]{1,0:T(8,128)(2,1)}, bf16[2560,512]{1,0:T(8,128)(2,1)S(1)}, u32[]{:S(2)}) copy-start(bf16[2560,512]{1,0:T(8,128)(2,1)S(1)} %gather_fusion.1) | copy-start | bytes 7864324
  448.7 94.9 %copy-start.6 = (bf16[128,4352]{1,0:T(8,128)(2,1)S(1)}, bf16[128,4352]{1,0:T(8,128)(2,1)}, u32[]{:S(2)}) copy-start(bf16[128,4352]{1,0:T(8,128)(2,1)} %reduce-scatter.5.cloned.1.call-done) | copy-start | bytes 3342340
  448.7 94.9 %copy-start.8 = (bf16[128,2304]{1,0:T(8,128)(2,1)S(1)}, bf16[128,2304]{1,0:T(8,128)(2,1)}, u32[]{:S(2)}) copy-start(bf16[128,2304]{1,0:T(8,128)(2,1)} %copy-done.7) | copy-start | bytes 1769476
  546.9 6.4 %copy-start.4 = (bf16[640,1024]{1,0:T(8,128)(2,1)S(1)}, bf16[640,1024]{1,0:T(8,128)(2,1)}, u32[]{:S(2)}) copy-start(bf16[640,1024]{1,0:T(8,128)(2,1)} %get-tuple-element.178) | copy-start | bytes 3932164
  (5 other events, 12.7 us)
Sparse Core Ops, SparseCore 0:
  85.1 35.1 all-gather.3
  143.9 77.5 all-gather.7
  223.4 38.9 all-gather.5
  265.8 100.7 reduce-scatter.2
  370.0 73.8 reduce-scatter.4

commit v5 on v4

--- a/solution.py
+++ b/solution.py
@@ -691,11 +691,9 @@
     mixed_ref,
     places_ref,
     w_hbm,
-    result_hbm,
     feed_hbm,
     out_ref,
     dw_hbm,
-    result_out,
     w_ref,
     grad_s,
     in_s,
@@ -710,14 +708,8 @@
     cols = w_ref.shape[3]
     load = pltpu.make_async_copy(w_hbm, w_ref, local_sems.at[span])
     load.start()
-    dp, t = lax.axis_index("dp"), lax.axis_index("tensor")
-    p, c = dp // 2, lax.rem(dp, 2)
-    settled = c == t // (span // 2)
-    partner = (p * 2 + 1 - c, span - 1 - t)
-    group_barrier(span, place, partner)
+    group_barrier(span, place)
     load.wait()
-    swap = remote_copy(result_hbm, result_out, send_sems.at[0], recv_sems.at[0], partner)
-    keep = pltpu.make_async_copy(result_hbm, result_out, local_sems.at[span + 1])
     copies = {}
     for k in reversed(arrival_order(span)):
         block = dot_nn(b_ref[...], w_ref[:, chunk(k)].reshape(width, cols)).astype(BF16)
@@ -727,14 +719,6 @@
             copies[k].start()
         else:
             in_s[0] = block
-    @pl.when(settled)
-    def _():
-        keep.start()
-
-    @pl.when(jnp.logical_not(settled))
-    def _():
-        swap.start()
-
     bt_ref[...] = b_ref[...].T
     stores = []
     base = dw_hbm.shape[3] - span * cols
@@ -762,29 +746,20 @@
     for copy in copies.values():
         copy.wait_send()
 
-    @pl.when(settled)
-    def _():
-        keep.wait()
-
-    @pl.when(jnp.logical_not(settled))
-    def _():
-        swap.wait()
-
-
-def output_back(branch, mixed, places, weights, result, feed_grads):
+
+def output_back(branch, mixed, places, weights, feed_grads):
     devices, span, shard, cols = weights.shape
     rows, width = branch.shape
     any_ref = pl.BlockSpec(memory_space=pl.ANY)
     local_ref = pl.BlockSpec(memory_space=pltpu.VMEM)
     return pl.pallas_call(
         functools.partial(output_back_kernel, span),
-        in_specs=[local_ref, local_ref, local_ref, any_ref, any_ref, any_ref],
-        out_specs=[local_ref, any_ref, any_ref],
-        input_output_aliases={5: 1},
+        in_specs=[local_ref, local_ref, local_ref, any_ref, any_ref],
+        out_specs=[local_ref, any_ref],
+        input_output_aliases={4: 1},
         out_shape=[
             jax.ShapeDtypeStruct((span * rows, cols), BF16),
             jax.ShapeDtypeStruct(feed_grads.shape, BF16),
-            jax.ShapeDtypeStruct(result.shape, BF16),
         ],
         scratch_shapes=[
             pltpu.VMEM(weights.shape, BF16),
@@ -794,14 +769,14 @@
             pltpu.VMEM((width, rows), BF16),
             pltpu.SemaphoreType.DMA((span,)),
             pltpu.SemaphoreType.DMA((span,)),
-            pltpu.SemaphoreType.DMA((span + 2,)),
+            pltpu.SemaphoreType.DMA((span + 1,)),
         ],
         compiler_params=pltpu.CompilerParams(
             collective_id=2, has_side_effects=True, vmem_limit_bytes=VMEM_LIMIT
         ),
         cost_estimate=pl.CostEstimate(flops=0, bytes_accessed=100_000_000, transcendentals=0),
         name="output_back",
-    )(branch, mixed, places, weights, result, feed_grads)
+    )(branch, mixed, places, weights, feed_grads)
 
 
 def feed_kernel(last, x_ref, c_ref, w_ref, *refs):
@@ -954,7 +929,8 @@
     p, c = dp // 2, lax.rem(dp, 2)
     settled = c == t // half
     rows, width = middle_ref.shape
-    shard = output_ref.shape[1]
+    shard, parts = output_ref.shape[0], output_out.shape[2]
+    base = output_ref.shape[1] - span * parts
     place = lambda pp, cc, tt: (pp * 2 + cc, tt)
     sibling = place(p, 1 - c, t)
     used = [0]
@@ -996,7 +972,10 @@
     pl.semaphore_wait(barrier, greeted)
 
     wt_s[...] = w_ref[...].T
-    outputs = [copy_to(output_ref.at[r], output_out.at[r - 1], place(p, c, t ^ r)) for r in range(1, span)]
+    outputs = [
+        copy_to(output_ref.at[:, pl.ds(base + r * parts, parts)], output_out.at[r - 1], place(p, c, t ^ r))
+        for r in range(1, span)
+    ]
 
     piece = rows // 2
 
@@ -1175,10 +1154,10 @@
         passed.wait_recv()
 
 
-def last_transfers(pairs, span, grads, grads_sorted, normed, weights, middle_grad, tokens, gain, gains, output):
+def last_transfers(pairs, span, grads, grads_sorted, normed, weights, middle_grad, tokens, gain, gains, output, parts):
     rows, width = tokens.shape
     half = span // 2
-    shard = output.shape[1]
+    shard = output.shape[0]
     cols = weights.shape[1]
     count = len(grads)
     any_ref = pl.BlockSpec(memory_space=pl.ANY)
@@ -1192,7 +1171,7 @@
             jax.ShapeDtypeStruct((rows, width), BF16),
             jax.ShapeDtypeStruct((shard, cols), F32),
             jax.ShapeDtypeStruct((8, width), F32),
-            jax.ShapeDtypeStruct((span - 1, *output.shape[1:]), BF16),
+            jax.ShapeDtypeStruct((span - 1, shard, parts), BF16),
         ],
         scratch_shapes=[
             pltpu.VMEM((span, rows, cols), BF16),
@@ -1227,6 +1206,43 @@
     )(*grads, *grads_sorted, normed, weights, middle_grad, tokens, gain, gains, output)
 
 
+def finish_kernel(lines, span, key_heads, both_ref, *refs):
+    line_refs = refs[:lines]
+    output_ref, heads_ref, q_ref, k_ref, v_ref, o_ref, gate_ref, up_ref, down_ref = refs[lines:]
+    hidden = gate_ref.shape[1]
+    cols = o_ref.shape[0]
+
+    def part(k):
+        at = slice(k * hidden, (k + 1) * hidden)
+        total = both_ref[:, at].astype(F32)
+        for ref in line_refs:
+            total = total + ref[:, at].astype(F32)
+        return total
+
+    gate_ref[...] = part(0)
+    up_ref[...] = part(1)
+    down_ref[...] = part(2).T
+    total = both_ref[:, 3 * hidden : 3 * hidden + cols].astype(F32)
+    for r in range(span - 1):
+        total = total + output_ref[r].astype(F32)
+    o_ref[...] = total.T
+    query, key = q_ref.shape[1] // key_heads, k_ref.shape[1] // key_heads
+    for kv in range(key_heads):
+        at = kv * (query + 2 * key)
+        q_ref[:, kv * query : (kv + 1) * query] = heads_ref[:, at : at + query]
+        k_ref[:, kv * key : (kv + 1) * key] = heads_ref[:, at + query : at + query + key]
+        v_ref[:, kv * key : (kv + 1) * key] = heads_ref[:, at + query + key : at + query + 2 * key]
+
+
+def finish(both, lines, output, heads, shapes, span, key_heads):
+    return pl.pallas_call(
+        functools.partial(finish_kernel, len(lines), span, key_heads),
+        out_shape=[jax.ShapeDtypeStruct(shape, F32) for shape in shapes],
+        compiler_params=pltpu.CompilerParams(vmem_limit_bytes=VMEM_LIMIT),
+        name="finish",
+    )(both, *lines, output, heads)
+
+
 def local(
     tokens,
     lengths,
@@ -1368,16 +1384,14 @@
     )
     line_sum = scatter_wide(line_grad)
 
-    attended_grad, own_grad, layer_output = output_back(
-        branch, mixed, places.reshape(span, 1, rows), output_weights, result, own_grad
-    )
+    attended_grad, own_grad = output_back(branch, mixed, places.reshape(span, 1, rows), output_weights, own_grad)
+    layer_output = swap(behind(result, attended_grad))
     [both_sum] = scatter_wide(own_grad)
-    own_sum = both_sum[:, : 3 * hidden]
 
     head_grads, head_gains = [], 0.0
     for kv in range(key_heads):
         if kv > 0:
-            info = jnp.where(never, behind(line_sum[0], head_grads[0])[0, 0].astype(jnp.int32), info)
+            info = jnp.where(never, behind(line_sum[0], head_grads[0])[0, 0].astype(jnp.int32) + layer_output[0, 0].astype(jnp.int32), info)
         grads, gains_of = attention_backward(
             info,
             qkv,
@@ -1407,8 +1421,6 @@
         jnp.take(grads, places if kv + 1 < key_heads else tied, axis=0, mode="clip")
         for kv, grads in enumerate(head_grads)
     ]
-    output_sum = behind(both_sum, qkv_rows[-1])[:, 3 * hidden :]
-    output_sum = output_sum.reshape(shard, span, head_columns).transpose(1, 0, 2)
     gain_rows = jnp.concatenate(
         [
             jnp.zeros((1, width), F32),
@@ -1428,20 +1440,18 @@
         swapped,
         gain_one,
         gain_rows,
-        output_sum,
+        both_sum,
+        head_columns,
     )
 
-    def total(first, others):
-        out = first.astype(F32)
-        for other in others:
-            out = out + other.astype(F32)
-        return out
-
-    wide_sum = total(behind(own_sum, gain_sums), [behind(piece, gain_sums) for piece in line_in])
-    output_sum = total(output_sum[0], [output_in[k] for k in range(span - 1)])
-    stride = per_query + 2 * per_key
-    columns = lambda at, size: jnp.concatenate(
-        [heads_sum[:, kv * stride + at : kv * stride + at + size] for kv in range(key_heads)], axis=1
+    weight_grads = finish(
+        both_sum,
+        line_in,
+        output_in,
+        heads_sum,
+        [x.shape for x in (query_weight, key_matrix, value_matrix, output_weight, gate_weight, up_weight, down_weight)],
+        span,
+        key_heads,
     )
     cut = lambda row, at, size: lax.dynamic_slice(gain_sums[row], (at + dp * size,), (size,))
     return (
@@ -1450,14 +1460,9 @@
         cut(0, 0, small),
         cut(2, 0, tiny),
         cut(2, HEAD_SIZE, tiny),
-        columns(0, per_query),
-        columns(per_query, per_key),
-        columns(per_query + per_key, per_key),
-        output_sum.T,
+        *weight_grads[:4],
         cut(1, 0, small),
-        wide_sum[:, :hidden],
-        wide_sum[:, hidden : 2 * hidden],
-        wide_sum[:, 2 * hidden :].T,
+        *weight_grads[4:],
     )
 
 

time: 570 us -> 557 us (0.977)
  Pallas kernels: 428 us -> 437 us
  local copies, waits for them, and re-layouts: 60.2 us -> 51.8 us
  other arithmetic: 28.1 us -> 21.5 us
    pallas_call x1, Pallas kernels: 51.4 us -> 43.4 us  [output_back(): pl.pallas_call(functools.partial(output_back_kernel, span), in_specs=[loc...]
    pallas_call x2, Pallas kernels: 57.9 us -> 65 us  [attention_backward(): pl.pallas_call(functools.partial(backward_kernel, group, blocks, docs), g...]
    ppermute x7 -> x8, starting transfers between devices: 13.6 us -> 11.5 us  [send(): return lax.ppermute(x, AXES, moves)]
  transfers between devices with their start and end apart: 12 -> 13, of which waited for: 2 -> 2; matrix products, arithmetic and copies ran while one was open for 10% -> 10% of each run, Pallas kernels for 48% -> 50%
where the time goes in v5:
time: 557 us; the launch traced here: 551 us
  Pallas kernels  437 us (78%)
  local copies, waits for them, and re-layouts  51.8 us (9%)
  other arithmetic  21.5 us (4%)
  between operations  19.7 us (4%)
  starting transfers between devices  11.7 us (2%)
  waiting for transfers between devices  9.39 us (2%)
    pallas_call x1, Pallas kernels, last_transfers(): pl.pallas_call(functools.partial(last_kernel, pairs, span, count), in_spe...  93 us
    pallas_call x1, Pallas kernels, first_transfers(): pl.pallas_call(functools.partial(first_kernel, pairs, span), in_specs=[an...  65.8 us
    pallas_call x2, Pallas kernels, attention_backward(): pl.pallas_call(functools.partial(backward_kernel, group, blocks, docs), g...  65 us
    pallas_call x2, Pallas kernels, feed(): pl.pallas_call(functools.partial(feed_kernel, last), grid=(span,), in_spe...  63.3 us
    pallas_call x1, Pallas kernels, output_project(): pl.pallas_call(functools.partial(output_kernel, span), in_specs=[local_re...  45.3 us
    pallas_call x1, Pallas kernels, output_back(): pl.pallas_call(functools.partial(output_back_kernel, span), in_specs=[loc...  43.4 us
    pallas_call x1, Pallas kernels, project(): pl.pallas_call(functools.partial(project_kernel, query_heads, key_heads),...  32 us
    pallas_call x1, Pallas kernels, attention_forward(): pl.pallas_call(functools.partial(forward_kernel, group, blocks, docs), gr...  25.3 us
  transfers between devices with their start and end apart: 13, of which 2 were waited for; matrix products, arithmetic and copies ran while one was open for 10% of the time, Pallas kernels for 50%

profile of v5, /device:TPU:0, one launch (start us, length us, event | category | flops | bytes accessed | tf_op | source)
XLA Modules:
  0.0 550.7 jit_solution(6399555979266073442)
XLA Ops:
  14.0 1.8 copy.38
  17.2 65.8 %first_transfers.1 = (bf16[4,640,1024]{2,1,0:T(8,128)(2,1)}, bf16[1024,1024]{1,0:T(8,128)(2,1)}, bf16[4,128,512]{2,1,0:T(8,128)(2,1)}, bf16[128,384]{1,0:T(8,128)(2,1)}, s32[24,128]{1,0:T(8,128)}) custom-call(bf16[640,1024]{1,0:T(8,128)(2,1)} %tokens_ref.1, bf16[128,1024]{1,0:T(8,128)(2,1)} %copy-done.8, bf16[128,512]{1,0:T(8,128)(2,1)} %bitcast.78, ...), custom_call_target="tpu_custom_call" | custom-call | bytes 150000000 | tf_op jit(solution)/shard_map/first_transfers/pallas_call | solution.py:251
  89.1 1.6 broadcast_select_fusion.6
  91.2 3.8 collective-permute-start.1
  101.1 3.2 dynamic-slice_select_fusion
  104.3 1.7 fusion.30
  106.1 32.0 %project.1 = (bf16[2560,1024]{1,0:T(8,128)(2,1)}, bf16[2560,1024]{1,0:T(8,128)(2,1)}, f32[2,2560,128]{2,1,0:T(8,128)}) custom-call(bf16[2560,1024]{1,0:T(8,128)(2,1)} %bitcast.75, s32[1,2560]{1,0:T(1,128)} %broadcast_in_dim.96.places_ref, f32[1,1024]{1,0:T(1,128)} %bitcast.80, bf16[1024,1024]{1,0:T(8,128)(2,1)} %get-tuple-element.54.w_ref.refs_5_, ...), custom_call_target="tpu_custom_call" | custom-call | tf_op jit(solution)/shard_map/project/pallas_call | solution.py:309
  139.3 1.8 broadcast_select_fusion.3
  145.5 2.0 broadcast_in_dim.107.places_ref
  148.2 25.3 %attention_forward.1 = (bf16[2560,512]{1,0:T(8,128)(2,1)}, f32[2,5,8,1024]{3,2,1,0:T(8,128)}) custom-call(s32[12]{0:T(128)} %pad_add_fusion.3.info_ref, bf16[2560,1024]{1,0:T(8,128)(2,1)} %get-tuple-element.55.q_ref.k_ref.v_ref, bf16[2560,1024]{1,0:T(8,128)(2,1)} %get-tuple-element.55.q_ref.k_ref.v_ref, bf16[2560,1024]{1,0:T(8,128)(2,1)} %get-tuple-element.55.q_ref.k_ref.v_ref), custom_call_target="tpu_custom_call" | custom-call | bytes 100000000 | tf_op jit(solution)/shard_map/attention_forward/pallas_call | solution.py:405
  174.7 45.3 %output_project.1 = (f32[640,1024]{1,0:T(8,128)}, bf16[640,1024]{1,0:T(8,128)(2,1)}, bf16[4,640,512]{2,1,0:T(8,128)(2,1)}) custom-call(bf16[2560,512]{1,0:T(8,128)(2,1)} %get-tuple-element.56.heads_ref.o_ref, s32[2560,1]{1,0:T(8,128)} %broadcast_in_dim.107.places_ref, bf16[8,4,128,512]{3,2,1,0:T(8,128)(2,1)} %bitcast.71, bf16[640,1024]{1,0:T(8,128)(2,1)} %copy-done, ...), custom_call_target="tpu_custom_call" | custom-call | bytes 100000000 | tf_op jit(solution)/shard_map/output_project/pallas_call | solution.py:664
  221.4 40.5 %feed_forward.2 = (f32[640,1024]{1,0:T(8,128)}, f32[640,1024]{1,0:T(8,128)}, bf16[8,3,128,2304]{3,2,1,0:T(8,128)(2,1)}) custom-call(bf16[640,1024]{1,0:T(8,128)(2,1)} %get-tuple-element.58.x_ref, bf16[640,1024]{1,0:T(8,128)(2,1)} %broadcast_select_fusion.2.c_ref, bf16[8,3,128,2304]{3,2,1,0:T(8,128)(2,1)} %bitcast.74), custom_call_target="tpu_custom_call" | custom-call | tf_op jit(solution)/shard_map/feed_forward/pallas_call | solution.py:862
  262.7 22.8 %feed_forward.3 = (bf16[640,1024]{1,0:T(8,128)(2,1)}, f32[640,1024]{1,0:T(8,128)}, bf16[640,1024]{1,0:T(8,128)(2,1)}, f32[8,1024]{1,0:T(8,128)}, bf16[8,1,128,4352]{3,2,1,0:T(8,128)(2,1)}) custom-call(bf16[640,1024]{1,0:T(8,128)(2,1)} %get-tuple-element.58.x_ref, bf16[640,1024]{1,0:T(8,128)(2,1)} %broadcast_select_fusion.2.c_ref, ...), custom_call_target="tpu_custom_call" | custom-call | tf_op jit(solution)/shard_map/feed_forward/pallas_call | solution.py:862
  285.4 43.4 %output_back.1 = (bf16[2560,512]{1,0:T(8,128)(2,1)}, bf16[8,1,128,4352]{3,2,1,0:T(8,128)(2,1)}) custom-call(bf16[640,1024]{1,0:T(8,128)(2,1)} %get-tuple-element.62.b_ref, bf16[4,640,512]{2,1,0:T(8,128)(2,1)} %get-tuple-element.63.mixed_ref, s32[4,1,640]{2,1,0:T(1,128)} %pad_add_fusion.2.places_ref, ...), custom_call_target="tpu_custom_call", output_to_operand_aliasing={{1}: (4, {})} | custom-call | bytes 100000000 | tf_op jit(solution)/shard_map/output_back/pallas_call | solution.py:755
  330.9 1.8 collective-permute-start.4
  332.8 32.5 %attention_backward.2 = (bf16[2560,512]{1,0:T(8,128)(2,1)}, f32[8,128]{1,0:T(8,128)}) custom-call(s32[12]{0:T(128)} %pad_add_fusion.3.info_ref, bf16[2560,1024]{1,0:T(8,128)(2,1)} %get-tuple-element.55.q_ref.k_ref.v_ref, bf16[2560,1024]{1,0:T(8,128)(2,1)} %get-tuple-element.55.q_ref.k_ref.v_ref, bf16[2560,1024]{1,0:T(8,128)(2,1)} %get-tuple-element.55.q_ref.k_ref.v_ref, ...), custom_call_target="tpu_custom_call" | custom-call | bytes 100000000 | tf_op jit(solution)/shard_map/attention_backward/pallas_call | solution.py:533
  367.2 10.4 %gather_fusion = bf16[2560,512]{1,0:T(8,128)(2,1)} fusion(bf16[2560,512]{1,0:T(8,128)(2,1)} %get-tuple-element.69.refs_2_, s32[3072]{0:T(1024)S(1)} %pad_clamp_fusion.1), kind=kCustom, calls=%fused_computation | custom fusion | bytes 5253120 | tf_op jit(solution)/shard_map/jit(_take)/gather | solution.py:1421
  377.6 2.6 slice_select_fusion
  380.8 3.5 collective-permute-start.6
  388.4 32.5 %attention_backward.3 = (bf16[2560,512]{1,0:T(8,128)(2,1)}, f32[8,128]{1,0:T(8,128)}) custom-call(s32[12]{0:T(128)} %broadcast_select_fusion.9.info_ref, bf16[2560,1024]{1,0:T(8,128)(2,1)} %get-tuple-element.55.q_ref.k_ref.v_ref, bf16[2560,1024]{1,0:T(8,128)(2,1)} %get-tuple-element.55.q_ref.k_ref.v_ref, ...), custom_call_target="tpu_custom_call" | custom-call | bytes 100000000 | tf_op jit(solution)/shard_map/attention_backward/pallas_call | solution.py:533
  426.3 10.4 %gather_fusion.1 = bf16[2560,512]{1,0:T(8,128)(2,1)} fusion(bf16[2560,512]{1,0:T(8,128)(2,1)} %get-tuple-element.71.refs_3_, s32[3072]{0:T(1024)S(1)} %pad_clamp_fusion), kind=kCustom, calls=%fused_computation.1 | custom fusion | bytes 5253120 | tf_op jit(solution)/shard_map/jit(_take)/gather | solution.py:1421
  436.7 7.1 %reduce-scatter.5.cloned.1.call-done.refs_10_.both_ref = bf16[128,4352]{1,0:T(8,128)(2,1)} async-done(((bf16[1024,4352]{1,0:T(8,128)(2,1)}), bf16[128,4352]{1,0:T(8,128)(2,1)}) %reduce-scatter.5.cloned.1.call-update) | async-done | bytes 1114128 | tf_op jit(solution)/shard_map/reduce_scatter | solution.py:1311
  443.9 93.0 %last_transfers.1 = (bf16[640,1024]{1,0:T(8,128)(2,1)}, f32[128,1024]{1,0:T(8,128)}, f32[8,1024]{1,0:T(8,128)}, bf16[3,128,512]{2,1,0:T(8,128)(2,1)}) custom-call(bf16[2560,512]{1,0:T(8,128)(2,1)} %gather_fusion, bf16[2560,512]{1,0:T(8,128)(2,1)} %gather_fusion.1, bf16[2560,512]{1,0:T(8,128)(2,1)} %get-tuple-element.69.refs_2_, ...), custom_call_target="tpu_custom_call" | custom-call | tf_op jit(solution)/shard_map/last_transfers/pallas_call | solution.py:1166
  539.4 3.5 finish.1
  (126 shorter events, 43.0 us)
Async XLA Ops:
  7.2 167.5 %all-gather.4.cloned.1.call-start = ((), (), s32[]{:S(2)}) async-start(), calls=%async_computation.2 | async-start | bytes 4718592 | tf_op jit(solution)/shard_map/all_gather | solution.py:1305
  14.0 3.2 copy-start.8
  84.1 4.1 copy-start.11
  84.1 4.9 copy-start.9
  84.2 4.9 copy-start.10
  85.0 136.4 %all-gather.8.cloned.1.call-start = ((), (), s32[]{:S(2)}) async-start(), calls=%async_computation.4 | async-start | bytes 15925248 | tf_op jit(solution)/shard_map/all_gather | solution.py:1305
  86.2 8.8 %copy-start.12 = (s32[24,128]{1,0:T(8,128)S(1)}, s32[24,128]{1,0:T(8,128)}, u32[]{:S(2)}) copy-start(s32[24,128]{1,0:T(8,128)} %get-tuple-element.51) | copy-start | bytes 36868
  87.7 16.7 %copy-start = (bf16[640,1024]{1,0:T(8,128)(2,1)}, bf16[640,1024]{1,0:T(8,128)(2,1)S(1)}, u32[]{:S(2)}) copy-start(bf16[640,1024]{1,0:T(8,128)(2,1)S(1)} %slice_bitcast_fusion.tokens_ref.refs_7_) | copy-start | bytes 3932164
  90.6 48.7 %collective-permute-start.3 = (bf16[128,2304]{1,0:T(8,128)(2,1)S(1)}, bf16[128,2304]{1,0:T(8,128)(2,1)}, u32[]{:S(2)}, u32[]{:S(2)}) collective-permute-start(bf16[128,2304]{1,0:T(8,128)(2,1)S(1)} %get-tuple-element.100), channel_id=1, source_target_pairs={{0,3},{1,2},{2,1},{3,0},{4,7},{5,6},{6,5},{7,4},{8,11},{9,10},{10,... | collective-permute-start | bytes 1769480 | tf_op jit(solution)/shard_map/ppermute | solution.py:1289
  90.6 50.4 %collective-permute-start.2 = (bf16[128,2304]{1,0:T(8,128)(2,1)S(1)}, bf16[128,2304]{1,0:T(8,128)(2,1)S(1)}, u32[]{:S(2)}, u32[]{:S(2)}) collective-permute-start(bf16[128,2304]{1,0:T(8,128)(2,1)S(1)} %get-tuple-element.100), channel_id=1, source_target_pairs={{0,2},{1,3},{2,0},{3,1},{4,6},{5,7},{6,4},{7,5},{8,10},{9,11},{10,... | collective-permute-start | bytes 1769480 | tf_op jit(solution)/shard_map/ppermute | solution.py:1289
  91.2 50.5 %collective-permute-start.1 = (bf16[128,2304]{1,0:T(8,128)(2,1)S(1)}, bf16[128,2304]{1,0:T(8,128)(2,1)S(1)}, u32[]{:S(2)}, u32[]{:S(2)}) collective-permute-start(bf16[128,2304]{1,0:T(8,128)(2,1)S(1)} %get-tuple-element.100), channel_id=1, source_target_pairs={{0,1},{1,0},{2,3},{3,2},{4,5},{5,4},{6,7},{7,6},{8,9},{9,8},{10,11... | collective-permute-start | bytes 1769480 | tf_op jit(solution)/shard_map/ppermute | solution.py:1289
  143.8 118.8 %all-gather.6.cloned.1.call-start = ((), (), s32[]{:S(2)}) async-start(), calls=%async_computation.3 | async-start | bytes 5308416 | tf_op jit(solution)/shard_map/all_gather | solution.py:1305
  144.6 233.1 %reduce-scatter.3.cloned.1.call-start = ((), (), s32[]{:S(2)}) async-start(), calls=%async_computation.5 | async-start | bytes 15925248 | tf_op jit(solution)/shard_map/reduce_scatter | solution.py:1311
  144.6 28.9 %collective-permute-start = (bf16[640,1024]{1,0:T(8,128)(2,1)S(1)}, bf16[640,1024]{1,0:T(8,128)(2,1)S(1)}, u32[]{:S(2)}, u32[]{:S(2)}) collective-permute-start(bf16[640,1024]{1,0:T(8,128)(2,1)S(1)} %copy-done.3), channel_id=1, source_target_pairs={{2,5},{3,4},{4,3},{5,2},{10,13},{11,12},{12,11},{13,10},{18,21},{1... | collective-permute-start | bytes 3932168 | tf_op jit(solution)/shard_map/ppermute | solution.py:1289
  262.0 181.9 %reduce-scatter.5.cloned.1.call-start = ((), (), s32[]{:S(2)}) async-start(), calls=%async_computation.6 | async-start | bytes 10027008 | tf_op jit(solution)/shard_map/reduce_scatter | solution.py:1311
  330.9 53.8 %collective-permute-start.4 = (bf16[640,1024]{1,0:T(8,128)(2,1)S(1)}, bf16[640,1024]{1,0:T(8,128)(2,1)}, u32[]{:S(2)}, u32[]{:S(2)}) collective-permute-start(bf16[640,1024]{1,0:T(8,128)(2,1)S(1)} %broadcast_select_fusion), channel_id=1, source_target_pairs={{2,5},{3,4},{4,3},{5,2},{10,13},{11,12},{12,11},{13,10},{18,21},{1... | collective-permute-start | bytes 3932168 | tf_op jit(solution)/shard_map/ppermute | solution.py:1289
  380.2 7.7 %copy-start.13 = (s32[12]{0:T(128)S(1)}, s32[12]{0:T(128)}, u32[]{:S(2)}) copy-start(s32[12]{0:T(128)} %pad_add_fusion.3.info_ref) | copy-start | bytes 148
  380.2 42.1 %collective-permute-start.5 = (bf16[128,2304]{1,0:T(8,128)(2,1)S(1)}, bf16[128,2304]{1,0:T(8,128)(2,1)S(1)}, u32[]{:S(2)}, u32[]{:S(2)}) collective-permute-start(bf16[128,2304]{1,0:T(8,128)(2,1)S(1)} %get-tuple-element.99), channel_id=1, source_target_pairs={{0,1},{1,0},{2,3},{3,2},{4,5},{5,4},{6,7},{7,6},{8,9},{9,8},{10,11... | collective-permute-start | bytes 1769480 | tf_op jit(solution)/shard_map/ppermute | solution.py:1289
  380.8 42.8 %collective-permute-start.6 = (bf16[128,2304]{1,0:T(8,128)(2,1)S(1)}, bf16[128,2304]{1,0:T(8,128)(2,1)S(1)}, u32[]{:S(2)}, u32[]{:S(2)}) collective-permute-start(bf16[128,2304]{1,0:T(8,128)(2,1)S(1)} %get-tuple-element.98), channel_id=1, source_target_pairs={{0,2},{1,3},{2,0},{3,1},{4,6},{5,7},{6,4},{7,5},{8,10},{9,11},{10,... | collective-permute-start | bytes 1769480 | tf_op jit(solution)/shard_map/ppermute | solution.py:1289
  384.3 40.5 %collective-permute-start.7 = (bf16[128,2304]{1,0:T(8,128)(2,1)S(1)}, bf16[128,2304]{1,0:T(8,128)(2,1)S(1)}, u32[]{:S(2)}, u32[]{:S(2)}) collective-permute-start(bf16[128,2304]{1,0:T(8,128)(2,1)S(1)} %get-tuple-element.97), channel_id=1, source_target_pairs={{0,3},{1,2},{2,1},{3,0},{4,7},{5,6},{6,5},{7,4},{8,11},{9,10},{10,... | collective-permute-start | bytes 1769480 | tf_op jit(solution)/shard_map/ppermute | solution.py:1289
  385.5 35.4 %copy-start.2 = (bf16[640,1024]{1,0:T(8,128)(2,1)}, bf16[640,1024]{1,0:T(8,128)(2,1)S(1)}, u32[]{:S(2)}) copy-start(bf16[640,1024]{1,0:T(8,128)(2,1)S(1)} %broadcast_select_fusion.1) | copy-start | bytes 3932164
  388.4 32.5 %copy-start.14 = (f32[8,128]{1,0:T(8,128)S(1)}, f32[8,128]{1,0:T(8,128)}, u32[]{:S(2)}) copy-start(f32[8,128]{1,0:T(8,128)} %get-tuple-element.75) | copy-start | bytes 12292
  422.3 14.4 %copy-start.5 = (bf16[128,2304]{1,0:T(8,128)(2,1)}, bf16[128,2304]{1,0:T(8,128)(2,1)S(1)}, u32[]{:S(2)}) copy-start(bf16[128,2304]{1,0:T(8,128)(2,1)S(1)} %collective-permute-done.5.refs_0_) | copy-start | bytes 1769476
  536.8 6.0 %copy-start.4 = (bf16[640,1024]{1,0:T(8,128)(2,1)S(1)}, bf16[640,1024]{1,0:T(8,128)(2,1)}, u32[]{:S(2)}) copy-start(bf16[640,1024]{1,0:T(8,128)(2,1)} %get-tuple-element.143) | copy-start | bytes 3932164
  (4 other events, 5.5 us)
Sparse Core Ops, SparseCore 0:
  85.1 35.1 all-gather.3
  143.9 77.4 all-gather.7
  223.3 38.9 all-gather.5
  265.7 100.8 reduce-scatter.2
  370.0 73.8 reduce-scatter.4
